TPU v7x, 128 devices: a whole 4x4x4 slice. The times are simulated.
128 devices in a mesh: grp: 4 (over y), gy: 32 (over x, z, core).
Axes of the slice: x: 4, y: 4, z: 4, core: 2. Of those that a mesh axis runs over, the one named last changes fastest.
Arguments:
- right_side: float32 [5, 4, 1024, 512], P(None, None, 'gy', 'grp'), may hold values from -7 to 7
- potential: float32 [4, 1024, 512], P(None, 'gy', 'grp'), may hold values from -3 to 3
- capacity: float32 [4, 1024, 512], P(None, 'gy', 'grp'), may hold values from 0.05 to 0.5
- diffusivity: float32 [5, 4], replicated, may hold values from 0.2 to 2
- material: int32 [4, 1024, 512], P(None, 'gy', 'grp'), may hold values from 0 to 3
- coarse_map: int32 [32, 4, 4], P('gy', 'grp'), may hold values from 0 to 511
- coarse_inverse: float32 [512, 5, 5], P(('grp', 'gy')), as said below
Outputs:
- solution_field: float32 [5, 4, 1024, 512], P(None, None, 'gy', 'grp')
- residual: float32 [5, 4, 1024, 512], P(None, None, 'gy', 'grp')
- smoothed: float32 [5, 4, 1024, 512], P(None, None, 'gy', 'grp')
Inputs may be any that keep to these rules, and one draw needn't show every extreme that they name: `coarse_inverse`: each 5 x 5 block is symmetric, with a positive diagonal entry larger than the sum of the magnitudes of the other entries of its row.
All inputs are finite; a program needn't handle non-finite values.
Results may differ from a plain program's by a relative error of at most 0.0003.
Values sent between devices are 32-bit elements; how exact they have to be, the bound alone decides.
No kernel may reach another device: no remote copies, remote signals or barrier semaphores. Data moves between devices by JAX's collectives and lax.ppermute only.
A program may use at most 64 MiB of HBM per device.

v0:
```python
import jax
import jax.numpy as jnp
from jax import lax
from jax.sharding import PartitionSpec as P

MATS = 4
SWEEPS = 4
ITERS = 2


VALENCE = (1.0, -1.0, 2.0, -2.0, 1.0)
VERTICAL = 0.5
DAMPING = 2.0 / 3.0


def with_halo(block, sides, width):
    for axis, dim in sides:
        count = lax.axis_size(axis)
        forward = [(i, i + 1) for i in range(count - 1)]
        forward.append((count - 1, 0))
        backward = [(target, source) for source, target in forward]
        low = lax.ppermute(
            lax.slice_in_dim(block, block.shape[dim] - width, None, axis=dim), axis, forward
        )
        high = lax.ppermute(lax.slice_in_dim(block, 0, width, axis=dim), axis, backward)
        block = jnp.concatenate([low, block, high], axis=dim)
    return block


def harmonic(lower_w, upper_w):
    return 2.0 * lower_w * upper_w / (lower_w + upper_w)


def cell_weights(diffusivity, material, potential):
    weights = jnp.zeros((diffusivity.shape[0],) + material.shape, jnp.float32)
    for mat_id in range(MATS):
        weights = weights + jnp.where(
            material[None] == mat_id, diffusivity[:, mat_id][:, None, None, None], 0.0
        )
    charge = jnp.asarray(VALENCE, jnp.float32)[:, None, None, None]
    return weights * jnp.exp(-0.5 * charge * potential[None])


def edge_tables(wide_w, column_start, grid_cols):
    gy_all = harmonic(wide_w[:, :, :-1, :], wide_w[:, :, 1:, :])
    gx_raw = harmonic(wide_w[..., :-1], wide_w[..., 1:])
    left_cell = column_start + jnp.arange(gx_raw.shape[-1])
    valid = (left_cell >= 0) & (left_cell <= grid_cols - 2)
    gx_all = jnp.where(valid, gx_raw, 0.0)
    gz_all = VERTICAL * harmonic(wide_w[:, :-1], wide_w[:, 1:])
    return (gy_all, gx_all, gz_all)


def cycle_tables(edges, wide_cap, margin, cycle_no):
    gy_all, gx_all, gz_all = edges
    start = margin - cycle_no
    height = wide_cap.shape[1] - 2 * start
    width = wide_cap.shape[2] - 2 * start
    gy_hi = gy_all[:, :, start : start + height, start : start + width]
    gy_lo = gy_all[:, :, start - 1 : start - 1 + height, start : start + width]
    gx_hi = gx_all[:, :, start : start + height, start : start + width]
    gx_lo = gx_all[:, :, start : start + height, start - 1 : start - 1 + width]
    gz_mid = gz_all[:, :, start : start + height, start : start + width]
    cap_mid = wide_cap[:, start : start + height, start : start + width]
    zero_layer = jnp.zeros_like(gz_mid[:, :1])
    gz_hi = jnp.concatenate([gz_mid, zero_layer], axis=1)
    gz_lo = jnp.concatenate([zero_layer, gz_mid], axis=1)
    diagonal = cap_mid[None] + gy_hi + gy_lo + gx_hi + gx_lo + gz_hi + gz_lo
    return (gy_hi, gy_lo, gx_hi, gx_lo, gz_hi, gz_lo, diagonal)


def apply_cycle(padded, tables):
    gy_hi, gy_lo, gx_hi, gx_lo, gz_hi, gz_lo, diagonal = tables
    center = padded[:, :, 1:-1, 1:-1]
    beside_y = gy_hi * padded[:, :, 2:, 1:-1] + gy_lo * padded[:, :, :-2, 1:-1]
    beside_x = gx_hi * padded[:, :, 1:-1, 2:] + gx_lo * padded[:, :, 1:-1, :-2]
    zero_layer = jnp.zeros_like(center[:, :1])
    above = jnp.concatenate([center[:, 1:], zero_layer], axis=1)
    below = jnp.concatenate([zero_layer, center[:, :-1]], axis=1)
    beside_z = gz_hi * above + gz_lo * below
    return (diagonal * center - (beside_y + beside_x + beside_z), center)


def body(right_side, potential, capacity, diffusivity, material, coarse_map, coarse_inverse):
    cols = right_side.shape[3]
    grid_cols = cols * lax.axis_size("grp")
    weights = cell_weights(diffusivity, material, potential)
    stacked = jnp.concatenate([weights, capacity[None]], axis=0)
    margin = 1
    wide = with_halo(stacked, (("grp", 3), ("gy", 2)), 1)
    wide_w = wide[:-1]
    wide_cap = wide[-1]
    column_start = lax.axis_index("grp") * cols - margin
    edges = edge_tables(wide_w, column_start, grid_cols)
    levels = cycle_tables(edges, wide_cap, margin, 0)
    own_diag = levels[6]

    def image_of(field):
        padded = with_halo(field, (("grp", 3), ("gy", 2)), 1)
        return apply_cycle(padded, levels)[0]

    def smooth(resid):
        approx = DAMPING * resid / own_diag
        for sweep_no in range(1, SWEEPS):
            approx = approx + DAMPING * (resid - image_of(approx)) / own_diag
        return approx

    own_map = coarse_map.reshape(-1)
    coarse_count = coarse_inverse.shape[0] * lax.axis_size("grp") * lax.axis_size("gy")
    picks = (jnp.arange(coarse_count)[None, :] == own_map[:, None]).astype(jnp.float32)

    def coarse(resid):
        block_sums = jnp.stack(
            [
                jnp.sum(jnp.where(material[None] == mat_id, resid, 0.0), axis=(1, 2, 3))
                for mat_id in range(MATS)
            ]
        )
        contrib = jnp.sum(picks[:, :, None] * block_sums[:, None, :], axis=0)
        owned_res = lax.psum_scatter(contrib, ("grp", "gy"), scatter_dimension=0, tiled=True)
        owned_sol = jnp.sum(coarse_inverse * owned_res[:, None, :], axis=2)
        coarse_sol = lax.all_gather(owned_sol, ("grp", "gy"), axis=0, tiled=True)
        chosen = jnp.sum(picks[:, :, None] * coarse_sol[None], axis=1)
        field = jnp.zeros_like(resid)
        for mat_id in range(MATS):
            field = field + jnp.where(
                material[None] == mat_id, chosen[mat_id][:, None, None, None], 0.0
            )
        return field

    def precondition(resid, wanted):
        result = smooth(resid) + coarse(resid)
        if wanted:
            return (result, lax.psum(jnp.sum(resid * result), ("grp", "gy")))
        return (result, None)

    solution_field = jnp.zeros_like(right_side)
    residual = right_side
    smoothed, inner_now = precondition(residual, True)
    direction = smoothed
    for step_no in range(ITERS):
        image = image_of(direction)
        alpha = inner_now / lax.psum(jnp.sum(direction * image), ("grp", "gy"))
        solution_field = solution_field + alpha * direction
        residual = residual - alpha * image
        smoothed, inner_next = precondition(residual, step_no + 1 < ITERS)
        if step_no + 1 < ITERS:
            direction = smoothed + inner_next / inner_now * direction
            inner_now = inner_next
    return (solution_field, residual, smoothed)


def solution(mesh):
    placed = (
        P(None, None, "gy", "grp"),
        P(None, "gy", "grp"),
        P(None, "gy", "grp"),
        P(),
        P(None, "gy", "grp"),
        P("gy", "grp", None),
        P(("grp", "gy"), None, None),
    )
    return jax.shard_map(
        body,
        mesh=mesh,
        in_specs=placed,
        out_specs=(
            P(None, None, "gy", "grp"),
            P(None, None, "gy", "grp"),
            P(None, None, "gy", "grp"),
        ),
        check_vma=False,
    )
```

profile of v0, /device:TPU:1, one launch (start us, length us, event | category | flops | bytes accessed | tf_op | source)
XLA Modules:
  0.0 739.2 jit_solution(11586583054932258400)
XLA Ops:
  4.1 2.2 collective-permute-start
  7.9 8.5 %collective-permute-done = f32[6,4,32,1]{3,2,1,0:T(8,128)S(1)} collective-permute-done((f32[6,4,32,1]{3,2,1,0:T(8,128)S(1)}, f32[6,4,32,1]{3,2,1,0:T(8,128)S(1)}, u32[]{:S(2)}, u32[]{:S(2)}) %collective-permute-start) | collective-permute-done | bytes 3104 | tf_op jit(solution)/shard_map/ppermute | solution.py:22
  16.6 3.0 collective-permute-start.2
  20.5 2.6 collective-permute-done.3
  28.9 69.8 %all-reduce.24 = f32[512,5]{1,0:T(8,128)} all-reduce(f32[512,5]{1,0:T(8,128)S(1)} %copy.27), channel_id=2, replica_groups=mesh['grp'=4,'gy'=32] {'grp','gy'}, use_global_device_ids=true, to_apply=%region_5.6.clone | all-reduce | flops 2560 | bytes 20480
  100.9 6.1 collective-permute-done.5
  107.0 2.5 collective-permute-done.4
  112.1 36.9 %all-gather = f32[128,4,5]{2,1,0:T(4,128)} all-gather(f32[1,4,5]{2,1,0:T(4,128)S(1)} %bitcast.38), channel_id=1, replica_groups=mesh['grp'=4,'gy'=32] {'grp','gy'}, dimensions={0}, use_global_device_ids=true | all-gather | bytes 10320 | tf_op jit(solution)/shard_map/all_gather | solution.py:122
  150.1 1.9 fusion.6
  152.1 1.6 collective-permute-start.9
  153.8 7.5 %collective-permute-done.9 = f32[5,4,32,1]{3,2,1,0:T(8,128)S(1)} collective-permute-done((f32[5,4,32,1]{3,2,1,0:T(8,128)S(1)}, f32[5,4,32,1]{3,2,1,0:T(8,128)S(1)}, u32[]{:S(2)}, u32[]{:S(2)}) %collective-permute-start.9) | collective-permute-done | bytes 2592 | tf_op jit(solution)/shard_map/ppermute | solution.py:25
  161.4 2.4 collective-permute-done.8
  170.7 4.2 collective-permute-done.13
  176.7 7.3 collective-permute-start.14
  187.9 4.5 collective-permute-done.17
  193.9 7.1 collective-permute-start.18
  203.5 67.1 %all-reduce.27 = (f32[]{:T(128)}, f32[]{:T(128)}) all-reduce(f32[]{:T(128)} %get-tuple-element.12, f32[]{:T(128)} %get-tuple-element.11), channel_id=1, replica_groups=mesh['grp'=4,'gy'=32] {'grp','gy'}, use_global_device_ids=true, to_apply=%region_9.10 | all-reduce | flops 2 | bytes 16 | tf_op jit(solution)/shard_map/psum | solution.py:134
  274.7 64.3 %all-reduce.25 = f32[512,5]{1,0:T(8,128)} all-reduce(f32[512,5]{1,0:T(8,128)S(1)} %copy.31), channel_id=3, replica_groups=mesh['grp'=4,'gy'=32] {'grp','gy'}, use_global_device_ids=true, to_apply=%region_17.18.clone | all-reduce | flops 2560 | bytes 20480
  339.1 2.0 collective-permute-start.21
  341.7 6.3 collective-permute-done.21
  348.1 2.1 collective-permute-done.20
  350.8 2.5 collective-permute-start.22
  353.5 37.1 %all-gather.1 = f32[128,4,5]{2,1,0:T(4,128)} all-gather(f32[1,4,5]{2,1,0:T(4,128)S(1)} %bitcast.39), channel_id=1, replica_groups=mesh['grp'=4,'gy'=32] {'grp','gy'}, dimensions={0}, use_global_device_ids=true | all-gather | bytes 10320 | tf_op jit(solution)/shard_map/all_gather | solution.py:122
  391.6 2.2 fusion.31
  393.9 1.9 collective-permute-start.25
  395.9 7.2 collective-permute-done.25
  403.2 2.7 collective-permute-done.24
  412.4 4.2 collective-permute-done.29
  418.4 7.3 collective-permute-start.30
  426.9 1.6 multiply_reduce_fusion.1
  428.5 67.2 %psum.30 = f32[]{:T(128)} all-reduce(f32[]{:T(128)} %get-tuple-element.34), channel_id=1, replica_groups=mesh['grp'=4,'gy'=32] {'grp','gy'}, use_global_device_ids=true, to_apply=%region_21.22 | all-reduce | flops 1 | bytes 8 | tf_op jit(solution)/shard_map/psum | solution.py:134
  498.9 6.6 collective-permute-done.33
  505.5 2.5 collective-permute-done.32
  511.8 2.1 multiply_reduce_fusion
  513.9 66.9 %psum.31 = f32[]{:T(128)} all-reduce(f32[]{:T(128)} %get-tuple-element.32), channel_id=1, replica_groups=mesh['grp'=4,'gy'=32] {'grp','gy'}, use_global_device_ids=true, to_apply=%region_23.24 | all-reduce | flops 1 | bytes 8 | tf_op jit(solution)/shard_map/psum | solution.py:143
  586.0 64.3 %all-reduce.26 = f32[512,5]{1,0:T(8,128)} all-reduce(f32[512,5]{1,0:T(8,128)S(1)} %copy.35), channel_id=4, replica_groups=mesh['grp'=4,'gy'=32] {'grp','gy'}, use_global_device_ids=true, to_apply=%region_29.30.clone | all-reduce | flops 2560 | bytes 20480
  650.3 2.0 collective-permute-start.37
  652.9 6.3 collective-permute-done.37
  659.3 2.1 collective-permute-done.36
  661.5 2.5 collective-permute-start.38
  664.3 36.9 %all-gather.2 = f32[128,4,5]{2,1,0:T(4,128)} all-gather(f32[1,4,5]{2,1,0:T(4,128)S(1)} %bitcast.40), channel_id=1, replica_groups=mesh['grp'=4,'gy'=32] {'grp','gy'}, dimensions={0}, use_global_device_ids=true | all-gather | bytes 10320 | tf_op jit(solution)/shard_map/all_gather | solution.py:122
  702.2 1.9 fusion.56
  704.3 2.0 collective-permute-start.41
  706.3 7.2 collective-permute-done.41
  713.5 2.8 collective-permute-done.40
  722.8 4.2 collective-permute-done.45
  728.7 7.3 collective-permute-start.46
  737.3 1.6 fusion.71
  (178 shorter events, 70.5 us)
Async XLA Ops:
  4.1 12.3 %collective-permute-start = (f32[6,4,32,1]{3,2,1,0:T(8,128)S(1)}, f32[6,4,32,1]{3,2,1,0:T(8,128)S(1)}, u32[]{:S(2)}, u32[]{:S(2)}) collective-permute-start(f32[6,4,32,1]{3,2,1,0:T(8,128)S(1)} %get-tuple-element.64), channel_id=1, source_target_pairs={{0,32},{32,64},{64,96},{96,0},{1,33},{33,65},{65,97},{97,1},{2,34}... | collective-permute-start | bytes 9224 | tf_op jit(solution)/shard_map/ppermute | solution.py:22
  6.3 10.1 %collective-permute-start.1 = (f32[6,4,32,1]{3,2,1,0:T(8,128)S(1)}, f32[6,4,32,1]{3,2,1,0:T(8,128)S(1)}, u32[]{:S(2)}, u32[]{:S(2)}) collective-permute-start(f32[6,4,32,1]{3,2,1,0:T(8,128)S(1)} %get-tuple-element.65), channel_id=1, source_target_pairs={{32,0},{64,32},{96,64},{0,96},{33,1},{65,33},{97,65},{1,97},{34,2}... | collective-permute-start | bytes 9224 | tf_op jit(solution)/shard_map/ppermute | solution.py:25
  16.6 3.9 collective-permute-start.2
  19.6 3.5 collective-permute-start.3
  98.7 8.3 %collective-permute-start.5 = (f32[5,4,32,1]{3,2,1,0:T(8,128)}, f32[5,4,32,1]{3,2,1,0:T(8,128)S(1)}, u32[]{:S(2)}, u32[]{:S(2)}) collective-permute-start(f32[5,4,32,1]{3,2,1,0:T(8,128)} %get-tuple-element.109), channel_id=1, source_target_pairs={{32,0},{64,32},{96,64},{0,96},{33,1},{65,33},{97,65},{1,97},{34,2}... | collective-permute-start | bytes 7688 | tf_op jit(solution)/shard_map/ppermute | solution.py:25
  99.3 10.2 %collective-permute-start.4 = (f32[5,4,32,1]{3,2,1,0:T(8,128)}, f32[5,4,32,1]{3,2,1,0:T(8,128)S(1)}, u32[]{:S(2)}, u32[]{:S(2)}) collective-permute-start(f32[5,4,32,1]{3,2,1,0:T(8,128)} %get-tuple-element.110), channel_id=1, source_target_pairs={{0,32},{32,64},{64,96},{96,0},{1,33},{33,65},{65,97},{97,1},{2,34}... | collective-permute-start | bytes 7688 | tf_op jit(solution)/shard_map/ppermute | solution.py:22
  109.7 40.4 %collective-permute-start.6 = (f32[5,4,1,130]{3,2,1,0:T(1,128)S(1)}, f32[5,4,1,130]{3,2,1,0:T(1,128)S(1)}, u32[]{:S(2)}, u32[]{:S(2)}) collective-permute-start(f32[5,4,1,130]{3,2,1,0:T(1,128)S(1)} %get-tuple-element.60), channel_id=1, source_target_pairs={{1,0},{2,1},{3,2},{4,3},{5,4},{6,5},{7,6},{8,7},{9,8},{10,9},{11,1... | collective-permute-start | bytes 31208 | tf_op jit(solution)/shard_map/ppermute | solution.py:25
  111.1 38.9 %collective-permute-start.7 = (f32[5,4,1,130]{3,2,1,0:T(1,128)S(1)}, f32[5,4,1,130]{3,2,1,0:T(1,128)S(1)}, u32[]{:S(2)}, u32[]{:S(2)}) collective-permute-start(f32[5,4,1,130]{3,2,1,0:T(1,128)S(1)} %get-tuple-element.61), channel_id=1, source_target_pairs={{0,1},{1,2},{2,3},{3,4},{4,5},{5,6},{6,7},{7,8},{8,9},{9,10},{10,1... | collective-permute-start | bytes 31208 | tf_op jit(solution)/shard_map/ppermute | solution.py:22
  152.1 9.2 %collective-permute-start.9 = (f32[5,4,32,1]{3,2,1,0:T(8,128)S(1)}, f32[5,4,32,1]{3,2,1,0:T(8,128)S(1)}, u32[]{:S(2)}, u32[]{:S(2)}) collective-permute-start(f32[5,4,32,1]{3,2,1,0:T(8,128)S(1)} %get-tuple-element.105), channel_id=1, source_target_pairs={{32,0},{64,32},{96,64},{0,96},{33,1},{65,33},{97,65},{1,97},{34,2}... | collective-permute-start | bytes 7688 | tf_op jit(solution)/shard_map/ppermute | solution.py:25
  153.7 10.1 %collective-permute-start.8 = (f32[5,4,32,1]{3,2,1,0:T(8,128)S(1)}, f32[5,4,32,1]{3,2,1,0:T(8,128)S(1)}, u32[]{:S(2)}, u32[]{:S(2)}) collective-permute-start(f32[5,4,32,1]{3,2,1,0:T(8,128)S(1)} %get-tuple-element.106), channel_id=1, source_target_pairs={{0,32},{32,64},{64,96},{96,0},{1,33},{33,65},{65,97},{97,1},{2,34}... | collective-permute-start | bytes 7688 | tf_op jit(solution)/shard_map/ppermute | solution.py:22
  164.0 3.3 collective-permute-start.10
  165.3 2.7 collective-permute-start.11
  169.0 6.0 collective-permute-start.13
  169.3 7.1 collective-permute-start.12
  176.7 8.2 %collective-permute-start.14 = (f32[5,4,1,130]{3,2,1,0:T(1,128)S(1)}, f32[5,4,1,130]{3,2,1,0:T(1,128)S(1)}, u32[]{:S(2)}, u32[]{:S(2)}) collective-permute-start(f32[5,4,1,130]{3,2,1,0:T(1,128)S(1)} %get-tuple-element.56), channel_id=1, source_target_pairs={{1,0},{2,1},{3,2},{4,3},{5,4},{6,5},{7,6},{8,7},{9,8},{10,9},{11,1... | collective-permute-start | bytes 31208 | tf_op jit(solution)/shard_map/ppermute | solution.py:25
  184.0 1.2 collective-permute-start.15
  186.4 6.0 collective-permute-start.17
  186.5 7.2 collective-permute-start.16
  193.9 7.9 %collective-permute-start.18 = (f32[5,4,1,130]{3,2,1,0:T(1,128)S(1)}, f32[5,4,1,130]{3,2,1,0:T(1,128)S(1)}, u32[]{:S(2)}, u32[]{:S(2)}) collective-permute-start(f32[5,4,1,130]{3,2,1,0:T(1,128)S(1)} %get-tuple-element.54), channel_id=1, source_target_pairs={{1,0},{2,1},{3,2},{4,3},{5,4},{6,5},{7,6},{8,7},{9,8},{10,9},{11,1... | collective-permute-start | bytes 31208 | tf_op jit(solution)/shard_map/ppermute | solution.py:25
  200.9 1.2 collective-permute-start.19
  339.1 9.0 %collective-permute-start.21 = (f32[5,4,32,1]{3,2,1,0:T(8,128)}, f32[5,4,32,1]{3,2,1,0:T(8,128)S(1)}, u32[]{:S(2)}, u32[]{:S(2)}) collective-permute-start(f32[5,4,32,1]{3,2,1,0:T(8,128)} %get-tuple-element.92), channel_id=1, source_target_pairs={{32,0},{64,32},{96,64},{0,96},{33,1},{65,33},{97,65},{1,97},{34,2}... | collective-permute-start | bytes 7688 | tf_op jit(solution)/shard_map/ppermute | solution.py:25
  341.0 9.1 %collective-permute-start.20 = (f32[5,4,32,1]{3,2,1,0:T(8,128)}, f32[5,4,32,1]{3,2,1,0:T(8,128)S(1)}, u32[]{:S(2)}, u32[]{:S(2)}) collective-permute-start(f32[5,4,32,1]{3,2,1,0:T(8,128)} %get-tuple-element.93), channel_id=1, source_target_pairs={{0,32},{32,64},{64,96},{96,0},{1,33},{33,65},{65,97},{97,1},{2,34}... | collective-permute-start | bytes 7688 | tf_op jit(solution)/shard_map/ppermute | solution.py:22
  350.8 40.8 %collective-permute-start.22 = (f32[5,4,1,130]{3,2,1,0:T(1,128)S(1)}, f32[5,4,1,130]{3,2,1,0:T(1,128)S(1)}, u32[]{:S(2)}, u32[]{:S(2)}) collective-permute-start(f32[5,4,1,130]{3,2,1,0:T(1,128)S(1)} %get-tuple-element.52), channel_id=1, source_target_pairs={{1,0},{2,1},{3,2},{4,3},{5,4},{6,5},{7,6},{8,7},{9,8},{10,9},{11,1... | collective-permute-start | bytes 31208 | tf_op jit(solution)/shard_map/ppermute | solution.py:25
  353.3 38.3 %collective-permute-start.23 = (f32[5,4,1,130]{3,2,1,0:T(1,128)S(1)}, f32[5,4,1,130]{3,2,1,0:T(1,128)S(1)}, u32[]{:S(2)}, u32[]{:S(2)}) collective-permute-start(f32[5,4,1,130]{3,2,1,0:T(1,128)S(1)} %get-tuple-element.53), channel_id=1, source_target_pairs={{0,1},{1,2},{2,3},{3,4},{4,5},{5,6},{6,7},{7,8},{8,9},{9,10},{10,1... | collective-permute-start | bytes 31208 | tf_op jit(solution)/shard_map/ppermute | solution.py:22
  393.9 9.2 %collective-permute-start.25 = (f32[5,4,32,1]{3,2,1,0:T(8,128)S(1)}, f32[5,4,32,1]{3,2,1,0:T(8,128)S(1)}, u32[]{:S(2)}, u32[]{:S(2)}) collective-permute-start(f32[5,4,32,1]{3,2,1,0:T(8,128)S(1)} %get-tuple-element.88), channel_id=1, source_target_pairs={{32,0},{64,32},{96,64},{0,96},{33,1},{65,33},{97,65},{1,97},{34,2}... | collective-permute-start | bytes 7688 | tf_op jit(solution)/shard_map/ppermute | solution.py:25
  395.8 10.1 %collective-permute-start.24 = (f32[5,4,32,1]{3,2,1,0:T(8,128)S(1)}, f32[5,4,32,1]{3,2,1,0:T(8,128)S(1)}, u32[]{:S(2)}, u32[]{:S(2)}) collective-permute-start(f32[5,4,32,1]{3,2,1,0:T(8,128)S(1)} %get-tuple-element.89), channel_id=1, source_target_pairs={{0,32},{32,64},{64,96},{96,0},{1,33},{33,65},{65,97},{97,1},{2,34}... | collective-permute-start | bytes 7688 | tf_op jit(solution)/shard_map/ppermute | solution.py:22
  406.1 3.3 collective-permute-start.26
  407.4 2.2 collective-permute-start.27
  410.6 6.0 collective-permute-start.29
  411.0 7.1 collective-permute-start.28
  418.4 8.2 %collective-permute-start.30 = (f32[5,4,1,130]{3,2,1,0:T(1,128)S(1)}, f32[5,4,1,130]{3,2,1,0:T(1,128)S(1)}, u32[]{:S(2)}, u32[]{:S(2)}) collective-permute-start(f32[5,4,1,130]{3,2,1,0:T(1,128)S(1)} %get-tuple-element.48), channel_id=1, source_target_pairs={{1,0},{2,1},{3,2},{4,3},{5,4},{6,5},{7,6},{8,7},{9,8},{10,9},{11,1... | collective-permute-start | bytes 31208 | tf_op jit(solution)/shard_map/ppermute | solution.py:25
  425.7 1.2 collective-permute-start.31
  497.4 8.2 %collective-permute-start.33 = (f32[5,4,32,1]{3,2,1,0:T(8,128)S(1)}, f32[5,4,32,1]{3,2,1,0:T(8,128)S(1)}, u32[]{:S(2)}, u32[]{:S(2)}) collective-permute-start(f32[5,4,32,1]{3,2,1,0:T(8,128)S(1)} %get-tuple-element.78), channel_id=1, source_target_pairs={{32,0},{64,32},{96,64},{0,96},{33,1},{65,33},{97,65},{1,97},{34,2}... | collective-permute-start | bytes 7688 | tf_op jit(solution)/shard_map/ppermute | solution.py:25
  498.1 9.9 %collective-permute-start.32 = (f32[5,4,32,1]{3,2,1,0:T(8,128)S(1)}, f32[5,4,32,1]{3,2,1,0:T(8,128)S(1)}, u32[]{:S(2)}, u32[]{:S(2)}) collective-permute-start(f32[5,4,32,1]{3,2,1,0:T(8,128)S(1)} %get-tuple-element.79), channel_id=1, source_target_pairs={{0,32},{32,64},{64,96},{96,0},{1,33},{33,65},{65,97},{97,1},{2,34}... | collective-permute-start | bytes 7688 | tf_op jit(solution)/shard_map/ppermute | solution.py:22
  508.2 3.6 collective-permute-start.34
  509.7 2.1 collective-permute-start.35
  650.3 9.0 %collective-permute-start.37 = (f32[5,4,32,1]{3,2,1,0:T(8,128)}, f32[5,4,32,1]{3,2,1,0:T(8,128)S(1)}, u32[]{:S(2)}, u32[]{:S(2)}) collective-permute-start(f32[5,4,32,1]{3,2,1,0:T(8,128)} %get-tuple-element.76), channel_id=1, source_target_pairs={{32,0},{64,32},{96,64},{0,96},{33,1},{65,33},{97,65},{1,97},{34,2}... | collective-permute-start | bytes 7688 | tf_op jit(solution)/shard_map/ppermute | solution.py:25
  652.3 9.1 %collective-permute-start.36 = (f32[5,4,32,1]{3,2,1,0:T(8,128)}, f32[5,4,32,1]{3,2,1,0:T(8,128)S(1)}, u32[]{:S(2)}, u32[]{:S(2)}) collective-permute-start(f32[5,4,32,1]{3,2,1,0:T(8,128)} %get-tuple-element.77), channel_id=1, source_target_pairs={{0,32},{32,64},{64,96},{96,0},{1,33},{33,65},{65,97},{97,1},{2,34}... | collective-permute-start | bytes 7688 | tf_op jit(solution)/shard_map/ppermute | solution.py:22
  661.5 40.7 %collective-permute-start.38 = (f32[5,4,1,130]{3,2,1,0:T(1,128)S(1)}, f32[5,4,1,130]{3,2,1,0:T(1,128)S(1)}, u32[]{:S(2)}, u32[]{:S(2)}) collective-permute-start(f32[5,4,1,130]{3,2,1,0:T(1,128)S(1)} %get-tuple-element.44), channel_id=1, source_target_pairs={{1,0},{2,1},{3,2},{4,3},{5,4},{6,5},{7,6},{8,7},{9,8},{10,9},{11,1... | collective-permute-start | bytes 31208 | tf_op jit(solution)/shard_map/ppermute | solution.py:25
  664.1 38.2 %collective-permute-start.39 = (f32[5,4,1,130]{3,2,1,0:T(1,128)S(1)}, f32[5,4,1,130]{3,2,1,0:T(1,128)S(1)}, u32[]{:S(2)}, u32[]{:S(2)}) collective-permute-start(f32[5,4,1,130]{3,2,1,0:T(1,128)S(1)} %get-tuple-element.45), channel_id=1, source_target_pairs={{0,1},{1,2},{2,3},{3,4},{4,5},{5,6},{6,7},{7,8},{8,9},{9,10},{10,1... | collective-permute-start | bytes 31208 | tf_op jit(solution)/shard_map/ppermute | solution.py:22
  704.3 9.2 %collective-permute-start.41 = (f32[5,4,32,1]{3,2,1,0:T(8,128)S(1)}, f32[5,4,32,1]{3,2,1,0:T(8,128)S(1)}, u32[]{:S(2)}, u32[]{:S(2)}) collective-permute-start(f32[5,4,32,1]{3,2,1,0:T(8,128)S(1)} %get-tuple-element.72), channel_id=1, source_target_pairs={{32,0},{64,32},{96,64},{0,96},{33,1},{65,33},{97,65},{1,97},{34,2}... | collective-permute-start | bytes 7688 | tf_op jit(solution)/shard_map/ppermute | solution.py:25
  706.2 10.1 %collective-permute-start.40 = (f32[5,4,32,1]{3,2,1,0:T(8,128)S(1)}, f32[5,4,32,1]{3,2,1,0:T(8,128)S(1)}, u32[]{:S(2)}, u32[]{:S(2)}) collective-permute-start(f32[5,4,32,1]{3,2,1,0:T(8,128)S(1)} %get-tuple-element.73), channel_id=1, source_target_pairs={{0,32},{32,64},{64,96},{96,0},{1,33},{33,65},{65,97},{97,1},{2,34}... | collective-permute-start | bytes 7688 | tf_op jit(solution)/shard_map/ppermute | solution.py:22
  716.5 3.3 collective-permute-start.42
  717.8 2.2 collective-permute-start.43
  721.0 6.0 collective-permute-start.45
  721.4 7.1 collective-permute-start.44
  728.7 8.2 %collective-permute-start.46 = (f32[5,4,1,130]{3,2,1,0:T(1,128)S(1)}, f32[5,4,1,130]{3,2,1,0:T(1,128)S(1)}, u32[]{:S(2)}, u32[]{:S(2)}) collective-permute-start(f32[5,4,1,130]{3,2,1,0:T(1,128)S(1)} %get-tuple-element.40), channel_id=1, source_target_pairs={{1,0},{2,1},{3,2},{4,3},{5,4},{6,5},{7,6},{8,7},{9,8},{10,9},{11,1... | collective-permute-start | bytes 31208 | tf_op jit(solution)/shard_map/ppermute | solution.py:25
  736.1 1.2 collective-permute-start.47
  (13 other events, 178.9 us)
where the time goes:
time: 753 us; the launch traced here: 739 us
  blocking collectives  511 us (68%)
  waiting for transfers between devices  111 us (15%)
  starting transfers between devices  69.7 us (9%)
  other arithmetic  25 us (3%)
  local copies, waits for them, and re-layouts  18 us (2%)
    unnamed x3, blocking collectives  198 us
    psum x2, blocking collectives, precondition(): return (result, lax.psum(jnp.sum(resid * result), ('grp', 'gy')))  134 us
    all_gather x3, blocking collectives, coarse(): coarse_sol = lax.all_gather(owned_sol, ('grp', 'gy'), axis=0, tiled=True)  111 us
    ppermute x24, waiting for transfers between devices, with_halo(): lax.ppermute(lax.slice_in_dim(block, 0, width, axis=dim), axis, backward)  75.5 us
    psum x1, blocking collectives, body(): alpha = inner_now / lax.psum(jnp.sum(direction * image), ('grp', 'gy'))  66.9 us
    ppermute x24, starting transfers between devices, with_halo(): lax.ppermute(lax.slice_in_dim(block, 0, width, axis=dim), axis, backward)  54.5 us
    ppermute x24, waiting for transfers between devices, with_halo(): lax.ppermute(lax.slice_in_dim(block, block.shape[dim] - width, None, axis...  35.2 us
    ppermute x24, starting transfers between devices, with_halo(): lax.ppermute(lax.slice_in_dim(block, block.shape[dim] - width, None, axis...  15.2 us
  transfers between devices with their start and end apart: 48, of which 40 were waited for; matrix products, arithmetic and copies ran while one was open for 1% of the time, Pallas kernels for 0%

commit v1 on v0

v1 whole, which is shorter than its diff:
```python
import functools

import jax
import jax.numpy as jnp
from jax import lax
from jax.experimental import pallas as pl
from jax.experimental.pallas import tpu as pltpu
from jax.sharding import PartitionSpec as P

SPECIES = 5
LAYERS = 4
MATS = 4
FIELDS = SPECIES * LAYERS
PLANES = FIELDS + 3 * LAYERS
ROWS = 32
COLS = 128
N_GRP = 4
N_GY = 32
TOTAL = N_GRP * N_GY
NC = 512
DAMPING = 2.0 / 3.0
BOTH = ("grp", "gy")

HALO = 12
PER = 10
GROUPS = -(-PLANES // PER)
RHALO = 16
PAD = 8
WIDE = 2 * COLS
TALL = ROWS + 2 * RHALO + 2 * PAD
TOP = PAD + RHALO
F32 = jnp.float32

G_RW, G_RAU, G_S, G_CY, G_CX, G_MOM = 0, 4, 8, 14, 30, 46
ROW_CAP = 250
MAP_LANE = 20
INV_LANE = 24


def lanes(shape):
    return lax.broadcasted_iota(jnp.int32, shape, 1)


def subs(shape):
    return lax.broadcasted_iota(jnp.int32, shape, 0)


def pack_kernel(b, pot, cap, mat, to_low, to_high):
    lane = lanes((ROWS, COLS))
    for g in range(GROUPS):
        low = jnp.zeros((ROWS, COLS), F32)
        high = jnp.zeros((ROWS, COLS), F32)
        for j in range(min(PER, PLANES - g * PER)):
            v = plane_of(b, pot, cap, mat, g * PER + j)
            inside = (lane >= HALO * j) & (lane < HALO * (j + 1))
            low = jnp.where(inside, turn(v, HALO * j), low)
            high = jnp.where(inside, turn(v, HALO * j + HALO), high)
        to_low[g] = low
        to_high[g] = high


def turn(v, shift):
    shift = shift % v.shape[1]
    return v if shift == 0 else pltpu.roll(v, shift, 1)


def plane_of(b, pot, cap, mat, k):
    if k < FIELDS:
        return b[k]
    which, layer = divmod(k - FIELDS, LAYERS)
    return (pot, cap, mat)[which][layer].astype(F32)


def place(rows):
    n = rows.shape[0]
    total = jnp.sum(rows, axis=1, keepdims=True)
    spread = jnp.where(lanes((n, COLS)) == subs((n, COLS)), total, 0.0)
    return jnp.sum(spread, axis=0, keepdims=True)


def fold(v):
    return jnp.sum(v, axis=0, keepdims=True)


def sums_kernel(b, mat, tail, out, acc):
    acc[...] = jnp.zeros(acc.shape, F32)
    for s in range(SPECIES):
        for m in range(MATS):
            total = jnp.zeros((ROWS, COLS), F32)
            for l in range(LAYERS):
                total = total + jnp.where(mat[l] == m, b[s * LAYERS + l], 0.0)
            acc[m * SPECIES + s : m * SPECIES + s + 1, :] = fold(total)
    row = place(acc[...]) + tail[...]
    out[...] = jnp.broadcast_to(row, (TOTAL, COLS))


def rows_kernel(b, pot, cap, mat, from_low, from_high, to_low, to_high):
    for k in range(PLANES):
        v = plane_of(b, pot, cap, mat, k)
        to_low[k] = v[:RHALO]
        to_high[k] = v[ROWS - RHALO :]
    for g in range(GROUPS):
        for i, part in enumerate((from_low, from_high)):
            k = PLANES + i * GROUPS + g
            to_low[k] = part[g, :RHALO]
            to_high[k] = part[g, ROWS - RHALO :]


def unpack_halo(low, high, j, fill):
    shape = low.shape
    lane = lanes(shape)
    right = turn(high, -HALO * j)
    left = turn(low, -HALO * (j + 1))
    return jnp.where(lane < HALO, right, jnp.where(lane >= COLS - HALO, left, fill))


def a_tile(src, cap, gy, gx, gz, s, row):
    base = s * LAYERS
    here = pl.ds(row, 8)
    below = pl.ds(row - 1, 8)
    above = pl.ds(row + 1, 8)
    us, outs = [], []
    flux_z = None
    for l in range(LAYERS):
        k = base + l
        u = src[k, here, :]
        if l == 0:
            nxt = u
        u = nxt
        flux_x = gx[k, here, :] * (u - pltpu.roll(u, WIDE - 1, 1))
        out = cap[l, here, :] * u + (flux_x - pltpu.roll(flux_x, 1, 1))
        out = out + gy[k, here, :] * (u - src[k, above, :])
        out = out + gy[k, below, :] * (u - src[k, below, :])
        if flux_z is not None:
            out = out - flux_z
        if l + 1 < LAYERS:
            nxt = src[k + 1, here, :]
            flux_z = gz[k, here, :] * (u - nxt)
            out = out + flux_z
        us.append(u)
        outs.append(out)
    return us, outs


def tile_rows(first, last):
    return [PAD + 8 * t for t in range(first, last + 1)]


def sweep(src, resid, dst, ops, tiles):
    cap, gy, gx, gz, scale = ops

    @pl.loop(0, SPECIES)
    def _(s):
        for row in tiles:
            us, outs = a_tile(src, cap, gy, gx, gz, s, row)
            for l in range(LAYERS):
                k = s * LAYERS + l
                here = pl.ds(row, 8)
                dst[k, here, :] = us[l] + scale[k, here, :] * (resid[k, here, :] - outs[l])


def image(src, dst, ops, tiles):
    cap, gy, gx, gz, _ = ops

    @pl.loop(0, SPECIES)
    def _(s):
        for row in tiles:
            _, outs = a_tile(src, cap, gy, gx, gz, s, row)
            for l in range(LAYERS):
                dst[s * LAYERS + l, pl.ds(row, 8), :] = outs[l]


def start_sweep(resid, dst, scale, tiles):
    @pl.loop(0, SPECIES)
    def _(s):
        for row in tiles:
            for l in range(LAYERS):
                k = s * LAYERS + l
                here = pl.ds(row, 8)
                dst[k, here, :] = scale[k, here, :] * resid[k, here, :]


def split3(x):
    hi = x.astype(jnp.bfloat16)
    rest = x - hi.astype(F32)
    mid = rest.astype(jnp.bfloat16)
    lo = (rest - mid.astype(F32)).astype(jnp.bfloat16)
    return jnp.concatenate([hi, mid, lo], axis=0)


def exact_dot(x, onehot):
    n = x.shape[0]
    y = jnp.dot(
        jnp.concatenate([split3(x)], axis=0), onehot, preferred_element_type=F32
    )
    return y[:n] + y[n : 2 * n] + y[2 * n :]


def build_scatter(got, onehot):
    for m in range(MATS):
        col = jnp.broadcast_to(got[:, MAP_LANE + m : MAP_LANE + m + 1], (TOTAL, COLS))
        for k in range(4):
            target = (lanes((TOTAL, COLS)) + k * COLS).astype(F32)
            onehot[m * TOTAL : (m + 1) * TOTAL, k * COLS : (k + 1) * COLS] = jnp.where(
                col == target, 1.0, 0.0
            ).astype(jnp.bfloat16)


def build_gather(turned, onehot):
    for m in range(MATS):
        row = jnp.broadcast_to(turned[MAP_LANE + m : MAP_LANE + m + 1, :], (COLS, TOTAL))
        for k in range(4):
            target = (subs((COLS, TOTAL)) + k * COLS).astype(F32)
            onehot[k * COLS : (k + 1) * COLS, m * TOTAL : (m + 1) * TOTAL] = jnp.where(
                row == target, 1.0, 0.0
            ).astype(jnp.bfloat16)


def build_near(got, onehot):
    gx, gy = lax.axis_index("grp"), lax.axis_index("gy")
    lane = lanes((1, COLS))
    row = jnp.full((1, COLS), -1.0, F32)
    for iy in range(3):
        y = lax.rem(gy + (N_GY - 1 + iy), N_GY)
        for ix in range(3):
            x = jnp.clip(gx + (ix - 1), 0, N_GRP - 1)
            region = iy * 3 + ix
            here = got[pl.ds(x * N_GY + y, 1), :]
            inside = (lane >= region * MATS) & (lane < (region + 1) * MATS)
            row = jnp.where(inside, turn(here, region * MATS - MAP_LANE), row)
    for k in range(4):
        target = (subs((COLS, COLS)) + k * COLS).astype(F32)
        onehot[k * COLS : (k + 1) * COLS, :] = jnp.where(
            jnp.broadcast_to(row, (COLS, COLS)) == target, 1.0, 0.0
        ).astype(jnp.bfloat16)


def coarse_solve(sums, turned, scatter):
    res = exact_dot(sums, scatter[...])
    parts = []
    for k in range(4):
        total = None
        for t in range(SPECIES):
            start = INV_LANE + k * SPECIES * SPECIES + t * SPECIES
            term = turned[start : start + 8, :] * res[t : t + 1, k * COLS : (k + 1) * COLS]
            total = term if total is None else total + term
        parts.append(total)
    sol = jnp.concatenate(parts, axis=1)
    return jnp.where(subs(sol.shape) < SPECIES, sol, 0.0)


def local_sums(turned, group):
    x = jnp.concatenate(
        [turned[(group + m) * SPECIES : (group + m) * SPECIES + 8, :] for m in range(MATS)], axis=1
    )
    return jnp.where(subs(x.shape) < SPECIES, x, 0.0)


def spread_values(near, values):
    lane = lanes((8, COLS))
    for iy in range(3):
        for m in range(MATS):
            cols = [
                jnp.broadcast_to(
                    near[:, (iy * 3 + ix) * MATS + m : (iy * 3 + ix) * MATS + m + 1], (8, COLS)
                )
                for ix in range(3)
            ]
            values[iy * MATS + m, :, 0:COLS] = cols[1]
            values[iy * MATS + m, :, COLS:WIDE] = jnp.where(lane < COLS // 2, cols[2], cols[0])


def region_of(row):
    return 0 if row < TOP else (1 if row < TOP + ROWS else 2)


def coarse_at(values, mat_tile, s, row):
    iy = region_of(row)
    v = [
        jnp.broadcast_to(values[iy * MATS + m, pl.ds(s, 1), :], mat_tile.shape) for m in range(MATS)
    ]
    out = jnp.where(mat_tile == 1.0, v[1], v[0])
    out = jnp.where(mat_tile == 2.0, v[2], out)
    return jnp.where(mat_tile == 3.0, v[3], out)


def fill_plane(dst, index, k, own, x_low, x_high, y_low, y_high, fill):
    g, j = divmod(k, PER)
    dst[index, PAD : PAD + RHALO, 0:COLS] = y_low[k]
    dst[index, TOP : TOP + ROWS, 0:COLS] = own
    dst[index, TOP + ROWS : TOP + ROWS + RHALO, 0:COLS] = y_high[k]
    dst[index, PAD : PAD + RHALO, COLS:WIDE] = unpack_halo(
        y_low[PLANES + g], y_low[PLANES + GROUPS + g], j, fill
    )
    dst[index, TOP : TOP + ROWS, COLS:WIDE] = unpack_halo(x_low[g], x_high[g], j, fill)
    dst[index, TOP + ROWS : TOP + ROWS + RHALO, COLS:WIDE] = unpack_halo(
        y_high[PLANES + g], y_high[PLANES + GROUPS + g], j, fill
    )


def harmonic(a, b):
    return 2.0 * a * b / (a + b)


def first_kernel(
    diff, b, pot, cap, mat, x_low, x_high, y_low, y_high, got,
    second, cap_w, mat_w, gy, gx, gz, scale, z0_out, w0_out, u_out,
    b_w, w, za, zb, w0, scatter, near_hot, turned, values, acc,
):
    halves = (x_low, x_high, y_low, y_high)
    for k in range(FIELDS):
        fill_plane(b_w, k, k, b[k], *halves, 0.0)
    for l in range(LAYERS):
        fill_plane(za, l, FIELDS + l, pot[l], *halves, 0.0)
        fill_plane(cap_w, l, FIELDS + LAYERS + l, cap[l], *halves, 1.0)
        fill_plane(mat_w, l, FIELDS + 2 * LAYERS + l, mat[l].astype(F32), *halves, 0.0)

    for row in tile_rows(0, 7):
        for l in range(LAYERS):
            here = pl.ds(row, 8)
            m = mat_w[l, here, :]
            is1, is2, is3 = m == 1.0, m == 2.0, m == 3.0
            down = jnp.exp(-0.5 * za[l, here, :])
            up = jnp.exp(0.5 * za[l, here, :])
            drift = (down, up, down * down, up * up, down)
            for s in range(SPECIES):
                d = jnp.where(is1, diff[s, 1], diff[s, 0])
                d = jnp.where(is2, diff[s, 2], d)
                d = jnp.where(is3, diff[s, 3], d)
                w[s * LAYERS + l, here, :] = d * drift[s]

    me_x = lax.axis_index("grp")
    lane = lanes((8, WIDE))
    closed = ((lane == COLS - 1) & (me_x == N_GRP - 1)) | ((lane == WIDE - 1) & (me_x == 0))

    @pl.loop(0, SPECIES)
    def _(s):
        for row in tile_rows(0, 7):
            here, above = pl.ds(row, 8), pl.ds(row + 1, 8)
            for l in range(LAYERS):
                k = s * LAYERS + l
                c = w[k, here, :]
                gy[k, here, :] = harmonic(c, w[k, above, :])
                gx[k, here, :] = jnp.where(closed, 0.0, harmonic(c, pltpu.roll(c, WIDE - 1, 1)))
                if l + 1 < LAYERS:
                    gz[k, here, :] = 0.5 * harmonic(c, w[k + 1, here, :])
        for row in tile_rows(0, 7):
            here, below = pl.ds(row, 8), pl.ds(row - 1, 8)
            for l in range(LAYERS):
                k = s * LAYERS + l
                ex = gx[k, here, :]
                d = cap_w[l, here, :] + gy[k, here, :] + gy[k, below, :] + ex + pltpu.roll(ex, 1, 1)
                if l + 1 < LAYERS:
                    d = d + gz[k, here, :]
                if l > 0:
                    d = d + gz[k - 1, here, :]
                scale[k, here, :] = DAMPING / d

    ops = (cap_w, gy, gx, gz, scale)
    all_tiles, mid, own = tile_rows(0, 7), tile_rows(1, 6), tile_rows(2, 5)

    turned[...] = got[...].T
    build_scatter(got, scatter)
    build_near(got, near_hot)
    sol = coarse_solve(local_sums(turned, 0), turned, scatter)
    spread_values(exact_dot(sol, near_hot[...]), values)

    start_sweep(b_w, za, scale, all_tiles)
    sweep(za, b_w, zb, ops, all_tiles)
    sweep(zb, b_w, za, ops, all_tiles)

    cap_o, gy_o, gx_o, gz_o, scale_o = ops

    @pl.loop(0, SPECIES)
    def _(s):
        for row in mid:
            here = pl.ds(row, 8)
            us, outs = a_tile(za, cap_o, gy_o, gx_o, gz_o, s, row)
            for l in range(LAYERS):
                k = s * LAYERS + l
                smooth = us[l] + scale[k, here, :] * (b_w[k, here, :] - outs[l])
                zb[k, here, :] = smooth + coarse_at(values, mat_w[l, here, :], s, row)

    for k in range(FIELDS):
        z0_out[k] = zb[k, TOP : TOP + ROWS, 0:COLS]
    image(zb, w0, ops, mid)
    for k in range(FIELDS):
        w0_out[k] = w0[k, TOP : TOP + ROWS, 0:COLS]
    start_sweep(w0, za, scale, mid)
    sweep(za, w0, zb, ops, mid)
    sweep(zb, w0, za, ops, mid)
    sweep(za, w0, u_out, ops, mid)

    acc[...] = jnp.zeros(acc.shape, F32)
    own_lane = lanes((8, COLS))
    sub = subs((8, COLS))

    @pl.loop(0, SPECIES)
    def _(s):
        def keep(group, v):
            acc[pl.ds(group * SPECIES + s, 1), :] = fold(v)

        zero = jnp.zeros((8, COLS), F32)
        rw, rau, mom = [zero] * MATS, [zero] * MATS, [zero] * 4
        pairs, cy, cx = [zero] * 6, [zero] * 16, [zero] * 16
        codes = (3.0, 5.0, 9.0, 6.0, 10.0, 12.0)

        def power(m):
            p = jnp.where(m == 1.0, 2.0, 1.0)
            p = jnp.where(m == 2.0, 4.0, p)
            return jnp.where(m == 3.0, 8.0, p)

        for row in own:
            here = pl.ds(row, 8)
            above = pl.ds(row + 1, 8)
            us, outs = a_tile(u_out, cap_o, gy_o, gx_o, gz_o, s, row)
            side_g, side_c = zero, zero - 1.0
            for l in range(LAYERS):
                k = s * LAYERS + l
                m_wide = mat_w[l, here, :]
                m = m_wide[:, :COLS]
                u, au = us[l][:, :COLS], outs[l][:, :COLS]
                wv, zv, bv = w0_out[k, row - TOP : row - TOP + 8, :], z0_out[k, row - TOP : row - TOP + 8, :], b[k, row - TOP : row - TOP + 8, :]
                mom[0] = mom[0] + bv * zv
                mom[1] = mom[1] + zv * wv
                mom[2] = mom[2] + wv * u
                mom[3] = mom[3] + u * au
                for i in range(MATS):
                    is_i = m == float(i)
                    rw[i] = rw[i] + jnp.where(is_i, wv, 0.0)
                    rau[i] = rau[i] + jnp.where(is_i, au, 0.0)
                m_y = mat_w[l, above, 0:COLS]
                m_x = pltpu.roll(m_wide, WIDE - 1, 1)[:, :COLS]
                ey, ex = gy[k, here, 0:COLS], gx[k, here, 0:COLS]
                p = power(m)
                last = row == own[-1]
                code = p + power(m_y)
                if last:
                    code = jnp.where(sub == 7, 0.0, code)
                kinds = [(code, ey), (jnp.where(own_lane == COLS - 1, 0.0, p + power(m_x)), ex)]
                if l + 1 < LAYERS:
                    kinds.append((p + power(mat_w[l + 1, here, 0:COLS]), gz[k, here, 0:COLS]))
                for code, edge in kinds:
                    for i in range(6):
                        pairs[i] = pairs[i] + jnp.where(code == codes[i], edge, 0.0)
                if last:
                    code = jnp.where(sub == 7, m * 4.0 + m_y, -1.0)
                    for i in range(16):
                        cy[i] = cy[i] + jnp.where(code == float(i), ey, 0.0)
                at_end = own_lane == COLS - 1 - l
                side_g = jnp.where(at_end, turn(ex, -l), side_g)
                side_c = jnp.where(at_end, turn(m * 4.0 + m_x, -l), side_c)
            for i in range(16):
                cx[i] = cx[i] + jnp.where(side_c == float(i), side_g, 0.0)
        for i in range(MATS):
            keep(G_RW + i, rw[i])
            keep(G_RAU + i, rau[i])
            keep(G_MOM + i, mom[i])
        for i in range(6):
            keep(G_S + i, pairs[i])
        for i in range(16):
            keep(G_CY + i, cy[i])
            keep(G_CX + i, cx[i])

    for i in range(MATS):
        total = jnp.zeros((ROWS, COLS), F32)
        for l in range(LAYERS):
            total = total + jnp.where(mat[l] == i, cap[l], 0.0)
        acc[ROW_CAP + i : ROW_CAP + i + 1, :] = fold(total)
    second[:, 0:COLS] = jnp.broadcast_to(place(acc[0:COLS, :]), (TOTAL, COLS))
    second[:, COLS:WIDE] = jnp.broadcast_to(place(acc[COLS:WIDE, :]), (TOTAL, COLS))


def next_y(x):
    y = lax.rem(lanes(x.shape), N_GY)
    return jnp.where(y == N_GY - 1, turn(x, N_GY - 1), turn(x, -1))


def prev_y(x):
    y = lax.rem(lanes(x.shape), N_GY)
    return jnp.where(y == 0, turn(x, -(N_GY - 1)), turn(x, 1))


def total_of(x):
    return jnp.sum(jnp.sum(x, axis=0, keepdims=True), axis=1, keepdims=True)


def second_kernel(
    b, got, got2, cap, mat, gy, gx, gz, scale, z0, w0, u,
    out_x, out_r, out_z,
    v1, w1, za, zb, scatter, gather, near_hot, turned, turned2, values, values2,
):
    turned[...] = got[...].T
    turned2[0:COLS, :] = got2[:, 0:COLS].T
    turned2[COLS:WIDE, :] = got2[:, COLS:WIDE].T
    build_scatter(got, scatter)
    build_gather(turned, gather)
    build_near(got, near_hot)

    sums_w = local_sums(turned2, G_RW)
    sol = coarse_solve(sums_w, turned, scatter)
    spread_values(exact_dot(sol, near_hot[...]), values)
    c_all = exact_dot(sol, gather[...])
    c = [c_all[:, m * TOTAL : (m + 1) * TOTAL] for m in range(MATS)]

    def rows5(group):
        return turned2[group * SPECIES : group * SPECIES + 8, :]

    live = subs((8, TOTAL)) < SPECIES
    bc = [turned2[ROW_CAP + m : ROW_CAP + m + 1, :] * c[m] for m in range(MATS)]
    n = 0
    for i in range(MATS):
        for j in range(i + 1, MATS):
            f = rows5(G_S + n) * (c[i] - c[j])
            bc[i] = bc[i] + f
            bc[j] = bc[j] - f
            n += 1
    c_y = [next_y(v) for v in c]
    c_x = [turn(v, -N_GY) for v in c]
    back_y = [jnp.zeros((8, TOTAL), F32)] * MATS
    back_x = [jnp.zeros((8, TOTAL), F32)] * MATS
    for i in range(MATS):
        for j in range(MATS):
            f = rows5(G_CY + 4 * i + j) * (c[i] - c_y[j])
            bc[i] = bc[i] + f
            back_y[j] = back_y[j] + f
            f = rows5(G_CX + 4 * i + j) * (c[i] - c_x[j])
            bc[i] = bc[i] + f
            back_x[j] = back_x[j] + f
    for j in range(MATS):
        bc[j] = jnp.where(live, bc[j] - prev_y(back_y[j]) - turn(back_x[j], N_GY), 0.0)
    bc_all = jnp.concatenate(bc, axis=1)
    sums_au = local_sums(turned2, G_RAU)
    sol2 = coarse_solve(sums_au + bc_all, turned, scatter)
    spread_values(exact_dot(sol2, near_hot[...]), values2)

    def moment(i):
        return total_of(jnp.where(live, rows5(G_MOM + i), 0.0))

    m0, m1 = moment(0), moment(1)
    m2 = moment(2) + total_of(sums_w * c_all)
    m3 = moment(3) + total_of((2.0 * sums_au + bc_all) * c_all)
    a0 = m0 / m1
    rz1 = m0 - 2.0 * a0 * m1 + a0 * a0 * m2
    g = 1.0 + rz1 / m0
    a1 = rz1 / (g * g * m1 - 2.0 * a0 * g * m2 + a0 * a0 * m3)
    ca = jnp.broadcast_to(a0 + a1 * g, (8, COLS))
    cb = jnp.broadcast_to(a1 * a0, (8, COLS))

    ops = (cap, gy, gx, gz, scale)
    mid, own = tile_rows(1, 6), tile_rows(2, 5)

    @pl.loop(0, SPECIES)
    def _(s):
        for row in mid:
            here = pl.ds(row, 8)
            for l in range(LAYERS):
                k = s * LAYERS + l
                v1[k, here, :] = u[k, here, :] + coarse_at(values, mat[l, here, :], s, row)

    image(v1, w1, ops, mid)
    start_sweep(w1, za, scale, mid)
    sweep(za, w1, zb, ops, mid)
    sweep(zb, w1, za, ops, mid)

    @pl.loop(0, SPECIES)
    def _(s):
        for row in own:
            here = pl.ds(row, 8)
            us, outs = a_tile(za, cap, gy, gx, gz, s, row)
            for l in range(LAYERS):
                k = s * LAYERS + l
                w1v = w1[k, here, :]
                v2 = us[l] + scale[k, here, :] * (w1v - outs[l])
                v2 = (v2 + coarse_at(values2, mat[l, here, :], s, row))[:, :COLS]
                w1v = w1v[:, :COLS]
                v1v = v1[k, here, 0:COLS]
                rows = pl.ds(row - TOP, 8)
                z0v, w0v = z0[k, rows, :], w0[k, rows, :]
                out_x[k, rows, :] = ca * z0v - cb * v1v
                out_r[k, rows, :] = b[k, rows, :] - ca * w0v + cb * w1v
                out_z[k, rows, :] = z0v - ca * v1v + cb * v2


def shape(*dims):
    return jax.ShapeDtypeStruct(dims, F32)


VMEM = pl.BlockSpec(memory_space=pltpu.VMEM)
SMEM = pl.BlockSpec(memory_space=pltpu.SMEM)
PARAMS = pltpu.CompilerParams(vmem_limit_bytes=56 * 1024 * 1024)


def run(kernel, outs, scratch, in_specs, *args):
    return pl.pallas_call(
        kernel,
        out_shape=outs,
        in_specs=in_specs,
        out_specs=jax.tree.map(lambda _: VMEM, outs),
        scratch_shapes=scratch,
        compiler_params=PARAMS,
    )(*args)


def shifts(axis, count):
    forward = [(i, (i + 1) % count) for i in range(count)]
    backward = [(target, source) for source, target in forward]
    return (functools.partial(lax.ppermute, axis_name=axis, perm=p) for p in (forward, backward))


def to_all(rows):
    width = rows.shape[1]
    got = lax.all_to_all(rows.reshape(TOTAL, 1, width), BOTH, 0, 0, tiled=True)
    return got.reshape(TOTAL, width)


def body(right_side, potential, capacity, diffusivity, material, coarse_map, coarse_inverse):
    b = right_side.reshape(FIELDS, ROWS, COLS)
    own = (b, potential, capacity, material)
    right, left = shifts("grp", N_GRP)
    down, up = shifts("gy", N_GY)

    packed = shape(GROUPS, ROWS, COLS)
    to_low, to_high = run(pack_kernel, (packed, packed), [], [VMEM] * 4, *own)
    x_low, x_high = right(to_high), left(to_low)

    q = coarse_map.reshape(-1)
    tail = jnp.concatenate(
        [
            jnp.zeros((MAP_LANE,), F32),
            ((q & 3) * TOTAL + (q >> 2)).astype(F32),
            coarse_inverse.reshape(-1),
            jnp.zeros((COLS - INV_LANE - 100,), F32),
        ]
    ).reshape(1, COLS)
    first = run(
        sums_kernel, shape(TOTAL, COLS), [pltpu.VMEM((24, COLS), F32)], [VMEM] * 3, b, material, tail
    )

    strips = shape(PLANES + 2 * GROUPS, RHALO, COLS)
    to_low, to_high = run(rows_kernel, (strips, strips), [], [VMEM] * 6, *own, x_low, x_high)
    first, to_low, to_high = lax.optimization_barrier((first, to_low, to_high))
    y_low, y_high = down(to_high), up(to_low)
    got = to_all(first)

    wide = shape(FIELDS, TALL, WIDE)
    thin = shape(LAYERS, TALL, WIDE)
    field = shape(FIELDS, ROWS, COLS)
    big = pltpu.VMEM((FIELDS, TALL, WIDE), F32)
    hot = pltpu.VMEM((NC, MATS * TOTAL), jnp.bfloat16)
    near = pltpu.VMEM((NC, COLS), jnp.bfloat16)
    square = pltpu.VMEM((COLS + 8, COLS), F32)
    values = pltpu.VMEM((3 * MATS, 8, WIDE), F32)
    second, cap_w, mat_w, gy, gx, gz, scale, z0, w0, u = run(
        first_kernel,
        (shape(TOTAL, WIDE), thin, thin, wide, wide, wide, wide, field, field, wide),
        [big] * 5 + [hot, near, pltpu.VMEM((COLS, COLS), F32), values, pltpu.VMEM((WIDE, COLS), F32)],
        [SMEM] + [VMEM] * 9,
        diffusivity, *own, x_low, x_high, y_low, y_high, got,
    )
    got2 = to_all(second)
    out = run(
        second_kernel,
        (field, field, field),
        [big] * 4
        + [hot, hot, near, pltpu.VMEM((COLS, COLS), F32), pltpu.VMEM((WIDE, COLS), F32), values, values],
        [VMEM] * 12,
        b, got, got2, cap_w, mat_w, gy, gx, gz, scale, z0, w0, u,
    )
    return tuple(o.reshape(right_side.shape) for o in out)


def solution(mesh):
    placed = (
        P(None, None, "gy", "grp"),
        P(None, "gy", "grp"),
        P(None, "gy", "grp"),
        P(),
        P(None, "gy", "grp"),
        P("gy", "grp", None),
        P(("grp", "gy"), None, None),
    )
    return jax.shard_map(
        body,
        mesh=mesh,
        in_specs=placed,
        out_specs=(P(None, None, "gy", "grp"),) * 3,
        check_vma=False,
    )
```

time: 753 us -> 83.2 us (0.11); the launches traced: 739 us -> 82.8 us
  blocking collectives: 511 us -> 14.4 us
  waiting for transfers between devices: 111 us -> 8.66 us
  starting transfers between devices: 69.7 us -> 15.3 us
  Pallas kernels: 0 us -> 37.3 us
  other arithmetic: 25 us -> 1.31 us
  local copies, waits for them, and re-layouts: 18 us -> 5.22 us
    psum x3 -> x0, blocking collectives: 201 us -> none  [the longest x2 134 us: precondition(): return (result, lax.psum(jnp.sum(resid * result), ('grp', 'gy')))]
    unnamed x3 -> x0, blocking collectives: 198 us -> none
    all_gather x3 -> x0, blocking collectives: 111 us -> none  [coarse(): coarse_sol = lax.all_gather(owned_sol, ('grp', 'gy'), axis=0, tiled=True)]
    ppermute x48 -> x4, waiting for transfers between devices: 111 us -> 0.01 us  [the longest x2 0.01 us: body(): y_low, y_high = (down(to_high), up(to_low))]
    ppermute x48 -> x4, starting transfers between devices: 69.7 us -> 6.27 us  [the longest x2 3.57 us: body(): x_low, x_high = (right(to_high), left(to_low))]
    pallas_call x0 -> x5, Pallas kernels: none -> 37.3 us  [run(): pl.pallas_call(kernel, out_shape=outs, in_specs=in_specs, out_specs=jax.t...]
    all_to_all x0 -> x1, blocking collectives: none -> 14.4 us  [to_all(): got = lax.all_to_all(rows.reshape(TOTAL, 1, width), BOTH, 0, 0, tiled=True)]
    add x10 -> x0, other arithmetic: 11.7 us -> none  [the longest x6 8.31 us: smooth(): approx = approx + DAMPING * (resid - image_of(approx)) / own_diag]
  transfers between devices with their start and end apart: 48 -> 5, of which waited for: 40 -> 1; matrix products, arithmetic and copies ran while one was open for 1% -> 3% of each run, Pallas kernels for 0% -> 2%
where the time goes in v1:
time: 83.2 us; the launch traced here: 82.8 us
  Pallas kernels  37.3 us (45%)
  starting transfers between devices  15.3 us (18%)
  blocking collectives  14.4 us (17%)
  waiting for transfers between devices  8.66 us (10%)
  local copies, waits for them, and re-layouts  5.22 us (6%)
  other arithmetic  1.31 us (2%)
    pallas_call x5, Pallas kernels, run(): pl.pallas_call(kernel, out_shape=outs, in_specs=in_specs, out_specs=jax.t...  37.3 us
    all_to_all x1, blocking collectives, to_all(): got = lax.all_to_all(rows.reshape(TOTAL, 1, width), BOTH, 0, 0, tiled=True)  14.4 us
    all_to_all x1, starting transfers between devices, to_all(): got = lax.all_to_all(rows.reshape(TOTAL, 1, width), BOTH, 0, 0, tiled=True)  9 us
    all_to_all x1, waiting for transfers between devices, to_all(): got = lax.all_to_all(rows.reshape(TOTAL, 1, width), BOTH, 0, 0, tiled=True)  8.65 us
    unnamed x15, local copies, waits for them, and re-layouts  4.09 us
    ppermute x2, starting transfers between devices, body(): x_low, x_high = (right(to_high), left(to_low))  3.57 us
    ppermute x2, starting transfers between devices, body(): y_low, y_high = (down(to_high), up(to_low))  2.7 us
  transfers between devices with their start and end apart: 5, of which 1 were waited for; matrix products, arithmetic and copies ran while one was open for 3% of the time, Pallas kernels for 2%

profile of v1, /device:TPU:1, one launch (start us, length us, event | category | flops | bytes accessed | tf_op | source)
XLA Modules:
  0.0 82.8 jit_solution(3210280762046440605)
XLA Ops:
  0.6 0.0 copy-start.5
  0.6 2.0 %shard_map.95 = (f32[4,32,128]{2,1,0:T(8,128)}, f32[4,32,128]{2,1,0:T(8,128)}) custom-call(f32[20,32,128]{2,1,0:T(8,128)} %bitcast.16, f32[4,32,128]{2,1,0:T(8,128)} %pot.5, f32[4,32,128]{2,1,0:T(8,128)} %cap.5, s32[4,32,128]{2,1,0:T(8,128)} %mat.7), custom_call_target="tpu_custom_call" | custom-call | tf_op jit(solution)/shard_map/pallas_call | solution.py:595
  2.6 2.1 %collective-permute-start = (f32[4,32,128]{2,1,0:T(8,128)}, f32[4,32,128]{2,1,0:T(8,128)S(1)}, u32[]{:S(2)}, u32[]{:S(2)}) collective-permute-start(f32[4,32,128]{2,1,0:T(8,128)} %get-tuple-element.23), channel_id=1, source_target_pairs={{0,32},{32,64},{64,96},{96,0},{1,33},{33,65},{65,97},{97,1},{2,34}... | collective-permute-start | bytes 196616 | tf_op jit(solution)/shard_map/ppermute | solution.py:625
  4.8 1.4 %collective-permute-start.1 = (f32[4,32,128]{2,1,0:T(8,128)}, f32[4,32,128]{2,1,0:T(8,128)S(1)}, u32[]{:S(2)}, u32[]{:S(2)}) collective-permute-start(f32[4,32,128]{2,1,0:T(8,128)} %get-tuple-element.24), channel_id=1, source_target_pairs={{32,0},{64,32},{96,64},{0,96},{33,1},{65,33},{97,65},{1,97},{34,2}... | collective-permute-start | bytes 196616 | tf_op jit(solution)/shard_map/ppermute | solution.py:625
  6.2 0.7 convert_bitcast_fusion
  6.9 0.7 copy.14
  7.6 0.1 reshape.46
  7.7 0.7 maximum_bitcast_fusion.tail
  8.3 1.9 %shard_map.94 = f32[128,128]{1,0:T(8,128)} custom-call(f32[20,32,128]{2,1,0:T(8,128)} %bitcast.17, s32[4,32,128]{2,1,0:T(8,128)} %mat.7, f32[1,128]{1,0:T(1,128)} %maximum_bitcast_fusion.tail), custom_call_target="tpu_custom_call" | custom-call | tf_op jit(solution)/shard_map/pallas_call | solution.py:595
  10.2 0.0 collective-permute-done.from_low.x_low
  10.2 0.0 copy-start.3
  10.2 0.0 collective-permute-done.1.from_high.x_high
  10.2 0.6 copy-done.3
  10.8 0.0 copy-start.4
  10.8 0.6 copy-done.4
  11.4 1.9 %shard_map.96 = (f32[40,16,128]{2,1,0:T(8,128)}, f32[40,16,128]{2,1,0:T(8,128)}) custom-call(f32[20,32,128]{2,1,0:T(8,128)} %bitcast.18, f32[4,32,128]{2,1,0:T(8,128)} %pot.5, f32[4,32,128]{2,1,0:T(8,128)} %cap.5, s32[4,32,128]{2,1,0:T(8,128)} %mat.7, f32[4,32,128]{2,1,0:T(8,128)} %copy-done.3, f32[4,32,128]{2,1,0:T(8,128)} %copy-done.4), custom_call_target="tpu_custom_call" | custom-call | tf_op jit(solution)/shard_map/pallas_call | solution.py:595
  13.4 2.7 %collective-permute-start.2 = (f32[40,16,128]{2,1,0:T(8,128)}, f32[40,16,128]{2,1,0:T(8,128)S(1)}, u32[]{:S(2)}, u32[]{:S(2)}) collective-permute-start(f32[40,16,128]{2,1,0:T(8,128)} %get-tuple-element.28), channel_id=1, source_target_pairs={{0,1},{1,2},{2,3},{3,4},{4,5},{5,6},{6,7},{7,8},{8,9},{9,10},{10,1... | collective-permute-start | bytes 983048 | tf_op jit(solution)/shard_map/ppermute | solution.py:643
  16.1 0.0 collective-permute-start.3
  16.1 9.0 %all-to-all-start = ((f32[128,1,128]{2,1,0:T(1,128)}), f32[128,1,128]{2,1,0:T(1,128)S(1)}, u32[]{:S(2)}, u32[]{:S(2)}) async-start(f32[128,1,128]{2,1,0:T(1,128)} %bitcast.24), calls=%async_computation | async-start | bytes 131072 | tf_op jit(solution)/shard_map/all_to_all | solution.py:613
  25.1 0.0 copy-done.5
  25.1 0.7 copy.16.diff
  25.8 8.6 %all-to-all-done = f32[128,1,128]{2,1,0:T(1,128)S(1)} async-done(((f32[128,1,128]{2,1,0:T(1,128)}), f32[128,1,128]{2,1,0:T(1,128)S(1)}, u32[]{:S(2)}, u32[]{:S(2)}) %all-to-all-start) | async-done | bytes 65568 | tf_op jit(solution)/shard_map/all_to_all | solution.py:613
  34.4 0.0 copy-start
  34.4 0.0 collective-permute-done.2.y_low
  34.4 0.0 copy-start.1
  34.4 0.0 collective-permute-done.3.y_high
  34.4 0.0 copy-start.2
  34.4 0.6 copy-done
  35.0 0.1 copy-done.1
  35.1 0.1 copy-done.2
  35.3 20.1 %shard_map.97 = (f32[128,256]{1,0:T(8,128)}, f32[4,80,256]{2,1,0:T(8,128)}, f32[4,80,256]{2,1,0:T(8,128)}, f32[20,80,256]{2,1,0:T(8,128)}, f32[20,80,256]{2,1,0:...) custom-call(f32[5,4]{1,0:T(8,128)} %copy.16.diff, ...), custom_call_target="tpu_custom_call" | custom-call | tf_op jit(solution)/shard_map/pallas_call | solution.py:595
  55.3 1.0 %copy.17 = f32[128,1,256]{2,1,0:T(1,128)S(1)} copy(f32[128,1,256]{2,0,1:T(8,128)} %bitcast.25) | data formatting | bytes 262144 | tf_op jit(solution)/shard_map/reshape | solution.py:613
  56.4 14.4 %all_to_all.10 = f32[128,1,256]{2,1,0:T(1,128)S(1)} all-to-all(f32[128,1,256]{2,1,0:T(1,128)S(1)} %copy.17), channel_id=1, replica_groups=mesh['grp'=4,'gy'=32] {'grp','gy'}, dimensions={0} | all-to-all | bytes 262144 | tf_op jit(solution)/shard_map/all_to_all | solution.py:613
  70.8 0.7 copy.20
  71.4 11.4 %shard_map.98 = (f32[20,32,128]{2,1,0:T(8,128)}, f32[20,32,128]{2,1,0:T(8,128)}, f32[20,32,128]{2,1,0:T(8,128)}) custom-call(f32[20,32,128]{2,1,0:T(8,128)} %bitcast.20, f32[128,128]{1,0:T(8,128)} %bitcast.22, f32[128,256]{1,0:T(8,128)} %bitcast.23, f32[4,80,256]{2,1,0:T(8,128)} %get-tuple-element.31.cap, f32[4,80,256]{2,1,0:T(8,128)} %get-tuple-element.32.mat, ...), custom_call_target="tpu_custom_call" | custom-call | tf_op jit(solution)/shard_map/pallas_call | solution.py:595
  (2 shorter events, 0.0 us)
Async XLA Ops:
  0.6 24.4 %copy-start.5 = (f32[5,4]{0,1:T(4,128)S(1)}, f32[5,4]{0,1:T(4,128)}, u32[]{:S(2)}) copy-start(f32[5,4]{0,1:T(4,128)} %param.10) | copy-start | bytes 244
  2.6 7.6 %collective-permute-start = (f32[4,32,128]{2,1,0:T(8,128)}, f32[4,32,128]{2,1,0:T(8,128)S(1)}, u32[]{:S(2)}, u32[]{:S(2)}) collective-permute-start(f32[4,32,128]{2,1,0:T(8,128)} %get-tuple-element.23), channel_id=1, source_target_pairs={{0,32},{32,64},{64,96},{96,0},{1,33},{33,65},{65,97},{97,1},{2,34}... | collective-permute-start | bytes 196616 | tf_op jit(solution)/shard_map/ppermute | solution.py:625
  4.8 5.5 %collective-permute-start.1 = (f32[4,32,128]{2,1,0:T(8,128)}, f32[4,32,128]{2,1,0:T(8,128)S(1)}, u32[]{:S(2)}, u32[]{:S(2)}) collective-permute-start(f32[4,32,128]{2,1,0:T(8,128)} %get-tuple-element.24), channel_id=1, source_target_pairs={{32,0},{64,32},{96,64},{0,96},{33,1},{65,33},{97,65},{1,97},{34,2}... | collective-permute-start | bytes 196616 | tf_op jit(solution)/shard_map/ppermute | solution.py:625
  10.2 0.6 copy-start.3
  10.8 0.6 copy-start.4
  13.4 21.0 %collective-permute-start.2 = (f32[40,16,128]{2,1,0:T(8,128)}, f32[40,16,128]{2,1,0:T(8,128)S(1)}, u32[]{:S(2)}, u32[]{:S(2)}) collective-permute-start(f32[40,16,128]{2,1,0:T(8,128)} %get-tuple-element.28), channel_id=1, source_target_pairs={{0,1},{1,2},{2,3},{3,4},{4,5},{5,6},{6,7},{7,8},{8,9},{9,10},{10,1... | collective-permute-start | bytes 983048 | tf_op jit(solution)/shard_map/ppermute | solution.py:643
  16.1 18.4 %collective-permute-start.3 = (f32[40,16,128]{2,1,0:T(8,128)}, f32[40,16,128]{2,1,0:T(8,128)S(1)}, u32[]{:S(2)}, u32[]{:S(2)}) collective-permute-start(f32[40,16,128]{2,1,0:T(8,128)} %get-tuple-element.29), channel_id=1, source_target_pairs={{1,0},{2,1},{3,2},{4,3},{5,4},{6,5},{7,6},{8,7},{9,8},{10,9},{11,1... | collective-permute-start | bytes 983048 | tf_op jit(solution)/shard_map/ppermute | solution.py:643
  16.1 18.3 %all-to-all-start = ((f32[128,1,128]{2,1,0:T(1,128)}), f32[128,1,128]{2,1,0:T(1,128)S(1)}, u32[]{:S(2)}, u32[]{:S(2)}) async-start(f32[128,1,128]{2,1,0:T(1,128)} %bitcast.24), calls=%async_computation | async-start | bytes 131072 | tf_op jit(solution)/shard_map/all_to_all | solution.py:613
  34.4 0.6 copy-start
  34.4 0.7 copy-start.1
  34.4 0.8 %copy-start.2 = (f32[40,16,128]{2,1,0:T(8,128)}, f32[40,16,128]{2,1,0:T(8,128)S(1)}, u32[]{:S(2)}) copy-start(f32[40,16,128]{2,1,0:T(8,128)S(1)} %collective-permute-done.3.y_high) | copy-start | bytes 983044

commit v2 on v1

--- a/solution.py
+++ b/solution.py
@@ -82,15 +82,25 @@
     return jnp.sum(v, axis=0, keepdims=True)
 
 
-def sums_kernel(b, mat, tail, out, acc):
+def sums_kernel(b, mat, cmap, inverse, out, acc, ids):
     acc[...] = jnp.zeros(acc.shape, F32)
+    row = jnp.zeros((1, COLS), F32)
+    for s in range(SPECIES):
+        acc[0:4, 0:SPECIES] = inverse[s]
+        for k in range(4):
+            row = row + turn(acc[k : k + 1, :], INV_LANE + (k * SPECIES + s) * SPECIES)
+    acc[0:4, :] = jnp.zeros((4, COLS), F32)
+    ids[...] = jnp.zeros(ids.shape, jnp.int32)
+    ids[0:1, 0:MATS] = cmap[0]
+    q = ids[0:1, :]
+    row = row + turn(((q & 3) * TOTAL + (q >> 2)).astype(F32), MAP_LANE)
     for s in range(SPECIES):
         for m in range(MATS):
             total = jnp.zeros((ROWS, COLS), F32)
             for l in range(LAYERS):
                 total = total + jnp.where(mat[l] == m, b[s * LAYERS + l], 0.0)
             acc[m * SPECIES + s : m * SPECIES + s + 1, :] = fold(total)
-    row = place(acc[...]) + tail[...]
+    row = row + place(acc[...])
     out[...] = jnp.broadcast_to(row, (TOTAL, COLS))
 
 
@@ -324,9 +334,9 @@
             up = jnp.exp(0.5 * za[l, here, :])
             drift = (down, up, down * down, up * up, down)
             for s in range(SPECIES):
-                d = jnp.where(is1, diff[s, 1], diff[s, 0])
-                d = jnp.where(is2, diff[s, 2], d)
-                d = jnp.where(is3, diff[s, 3], d)
+                d = jnp.where(is1, diff[1, s], diff[0, s])
+                d = jnp.where(is2, diff[2, s], d)
+                d = jnp.where(is3, diff[3, s], d)
                 w[s * LAYERS + l, here, :] = d * drift[s]
 
     me_x = lax.axis_index("grp")
@@ -467,8 +477,8 @@
         for l in range(LAYERS):
             total = total + jnp.where(mat[l] == i, cap[l], 0.0)
         acc[ROW_CAP + i : ROW_CAP + i + 1, :] = fold(total)
-    second[:, 0:COLS] = jnp.broadcast_to(place(acc[0:COLS, :]), (TOTAL, COLS))
-    second[:, COLS:WIDE] = jnp.broadcast_to(place(acc[COLS:WIDE, :]), (TOTAL, COLS))
+    even = lax.rem(subs((WIDE, COLS)), 2) == 0
+    second[...] = jnp.where(even, place(acc[0:COLS, :]), place(acc[COLS:WIDE, :]))
 
 
 def next_y(x):
@@ -491,8 +501,8 @@
     v1, w1, za, zb, scatter, gather, near_hot, turned, turned2, values, values2,
 ):
     turned[...] = got[...].T
-    turned2[0:COLS, :] = got2[:, 0:COLS].T
-    turned2[COLS:WIDE, :] = got2[:, COLS:WIDE].T
+    turned2[0:COLS, :] = got2[pl.ds(0, TOTAL, stride=2), :].T
+    turned2[COLS:WIDE, :] = got2[pl.ds(1, TOTAL, stride=2), :].T
     build_scatter(got, scatter)
     build_gather(turned, gather)
     build_near(got, near_hot)
@@ -588,7 +598,7 @@
 
 VMEM = pl.BlockSpec(memory_space=pltpu.VMEM)
 SMEM = pl.BlockSpec(memory_space=pltpu.SMEM)
-PARAMS = pltpu.CompilerParams(vmem_limit_bytes=56 * 1024 * 1024)
+PARAMS = pltpu.CompilerParams(vmem_limit_bytes=26 * 1024 * 1024)
 
 
 def run(kernel, outs, scratch, in_specs, *args):
@@ -609,9 +619,8 @@
 
 
 def to_all(rows):
-    width = rows.shape[1]
-    got = lax.all_to_all(rows.reshape(TOTAL, 1, width), BOTH, 0, 0, tiled=True)
-    return got.reshape(TOTAL, width)
+    got = lax.all_to_all(rows.reshape(TOTAL, -1, COLS), BOTH, 0, 0, tiled=True)
+    return got.reshape(rows.shape)
 
 
 def body(right_side, potential, capacity, diffusivity, material, coarse_map, coarse_inverse):
@@ -624,17 +633,12 @@
     to_low, to_high = run(pack_kernel, (packed, packed), [], [VMEM] * 4, *own)
     x_low, x_high = right(to_high), left(to_low)
 
-    q = coarse_map.reshape(-1)
-    tail = jnp.concatenate(
-        [
-            jnp.zeros((MAP_LANE,), F32),
-            ((q & 3) * TOTAL + (q >> 2)).astype(F32),
-            coarse_inverse.reshape(-1),
-            jnp.zeros((COLS - INV_LANE - 100,), F32),
-        ]
-    ).reshape(1, COLS)
     first = run(
-        sums_kernel, shape(TOTAL, COLS), [pltpu.VMEM((24, COLS), F32)], [VMEM] * 3, b, material, tail
+        sums_kernel,
+        shape(TOTAL, COLS),
+        [pltpu.VMEM((24, COLS), F32), pltpu.VMEM((8, COLS), jnp.int32)],
+        [VMEM] * 4,
+        b, material, coarse_map, jnp.transpose(coarse_inverse, (1, 0, 2)),
     )
 
     strips = shape(PLANES + 2 * GROUPS, RHALO, COLS)
@@ -653,10 +657,10 @@
     values = pltpu.VMEM((3 * MATS, 8, WIDE), F32)
     second, cap_w, mat_w, gy, gx, gz, scale, z0, w0, u = run(
         first_kernel,
-        (shape(TOTAL, WIDE), thin, thin, wide, wide, wide, wide, field, field, wide),
+        (shape(2 * TOTAL, COLS), thin, thin, wide, wide, wide, wide, field, field, wide),
         [big] * 5 + [hot, near, pltpu.VMEM((COLS, COLS), F32), values, pltpu.VMEM((WIDE, COLS), F32)],
         [SMEM] + [VMEM] * 9,
-        diffusivity, *own, x_low, x_high, y_low, y_high, got,
+        diffusivity.T, *own, x_low, x_high, y_low, y_high, got,
     )
     got2 = to_all(second)
     out = run(

time: 83.2 us -> 75 us (0.901)
  blocking collectives: 14.4 us -> 33.5 us
  Pallas kernels: 37.3 us -> 26.5 us
  waiting for transfers between devices: 8.66 us -> 0.01 us
  starting transfers between devices: 15.3 us -> 7.38 us
  other arithmetic: 1.31 us -> 0 us
  local copies, waits for them, and re-layouts: 5.22 us -> 6.52 us
    all_to_all x1 -> x2, blocking collectives: 14.4 us -> 33.5 us  [to_all(): got = lax.all_to_all(rows.reshape(TOTAL, -1, COLS), BOTH, 0, 0, tiled=True)]
    pallas_call x5, Pallas kernels: 37.3 us -> 26.5 us  [run(): pl.pallas_call(kernel, out_shape=outs, in_specs=in_specs, out_specs=jax.t...]
    all_to_all x1 -> x0, starting transfers between devices: 9 us -> none  [to_all(): got = lax.all_to_all(rows.reshape(TOTAL, 1, width), BOTH, 0, 0, tiled=True)]
    all_to_all x1 -> x0, waiting for transfers between devices: 8.65 us -> none  [to_all(): got = lax.all_to_all(rows.reshape(TOTAL, 1, width), BOTH, 0, 0, tiled=True)]
    unnamed x15 -> x18, local copies, waits for them, and re-layouts: 4.09 us -> 6.52 us
    reshape x2 -> x0, local copies, waits for them, and re-layouts: 1.13 us -> none  [the longest x1 1.04 us: to_all(): got = lax.all_to_all(rows.reshape(TOTAL, 1, width), BOTH, 0, 0, tiled=True)]
    ppermute x2, starting transfers between devices: 2.7 us -> 3.66 us  [body(): y_low, y_high = (down(to_high), up(to_low))]
  transfers between devices with their start and end apart: 5 -> 4, of which waited for: 1 -> 0; matrix products, arithmetic and copies ran while one was open for 3% -> 0% of each run, Pallas kernels for 2% -> 0%
where the time goes in v2:
time: 75 us; the launch traced here: 74.6 us
  blocking collectives  33.5 us (45%)
  Pallas kernels  26.5 us (35%)
  starting transfers between devices  7.38 us (10%)
  local copies, waits for them, and re-layouts  6.52 us (9%)
    all_to_all x2, blocking collectives, to_all(): got = lax.all_to_all(rows.reshape(TOTAL, -1, COLS), BOTH, 0, 0, tiled=True)  33.5 us
    pallas_call x5, Pallas kernels, run(): pl.pallas_call(kernel, out_shape=outs, in_specs=in_specs, out_specs=jax.t...  26.5 us
    unnamed x18, local copies, waits for them, and re-layouts  6.52 us
    ppermute x2, starting transfers between devices, body(): x_low, x_high = (right(to_high), left(to_low))  3.71 us
    ppermute x2, starting transfers between devices, body(): y_low, y_high = (down(to_high), up(to_low))  3.66 us
  transfers between devices with their start and end apart: 4, of which 0 were waited for; matrix products, arithmetic and copies ran while one was open for 0% of the time, Pallas kernels for 0%

profile of v2, /device:TPU:1, one launch (start us, length us, event | category | flops | bytes accessed | tf_op | source)
XLA Modules:
  0.0 74.6 jit_solution(14375745997520753658)
XLA Ops:
  0.6 0.0 copy-start
  0.6 1.0 %copy-done = f32[5,4,32,128]{3,2,1,0:T(8,128)S(1)} copy-done((f32[5,4,32,128]{3,2,1,0:T(8,128)S(1)}, f32[5,4,32,128]{3,2,1,0:T(8,128)}, u32[]{:S(2)}) %copy-start) | copy-done | bytes 327704
  1.6 0.0 copy-start.1
  1.6 0.8 %copy-done.1 = s32[4,32,128]{2,1,0:T(8,128)S(1)} copy-done((s32[4,32,128]{2,1,0:T(8,128)S(1)}, s32[4,32,128]{2,1,0:T(8,128)}, u32[]{:S(2)}) %copy-start.1) | copy-done | bytes 65560
  2.4 0.0 copy-start.2
  2.4 0.8 %copy-done.2 = f32[4,32,128]{2,1,0:T(8,128)S(1)} copy-done((f32[4,32,128]{2,1,0:T(8,128)S(1)}, f32[4,32,128]{2,1,0:T(8,128)}, u32[]{:S(2)}) %copy-start.2) | copy-done | bytes 65560
  3.3 0.0 copy-start.4
  3.3 0.8 %copy-done.4 = f32[4,32,128]{2,1,0:T(8,128)S(1)} copy-done((f32[4,32,128]{2,1,0:T(8,128)S(1)}, f32[4,32,128]{2,1,0:T(8,128)}, u32[]{:S(2)}) %copy-start.4) | copy-done | bytes 65560
  4.1 0.0 copy-start.7
  4.1 0.3 shard_map.95
  4.4 2.2 %collective-permute-start = (f32[4,32,128]{2,1,0:T(8,128)S(1)}, f32[4,32,128]{2,1,0:T(8,128)S(1)}, u32[]{:S(2)}, u32[]{:S(2)}) collective-permute-start(f32[4,32,128]{2,1,0:T(8,128)S(1)} %get-tuple-element.23), channel_id=1, source_target_pairs={{0,32},{32,64},{64,96},{96,0},{1,33},{33,65},{65,97},{97,1},{2,34}... | collective-permute-start | bytes 196616 | tf_op jit(solution)/shard_map/ppermute | solution.py:634
  6.6 1.5 %collective-permute-start.1 = (f32[4,32,128]{2,1,0:T(8,128)S(1)}, f32[4,32,128]{2,1,0:T(8,128)S(1)}, u32[]{:S(2)}, u32[]{:S(2)}) collective-permute-start(f32[4,32,128]{2,1,0:T(8,128)S(1)} %get-tuple-element.24), channel_id=1, source_target_pairs={{32,0},{64,32},{96,64},{0,96},{33,1},{65,33},{97,65},{1,97},{34,2}... | collective-permute-start | bytes 196616 | tf_op jit(solution)/shard_map/ppermute | solution.py:634
  8.2 0.0 copy-start.6
  8.2 0.7 copy-done.6
  8.9 0.0 copy-start.8
  8.9 0.7 copy-done.8
  9.5 0.2 shard_map.94
  9.8 0.0 collective-permute-done.from_low.x_low
  9.8 0.0 collective-permute-done.1.from_high.x_high
  9.8 0.0 copy-start.3
  9.8 0.8 %copy-done.3 = f32[4,32,128]{2,1,0:T(8,128)S(1)} copy-done((f32[4,32,128]{2,1,0:T(8,128)S(1)}, f32[4,32,128]{2,1,0:T(8,128)}, u32[]{:S(2)}) %copy-start.3) | copy-done | bytes 65560
  10.6 0.0 copy-start.5
  10.6 0.8 %copy-done.5 = f32[4,32,128]{2,1,0:T(8,128)S(1)} copy-done((f32[4,32,128]{2,1,0:T(8,128)S(1)}, f32[4,32,128]{2,1,0:T(8,128)}, u32[]{:S(2)}) %copy-start.5) | copy-done | bytes 65560
  11.5 3.7 %collective-permute-start.2 = (f32[40,16,128]{2,1,0:T(8,128)S(1)}, f32[40,16,128]{2,1,0:T(8,128)S(1)}, u32[]{:S(2)}, u32[]{:S(2)}) collective-permute-start(f32[40,16,128]{2,1,0:T(8,128)S(1)} %get-tuple-element.28), channel_id=1, source_target_pairs={{0,1},{1,2},{2,3},{3,4},{4,5},{5,6},{6,7},{7,8},{8,9},{9,10},{10,1... | collective-permute-start | bytes 983048 | tf_op jit(solution)/shard_map/ppermute | solution.py:647
  15.2 0.0 collective-permute-start.3
  15.2 19.1 %all_to_all.10 = f32[128,1,128]{2,1,0:T(1,128)S(1)} all-to-all(f32[128,1,128]{2,1,0:T(1,128)S(1)} %bitcast.20), channel_id=1, replica_groups=mesh['grp'=4,'gy'=32] {'grp','gy'}, dimensions={0} | all-to-all | bytes 131072 | tf_op jit(solution)/shard_map/all_to_all | solution.py:622
  34.3 0.0 collective-permute-done.2.y_low
  34.3 0.0 collective-permute-done.3.y_high
  34.3 0.0 copy-done.7
  34.3 17.8 %shard_map.97 = (f32[256,128]{1,0:T(8,128)S(1)}, f32[4,80,256]{2,1,0:T(8,128)S(1)}, f32[4,80,256]{2,1,0:T(8,128)S(1)}, f32[20,80,256]{2,1,0:T(8,128)S(1)}, f32[2...) custom-call(f32[4,5]{1,0:T(4,128)S(1)} %bitcast.23, ...), custom_call_target="tpu_custom_call" | custom-call | tf_op jit(solution)/shard_map/pallas_call | solution.py:605
  52.1 14.4 %all_to_all.11 = f32[128,2,128]{2,1,0:T(2,128)S(1)} all-to-all(f32[128,2,128]{2,1,0:T(2,128)S(1)} %bitcast.21), channel_id=1, replica_groups=mesh['grp'=4,'gy'=32] {'grp','gy'}, dimensions={0} | all-to-all | bytes 262144 | tf_op jit(solution)/shard_map/all_to_all | solution.py:622
  66.5 8.1 %shard_map.98 = (f32[20,32,128]{2,1,0:T(8,128)}, f32[20,32,128]{2,1,0:T(8,128)}, f32[20,32,128]{2,1,0:T(8,128)}) custom-call(f32[20,32,128]{2,1,0:T(8,128)S(1)} %bitcast.16, f32[128,128]{1,0:T(8,128)S(1)} %bitcast.18, f32[256,128]{1,0:T(8,128)S(1)} %bitcast.19, f32[4,80,256]{2,1,0:T(8,128)S(1)} %get-tuple-element.31.cap, ...), custom_call_target="tpu_custom_call" | custom-call | tf_op jit(solution)/shard_map/pallas_call | solution.py:605
  (1 shorter events, 0.0 us)
Async XLA Ops:
  0.6 1.0 %copy-start = (f32[5,4,32,128]{3,2,1,0:T(8,128)S(1)}, f32[5,4,32,128]{3,2,1,0:T(8,128)}, u32[]{:S(2)}) copy-start(f32[5,4,32,128]{3,2,1,0:T(8,128)} %param.7) | copy-start | bytes 983044
  1.6 0.8 %copy-start.1 = (s32[4,32,128]{2,1,0:T(8,128)S(1)}, s32[4,32,128]{2,1,0:T(8,128)}, u32[]{:S(2)}) copy-start(s32[4,32,128]{2,1,0:T(8,128)} %mat.7) | copy-start | bytes 196612
  2.4 0.8 %copy-start.2 = (f32[4,32,128]{2,1,0:T(8,128)S(1)}, f32[4,32,128]{2,1,0:T(8,128)}, u32[]{:S(2)}) copy-start(f32[4,32,128]{2,1,0:T(8,128)} %pot.5) | copy-start | bytes 196612
  3.3 0.8 %copy-start.4 = (f32[4,32,128]{2,1,0:T(8,128)S(1)}, f32[4,32,128]{2,1,0:T(8,128)}, u32[]{:S(2)}) copy-start(f32[4,32,128]{2,1,0:T(8,128)} %cap.5) | copy-start | bytes 196612
  4.1 30.2 %copy-start.7 = (f32[5,4]{0,1:T(4,128)S(1)}, f32[5,4]{0,1:T(4,128)}, u32[]{:S(2)}) copy-start(f32[5,4]{0,1:T(4,128)} %param.10) | copy-start | bytes 244
  4.4 5.3 %collective-permute-start = (f32[4,32,128]{2,1,0:T(8,128)S(1)}, f32[4,32,128]{2,1,0:T(8,128)S(1)}, u32[]{:S(2)}, u32[]{:S(2)}) collective-permute-start(f32[4,32,128]{2,1,0:T(8,128)S(1)} %get-tuple-element.23), channel_id=1, source_target_pairs={{0,32},{32,64},{64,96},{96,0},{1,33},{33,65},{65,97},{97,1},{2,34}... | collective-permute-start | bytes 196616 | tf_op jit(solution)/shard_map/ppermute | solution.py:634
  6.6 3.1 %collective-permute-start.1 = (f32[4,32,128]{2,1,0:T(8,128)S(1)}, f32[4,32,128]{2,1,0:T(8,128)S(1)}, u32[]{:S(2)}, u32[]{:S(2)}) collective-permute-start(f32[4,32,128]{2,1,0:T(8,128)S(1)} %get-tuple-element.24), channel_id=1, source_target_pairs={{32,0},{64,32},{96,64},{0,96},{33,1},{65,33},{97,65},{1,97},{34,2}... | collective-permute-start | bytes 196616 | tf_op jit(solution)/shard_map/ppermute | solution.py:634
  8.2 0.7 copy-start.6
  8.9 0.7 copy-start.8
  9.8 0.8 %copy-start.3 = (f32[4,32,128]{2,1,0:T(8,128)S(1)}, f32[4,32,128]{2,1,0:T(8,128)}, u32[]{:S(2)}) copy-start(f32[4,32,128]{2,1,0:T(8,128)} %pot.5) | copy-start | bytes 196612
  10.6 0.8 %copy-start.5 = (f32[4,32,128]{2,1,0:T(8,128)S(1)}, f32[4,32,128]{2,1,0:T(8,128)}, u32[]{:S(2)}) copy-start(f32[4,32,128]{2,1,0:T(8,128)} %cap.5) | copy-start | bytes 196612
  11.5 22.8 %collective-permute-start.2 = (f32[40,16,128]{2,1,0:T(8,128)S(1)}, f32[40,16,128]{2,1,0:T(8,128)S(1)}, u32[]{:S(2)}, u32[]{:S(2)}) collective-permute-start(f32[40,16,128]{2,1,0:T(8,128)S(1)} %get-tuple-element.28), channel_id=1, source_target_pairs={{0,1},{1,2},{2,3},{3,4},{4,5},{5,6},{6,7},{7,8},{8,9},{9,10},{10,1... | collective-permute-start | bytes 983048 | tf_op jit(solution)/shard_map/ppermute | solution.py:647
  15.2 19.1 %collective-permute-start.3 = (f32[40,16,128]{2,1,0:T(8,128)S(1)}, f32[40,16,128]{2,1,0:T(8,128)S(1)}, u32[]{:S(2)}, u32[]{:S(2)}) collective-permute-start(f32[40,16,128]{2,1,0:T(8,128)S(1)} %get-tuple-element.29), channel_id=1, source_target_pairs={{1,0},{2,1},{3,2},{4,3},{5,4},{6,5},{7,6},{8,7},{9,8},{10,9},{11,1... | collective-permute-start | bytes 983048 | tf_op jit(solution)/shard_map/ppermute | solution.py:647

commit v3 on v2

--- a/solution.py
+++ b/solution.py
@@ -12,6 +12,7 @@
 MATS = 4
 FIELDS = SPECIES * LAYERS
 PLANES = FIELDS + 3 * LAYERS
+POT0, CAP0, MAT0 = FIELDS, FIELDS + LAYERS, FIELDS + 2 * LAYERS
 ROWS = 32
 COLS = 128
 N_GRP = 4
@@ -45,13 +46,13 @@
     return lax.broadcasted_iota(jnp.int32, shape, 0)
 
 
-def pack_kernel(b, pot, cap, mat, to_low, to_high):
+def pack_kernel(planes, to_low, to_high):
     lane = lanes((ROWS, COLS))
     for g in range(GROUPS):
         low = jnp.zeros((ROWS, COLS), F32)
         high = jnp.zeros((ROWS, COLS), F32)
         for j in range(min(PER, PLANES - g * PER)):
-            v = plane_of(b, pot, cap, mat, g * PER + j)
+            v = planes[g * PER + j]
             inside = (lane >= HALO * j) & (lane < HALO * (j + 1))
             low = jnp.where(inside, turn(v, HALO * j), low)
             high = jnp.where(inside, turn(v, HALO * j + HALO), high)
@@ -64,13 +65,6 @@
     return v if shift == 0 else pltpu.roll(v, shift, 1)
 
 
-def plane_of(b, pot, cap, mat, k):
-    if k < FIELDS:
-        return b[k]
-    which, layer = divmod(k - FIELDS, LAYERS)
-    return (pot, cap, mat)[which][layer].astype(F32)
-
-
 def place(rows):
     n = rows.shape[0]
     total = jnp.sum(rows, axis=1, keepdims=True)
@@ -82,7 +76,7 @@
     return jnp.sum(v, axis=0, keepdims=True)
 
 
-def sums_kernel(b, mat, cmap, inverse, out, acc, ids):
+def sums_kernel(planes, cmap, inverse, out, acc, ids):
     acc[...] = jnp.zeros(acc.shape, F32)
     row = jnp.zeros((1, COLS), F32)
     for s in range(SPECIES):
@@ -98,17 +92,16 @@
         for m in range(MATS):
             total = jnp.zeros((ROWS, COLS), F32)
             for l in range(LAYERS):
-                total = total + jnp.where(mat[l] == m, b[s * LAYERS + l], 0.0)
+                total = total + jnp.where(planes[MAT0 + l] == m, planes[s * LAYERS + l], 0.0)
             acc[m * SPECIES + s : m * SPECIES + s + 1, :] = fold(total)
     row = row + place(acc[...])
     out[...] = jnp.broadcast_to(row, (TOTAL, COLS))
 
 
-def rows_kernel(b, pot, cap, mat, from_low, from_high, to_low, to_high):
+def rows_kernel(planes, from_low, from_high, to_low, to_high):
     for k in range(PLANES):
-        v = plane_of(b, pot, cap, mat, k)
-        to_low[k] = v[:RHALO]
-        to_high[k] = v[ROWS - RHALO :]
+        to_low[k] = planes[k, :RHALO]
+        to_high[k] = planes[k, ROWS - RHALO :]
     for g in range(GROUPS):
         for i, part in enumerate((from_low, from_high)):
             k = PLANES + i * GROUPS + g
@@ -124,32 +117,47 @@
     return jnp.where(lane < HALO, right, jnp.where(lane >= COLS - HALO, left, fill))
 
 
-def a_tile(src, cap, gy, gx, gz, s, row):
+def after(v, nxt, axis):
+    first = lax.broadcasted_iota(jnp.int32, v.shape, axis) == 0
+    return pltpu.roll(jnp.where(first, nxt, v), v.shape[axis] - 1, axis)
+
+
+def before(v, prev, axis):
+    last = lax.broadcasted_iota(jnp.int32, v.shape, axis) == v.shape[axis] - 1
+    return pltpu.roll(jnp.where(last, prev, v), 1, axis)
+
+
+def stencil(src, ops, s, tiles, exact, emit):
+    cap, gy, gx, gz = ops[:4]
     base = s * LAYERS
-    here = pl.ds(row, 8)
-    below = pl.ds(row - 1, 8)
-    above = pl.ds(row + 1, 8)
-    us, outs = [], []
-    flux_z = None
-    for l in range(LAYERS):
-        k = base + l
-        u = src[k, here, :]
-        if l == 0:
-            nxt = u
-        u = nxt
-        flux_x = gx[k, here, :] * (u - pltpu.roll(u, WIDE - 1, 1))
-        out = cap[l, here, :] * u + (flux_x - pltpu.roll(flux_x, 1, 1))
-        out = out + gy[k, here, :] * (u - src[k, above, :])
-        out = out + gy[k, below, :] * (u - src[k, below, :])
-        if flux_z is not None:
-            out = out - flux_z
-        if l + 1 < LAYERS:
-            nxt = src[k + 1, here, :]
-            flux_z = gz[k, here, :] * (u - nxt)
-            out = out + flux_z
-        us.append(u)
-        outs.append(out)
-    return us, outs
+
+    def load(ref, l, row):
+        return ref[base + l, pl.ds(row, 8), :]
+
+    now = [load(src, l, tiles[0]) for l in range(LAYERS)]
+    flux = [None] * LAYERS
+    if exact:
+        for l in range(LAYERS):
+            u = load(src, l, tiles[0] - 8)
+            flux[l] = load(gy, l, tiles[0] - 8) * (u - after(u, now[l], 0))
+    for row in tiles:
+        outer = row == tiles[-1] and not exact
+        nxt = now if outer else [load(src, l, row + 8) for l in range(LAYERS)]
+        flux_z = None
+        for l in range(LAYERS):
+            u = now[l]
+            flux_x = load(gx, l, row) * (u - pltpu.roll(u, WIDE - 1, 1))
+            out = cap[l, pl.ds(row, 8), :] * u + (flux_x - pltpu.roll(flux_x, 1, 1))
+            flux_y = load(gy, l, row) * (u - after(u, nxt[l], 0))
+            out = out + (flux_y - before(flux_y, flux_y if flux[l] is None else flux[l], 0))
+            flux[l] = flux_y
+            if flux_z is not None:
+                out = out - flux_z
+            if l + 1 < LAYERS:
+                flux_z = load(gz, l, row) * (u - now[l + 1])
+                out = out + flux_z
+            emit(row, l, u, out)
+        now = nxt
 
 
 def tile_rows(first, last):
@@ -157,27 +165,24 @@
 
 
 def sweep(src, resid, dst, ops, tiles):
-    cap, gy, gx, gz, scale = ops
-
-    @pl.loop(0, SPECIES)
-    def _(s):
-        for row in tiles:
-            us, outs = a_tile(src, cap, gy, gx, gz, s, row)
-            for l in range(LAYERS):
-                k = s * LAYERS + l
-                here = pl.ds(row, 8)
-                dst[k, here, :] = us[l] + scale[k, here, :] * (resid[k, here, :] - outs[l])
+    scale = ops[4]
+
+    @pl.loop(0, SPECIES)
+    def _(s):
+        def emit(row, l, u, out):
+            k, here = s * LAYERS + l, pl.ds(row, 8)
+            dst[k, here, :] = u + scale[k, here, :] * (resid[k, here, :] - out)
+
+        stencil(src, ops, s, tiles, False, emit)
 
 
 def image(src, dst, ops, tiles):
-    cap, gy, gx, gz, _ = ops
-
-    @pl.loop(0, SPECIES)
-    def _(s):
-        for row in tiles:
-            _, outs = a_tile(src, cap, gy, gx, gz, s, row)
-            for l in range(LAYERS):
-                dst[s * LAYERS + l, pl.ds(row, 8), :] = outs[l]
+    @pl.loop(0, SPECIES)
+    def _(s):
+        def emit(row, l, u, out):
+            dst[s * LAYERS + l, pl.ds(row, 8), :] = out
+
+        stencil(src, ops, s, tiles, False, emit)
 
 
 def start_sweep(resid, dst, scale, tiles):
@@ -286,8 +291,10 @@
 
 def coarse_at(values, mat_tile, s, row):
     iy = region_of(row)
+    n = mat_tile.shape[1]
     v = [
-        jnp.broadcast_to(values[iy * MATS + m, pl.ds(s, 1), :], mat_tile.shape) for m in range(MATS)
+        jnp.broadcast_to(values[iy * MATS + m, pl.ds(s, 1), :][:, :n], mat_tile.shape)
+        for m in range(MATS)
     ]
     out = jnp.where(mat_tile == 1.0, v[1], v[0])
     out = jnp.where(mat_tile == 2.0, v[2], out)
@@ -312,18 +319,18 @@
     return 2.0 * a * b / (a + b)
 
 
-def first_kernel(
-    diff, b, pot, cap, mat, x_low, x_high, y_low, y_high, got,
-    second, cap_w, mat_w, gy, gx, gz, scale, z0_out, w0_out, u_out,
-    b_w, w, za, zb, w0, scatter, near_hot, turned, values, acc,
+def table_kernel(
+    diff, planes, x_low, x_high, y_low, y_high,
+    cap_w, mat_w, gy, gx, gz, scale, y0, acc,
+    b_w, w, za, code_y, code_x, code_z, code_cx,
 ):
     halves = (x_low, x_high, y_low, y_high)
     for k in range(FIELDS):
-        fill_plane(b_w, k, k, b[k], *halves, 0.0)
+        fill_plane(b_w, k, k, planes[k], *halves, 0.0)
     for l in range(LAYERS):
-        fill_plane(za, l, FIELDS + l, pot[l], *halves, 0.0)
-        fill_plane(cap_w, l, FIELDS + LAYERS + l, cap[l], *halves, 1.0)
-        fill_plane(mat_w, l, FIELDS + 2 * LAYERS + l, mat[l].astype(F32), *halves, 0.0)
+        fill_plane(za, l, POT0 + l, planes[POT0 + l], *halves, 0.0)
+        fill_plane(cap_w, l, CAP0 + l, planes[CAP0 + l], *halves, 1.0)
+        fill_plane(mat_w, l, MAT0 + l, planes[MAT0 + l], *halves, 0.0)
 
     for row in tile_rows(0, 7):
         for l in range(LAYERS):
@@ -342,32 +349,115 @@
     me_x = lax.axis_index("grp")
     lane = lanes((8, WIDE))
     closed = ((lane == COLS - 1) & (me_x == N_GRP - 1)) | ((lane == WIDE - 1) & (me_x == 0))
-
-    @pl.loop(0, SPECIES)
-    def _(s):
-        for row in tile_rows(0, 7):
-            here, above = pl.ds(row, 8), pl.ds(row + 1, 8)
+    all_tiles, mid, own = tile_rows(0, 7), tile_rows(1, 6), tile_rows(2, 5)
+
+    @pl.loop(0, SPECIES)
+    def _(s):
+        def load(l, row):
+            return w[s * LAYERS + l, pl.ds(row, 8), :]
+
+        now = [load(l, all_tiles[0]) for l in range(LAYERS)]
+        edge_y = [None] * LAYERS
+        for row in all_tiles:
+            here = pl.ds(row, 8)
+            nxt = now if row == all_tiles[-1] else [load(l, row + 8) for l in range(LAYERS)]
+            ez_below = None
             for l in range(LAYERS):
                 k = s * LAYERS + l
-                c = w[k, here, :]
-                gy[k, here, :] = harmonic(c, w[k, above, :])
-                gx[k, here, :] = jnp.where(closed, 0.0, harmonic(c, pltpu.roll(c, WIDE - 1, 1)))
+                c = now[l]
+                ey = harmonic(c, after(c, nxt[l], 0))
+                ex = jnp.where(closed, 0.0, harmonic(c, pltpu.roll(c, WIDE - 1, 1)))
+                gy[k, here, :] = ey
+                gx[k, here, :] = ex
+                d = cap_w[l, here, :] + ey + before(ey, ey if edge_y[l] is None else edge_y[l], 0)
+                d = d + ex + pltpu.roll(ex, 1, 1)
+                edge_y[l] = ey
+                if ez_below is not None:
+                    d = d + ez_below
                 if l + 1 < LAYERS:
-                    gz[k, here, :] = 0.5 * harmonic(c, w[k + 1, here, :])
-        for row in tile_rows(0, 7):
-            here, below = pl.ds(row, 8), pl.ds(row - 1, 8)
+                    ez_below = 0.5 * harmonic(c, now[l + 1])
+                    gz[k, here, :] = ez_below
+                    d = d + ez_below
+                scale[k, here, :] = DAMPING / d
+            now = nxt
+
+    ops = (cap_w, gy, gx, gz, scale)
+    start_sweep(b_w, za, scale, all_tiles)
+    sweep(za, b_w, y0, ops, all_tiles)
+    sweep(y0, b_w, za, ops, all_tiles)
+    sweep(za, b_w, y0, ops, mid)
+
+    acc[...] = jnp.zeros(acc.shape, F32)
+    own_lane = lanes((8, COLS))
+    sub = subs((8, COLS))
+
+    def power(m):
+        p = jnp.where(m == 1.0, 2.0, 1.0)
+        p = jnp.where(m == 2.0, 4.0, p)
+        return jnp.where(m == 3.0, 8.0, p)
+
+    for row in own:
+        rows = pl.ds(row - TOP, 8)
+        side = jnp.full((8, COLS), -1.0, F32)
+        for l in range(LAYERS):
+            m_wide = mat_w[l, pl.ds(row, 8), :]
+            m = m_wide[:, :COLS]
+            m_y = after(m, mat_w[l, pl.ds(row + 8, 8), 0:COLS], 0)
+            m_x = pltpu.roll(m_wide, WIDE - 1, 1)[:, :COLS]
+            p = power(m)
+            code = p + power(m_y)
+            if row == own[-1]:
+                code = jnp.where(sub == 7, -1.0 - (m * 4.0 + m_y), code)
+            code_y[l, rows, :] = code
+            code_x[l, rows, :] = jnp.where(own_lane == COLS - 1, 0.0, p + power(m_x))
+            if l + 1 < LAYERS:
+                code_z[l, rows, :] = p + power(mat_w[l + 1, pl.ds(row, 8), 0:COLS])
+            side = jnp.where(own_lane == COLS - 1 - l, turn(m * 4.0 + m_x, -l), side)
+        code_cx[rows, :] = side
+
+    @pl.loop(0, SPECIES)
+    def _(s):
+        zero = jnp.zeros((8, COLS), F32)
+        pairs, cy, cx = [zero] * 6, [zero] * 16, [zero] * 16
+        codes = (3.0, 5.0, 9.0, 6.0, 10.0, 12.0)
+        for row in own:
+            here, rows = pl.ds(row, 8), pl.ds(row - TOP, 8)
+            side = zero
             for l in range(LAYERS):
                 k = s * LAYERS + l
-                ex = gx[k, here, :]
-                d = cap_w[l, here, :] + gy[k, here, :] + gy[k, below, :] + ex + pltpu.roll(ex, 1, 1)
+                ex = gx[k, here, 0:COLS]
+                ey = gy[k, here, 0:COLS]
+                kinds = [(code_y[l, rows, :], ey), (code_x[l, rows, :], ex)]
                 if l + 1 < LAYERS:
-                    d = d + gz[k, here, :]
-                if l > 0:
-                    d = d + gz[k - 1, here, :]
-                scale[k, here, :] = DAMPING / d
-
+                    kinds.append((code_z[l, rows, :], gz[k, here, 0:COLS]))
+                for code, edge in kinds:
+                    for i in range(6):
+                        pairs[i] = pairs[i] + jnp.where(code == codes[i], edge, 0.0)
+                if row == own[-1]:
+                    for i in range(16):
+                        cy[i] = cy[i] + jnp.where(kinds[0][0] == -1.0 - i, ey, 0.0)
+                side = jnp.where(own_lane == COLS - 1 - l, turn(ex, -l), side)
+            code = code_cx[rows, :]
+            for i in range(16):
+                cx[i] = cx[i] + jnp.where(code == float(i), side, 0.0)
+        for group, sums in ((G_S, pairs), (G_CY, cy), (G_CX, cx)):
+            for i, v in enumerate(sums):
+                acc[pl.ds((group + i) * SPECIES + s, 1), :] = fold(v)
+
+    for i in range(MATS):
+        total = jnp.zeros((ROWS, COLS), F32)
+        for l in range(LAYERS):
+            total = total + jnp.where(planes[MAT0 + l] == i, planes[CAP0 + l], 0.0)
+        acc[ROW_CAP + i : ROW_CAP + i + 1, :] = fold(total)
+
+
+def first_kernel(
+    planes, got, cap_w, mat_w, gy, gx, gz, scale, y0, acc_in,
+    second, z0_out, w0_out, u_out,
+    za, zb, w0, scatter, near_hot, turned, values, acc,
+):
     ops = (cap_w, gy, gx, gz, scale)
-    all_tiles, mid, own = tile_rows(0, 7), tile_rows(1, 6), tile_rows(2, 5)
+    mid, own = tile_rows(1, 6), tile_rows(2, 5)
 
     turned[...] = got[...].T
     build_scatter(got, scatter)
@@ -375,21 +465,13 @@
     sol = coarse_solve(local_sums(turned, 0), turned, scatter)
     spread_values(exact_dot(sol, near_hot[...]), values)
 
-    start_sweep(b_w, za, scale, all_tiles)
-    sweep(za, b_w, zb, ops, all_tiles)
-    sweep(zb, b_w, za, ops, all_tiles)
-
-    cap_o, gy_o, gx_o, gz_o, scale_o = ops
-
     @pl.loop(0, SPECIES)
     def _(s):
         for row in mid:
             here = pl.ds(row, 8)
-            us, outs = a_tile(za, cap_o, gy_o, gx_o, gz_o, s, row)
             for l in range(LAYERS):
                 k = s * LAYERS + l
-                smooth = us[l] + scale[k, here, :] * (b_w[k, here, :] - outs[l])
-                zb[k, here, :] = smooth + coarse_at(values, mat_w[l, here, :], s, row)
+                zb[k, here, :] = y0[k, here, :] + coarse_at(values, mat_w[l, here, :], s, row)
 
     for k in range(FIELDS):
         z0_out[k] = zb[k, TOP : TOP + ROWS, 0:COLS]
@@ -401,82 +483,32 @@
     sweep(zb, w0, za, ops, mid)
     sweep(za, w0, u_out, ops, mid)
 
-    acc[...] = jnp.zeros(acc.shape, F32)
-    own_lane = lanes((8, COLS))
-    sub = subs((8, COLS))
-
-    @pl.loop(0, SPECIES)
-    def _(s):
-        def keep(group, v):
-            acc[pl.ds(group * SPECIES + s, 1), :] = fold(v)
-
+    acc[...] = acc_in[...]
+
+    @pl.loop(0, SPECIES)
+    def _(s):
         zero = jnp.zeros((8, COLS), F32)
         rw, rau, mom = [zero] * MATS, [zero] * MATS, [zero] * 4
-        pairs, cy, cx = [zero] * 6, [zero] * 16, [zero] * 16
-        codes = (3.0, 5.0, 9.0, 6.0, 10.0, 12.0)
-
-        def power(m):
-            p = jnp.where(m == 1.0, 2.0, 1.0)
-            p = jnp.where(m == 2.0, 4.0, p)
-            return jnp.where(m == 3.0, 8.0, p)
-
-        for row in own:
-            here = pl.ds(row, 8)
-            above = pl.ds(row + 1, 8)
-            us, outs = a_tile(u_out, cap_o, gy_o, gx_o, gz_o, s, row)
-            side_g, side_c = zero, zero - 1.0
-            for l in range(LAYERS):
-                k = s * LAYERS + l
-                m_wide = mat_w[l, here, :]
-                m = m_wide[:, :COLS]
-                u, au = us[l][:, :COLS], outs[l][:, :COLS]
-                wv, zv, bv = w0_out[k, row - TOP : row - TOP + 8, :], z0_out[k, row - TOP : row - TOP + 8, :], b[k, row - TOP : row - TOP + 8, :]
-                mom[0] = mom[0] + bv * zv
-                mom[1] = mom[1] + zv * wv
-                mom[2] = mom[2] + wv * u
-                mom[3] = mom[3] + u * au
-                for i in range(MATS):
-                    is_i = m == float(i)
-                    rw[i] = rw[i] + jnp.where(is_i, wv, 0.0)
-                    rau[i] = rau[i] + jnp.where(is_i, au, 0.0)
-                m_y = mat_w[l, above, 0:COLS]
-                m_x = pltpu.roll(m_wide, WIDE - 1, 1)[:, :COLS]
-                ey, ex = gy[k, here, 0:COLS], gx[k, here, 0:COLS]
-                p = power(m)
-                last = row == own[-1]
-                code = p + power(m_y)
-                if last:
-                    code = jnp.where(sub == 7, 0.0, code)
-                kinds = [(code, ey), (jnp.where(own_lane == COLS - 1, 0.0, p + power(m_x)), ex)]
-                if l + 1 < LAYERS:
-                    kinds.append((p + power(mat_w[l + 1, here, 0:COLS]), gz[k, here, 0:COLS]))
-                for code, edge in kinds:
-                    for i in range(6):
-                        pairs[i] = pairs[i] + jnp.where(code == codes[i], edge, 0.0)
-                if last:
-                    code = jnp.where(sub == 7, m * 4.0 + m_y, -1.0)
-                    for i in range(16):
-                        cy[i] = cy[i] + jnp.where(code == float(i), ey, 0.0)
-                at_end = own_lane == COLS - 1 - l
-                side_g = jnp.where(at_end, turn(ex, -l), side_g)
-                side_c = jnp.where(at_end, turn(m * 4.0 + m_x, -l), side_c)
-            for i in range(16):
-                cx[i] = cx[i] + jnp.where(side_c == float(i), side_g, 0.0)
-        for i in range(MATS):
-            keep(G_RW + i, rw[i])
-            keep(G_RAU + i, rau[i])
-            keep(G_MOM + i, mom[i])
-        for i in range(6):
-            keep(G_S + i, pairs[i])
-        for i in range(16):
-            keep(G_CY + i, cy[i])
-            keep(G_CX + i, cx[i])
-
-    for i in range(MATS):
-        total = jnp.zeros((ROWS, COLS), F32)
-        for l in range(LAYERS):
-            total = total + jnp.where(mat[l] == i, cap[l], 0.0)
-        acc[ROW_CAP + i : ROW_CAP + i + 1, :] = fold(total)
+
+        def emit(row, l, u, au):
+            k, rows = s * LAYERS + l, pl.ds(row - TOP, 8)
+            m = mat_w[l, pl.ds(row, 8), 0:COLS]
+            u, au = u[:, :COLS], au[:, :COLS]
+            wv, zv, bv = w0_out[k, rows, :], z0_out[k, rows, :], planes[k, rows, :]
+            mom[0] = mom[0] + bv * zv
+            mom[1] = mom[1] + zv * wv
+            mom[2] = mom[2] + wv * u
+            mom[3] = mom[3] + u * au
+            for i in range(MATS):
+                is_i = m == float(i)
+                rw[i] = rw[i] + jnp.where(is_i, wv, 0.0)
+                rau[i] = rau[i] + jnp.where(is_i, au, 0.0)
+
+        stencil(u_out, ops, s, own, True, emit)
+        for group, sums in ((G_RW, rw), (G_RAU, rau), (G_MOM, mom)):
+            for i, v in enumerate(sums):
+                acc[pl.ds((group + i) * SPECIES + s, 1), :] = fold(v)
+
     even = lax.rem(subs((WIDE, COLS)), 2) == 0
     second[...] = jnp.where(even, place(acc[0:COLS, :]), place(acc[COLS:WIDE, :]))
 
@@ -496,7 +528,7 @@
 
 
 def second_kernel(
-    b, got, got2, cap, mat, gy, gx, gz, scale, z0, w0, u,
+    planes, got, got2, cap, mat, gy, gx, gz, scale, z0, w0, u,
     out_x, out_r, out_z,
     v1, w1, za, zb, scatter, gather, near_hot, turned, turned2, values, values2,
 ):
@@ -575,21 +607,18 @@
 
     @pl.loop(0, SPECIES)
     def _(s):
-        for row in own:
-            here = pl.ds(row, 8)
-            us, outs = a_tile(za, cap, gy, gx, gz, s, row)
-            for l in range(LAYERS):
-                k = s * LAYERS + l
-                w1v = w1[k, here, :]
-                v2 = us[l] + scale[k, here, :] * (w1v - outs[l])
-                v2 = (v2 + coarse_at(values2, mat[l, here, :], s, row))[:, :COLS]
-                w1v = w1v[:, :COLS]
-                v1v = v1[k, here, 0:COLS]
-                rows = pl.ds(row - TOP, 8)
-                z0v, w0v = z0[k, rows, :], w0[k, rows, :]
-                out_x[k, rows, :] = ca * z0v - cb * v1v
-                out_r[k, rows, :] = b[k, rows, :] - ca * w0v + cb * w1v
-                out_z[k, rows, :] = z0v - ca * v1v + cb * v2
+        def emit(row, l, u_, out):
+            k, here, rows = s * LAYERS + l, pl.ds(row, 8), pl.ds(row - TOP, 8)
+            w1v = w1[k, here, 0:COLS]
+            v2 = u_[:, :COLS] + scale[k, here, 0:COLS] * (w1v - out[:, :COLS])
+            v2 = v2 + coarse_at(values2, mat[l, here, 0:COLS], s, row)
+            v1v = v1[k, here, 0:COLS]
+            z0v, w0v = z0[k, rows, :], w0[k, rows, :]
+            out_x[k, rows, :] = ca * z0v - cb * v1v
+            out_r[k, rows, :] = planes[k, rows, :] - ca * w0v + cb * w1v
+            out_z[k, rows, :] = z0v - ca * v1v + cb * v2
+
+        stencil(za, ops, s, own, True, emit)
 
 
 def shape(*dims):
@@ -598,10 +627,10 @@
 
 VMEM = pl.BlockSpec(memory_space=pltpu.VMEM)
 SMEM = pl.BlockSpec(memory_space=pltpu.SMEM)
-PARAMS = pltpu.CompilerParams(vmem_limit_bytes=26 * 1024 * 1024)
-
-
-def run(kernel, outs, scratch, in_specs, *args):
+PARAMS = pltpu.CompilerParams(vmem_limit_bytes=18 * 1024 * 1024)
+
+
+def run(kernel, outs, scratch, in_specs, cost, *args):
     return pl.pallas_call(
         kernel,
         out_shape=outs,
@@ -609,6 +638,7 @@
         out_specs=jax.tree.map(lambda _: VMEM, outs),
         scratch_shapes=scratch,
         compiler_params=PARAMS,
+        cost_estimate=pl.CostEstimate(flops=cost, bytes_accessed=1 << 20, transcendentals=0),
     )(*args)
 
 
@@ -625,27 +655,29 @@
 
 def body(right_side, potential, capacity, diffusivity, material, coarse_map, coarse_inverse):
     b = right_side.reshape(FIELDS, ROWS, COLS)
-    own = (b, potential, capacity, material)
     right, left = shifts("grp", N_GRP)
     down, up = shifts("gy", N_GY)
 
+    planes = jnp.concatenate([b, potential, capacity, material.astype(F32)])
     packed = shape(GROUPS, ROWS, COLS)
-    to_low, to_high = run(pack_kernel, (packed, packed), [], [VMEM] * 4, *own)
+    to_low, to_high = run(pack_kernel, (packed, packed), [], [VMEM], 1 << 20, planes)
     x_low, x_high = right(to_high), left(to_low)
-
     first = run(
         sums_kernel,
         shape(TOTAL, COLS),
         [pltpu.VMEM((24, COLS), F32), pltpu.VMEM((8, COLS), jnp.int32)],
-        [VMEM] * 4,
-        b, material, coarse_map, jnp.transpose(coarse_inverse, (1, 0, 2)),
+        [VMEM] * 3,
+        1 << 20,
+        planes, coarse_map, jnp.transpose(coarse_inverse, (1, 0, 2)),
     )
 
     strips = shape(PLANES + 2 * GROUPS, RHALO, COLS)
-    to_low, to_high = run(rows_kernel, (strips, strips), [], [VMEM] * 6, *own, x_low, x_high)
+    to_low, to_high = run(
+        rows_kernel, (strips, strips), [], [VMEM] * 3, 1 << 20, planes, x_low, x_high
+    )
     first, to_low, to_high = lax.optimization_barrier((first, to_low, to_high))
     y_low, y_high = down(to_high), up(to_low)
-    got = to_all(first)
+    got, y_low, y_high = lax.optimization_barrier((to_all(first), y_low, y_high))
 
     wide = shape(FIELDS, TALL, WIDE)
     thin = shape(LAYERS, TALL, WIDE)
@@ -653,14 +685,23 @@
     big = pltpu.VMEM((FIELDS, TALL, WIDE), F32)
     hot = pltpu.VMEM((NC, MATS * TOTAL), jnp.bfloat16)
     near = pltpu.VMEM((NC, COLS), jnp.bfloat16)
-    square = pltpu.VMEM((COLS + 8, COLS), F32)
+    code = pltpu.VMEM((LAYERS, ROWS, COLS), F32)
     values = pltpu.VMEM((3 * MATS, 8, WIDE), F32)
-    second, cap_w, mat_w, gy, gx, gz, scale, z0, w0, u = run(
+    cap_w, mat_w, gy, gx, gz, scale, y0, acc = run(
+        table_kernel,
+        (thin, thin, wide, wide, wide, wide, wide, shape(WIDE, COLS)),
+        [big] * 3 + [code] * 3 + [pltpu.VMEM((ROWS, COLS), F32)],
+        [SMEM] + [VMEM] * 5,
+        1 << 30,
+        diffusivity.T, planes, x_low, x_high, y_low, y_high,
+    )
+    second, z0, w0, u = run(
         first_kernel,
-        (shape(2 * TOTAL, COLS), thin, thin, wide, wide, wide, wide, field, field, wide),
-        [big] * 5 + [hot, near, pltpu.VMEM((COLS, COLS), F32), values, pltpu.VMEM((WIDE, COLS), F32)],
-        [SMEM] + [VMEM] * 9,
-        diffusivity.T, *own, x_low, x_high, y_low, y_high, got,
+        (shape(2 * TOTAL, COLS), field, field, wide),
+        [big] * 3 + [hot, near, pltpu.VMEM((COLS, COLS), F32), values, pltpu.VMEM((WIDE, COLS), F32)],
+        [VMEM] * 10,
+        1 << 30,
+        planes, got, cap_w, mat_w, gy, gx, gz, scale, y0, acc,
     )
     got2 = to_all(second)
     out = run(
@@ -669,7 +710,8 @@
         [big] * 4
         + [hot, hot, near, pltpu.VMEM((COLS, COLS), F32), pltpu.VMEM((WIDE, COLS), F32), values, values],
         [VMEM] * 12,
-        b, got, got2, cap_w, mat_w, gy, gx, gz, scale, z0, w0, u,
+        1 << 30,
+        planes, got, got2, cap_w, mat_w, gy, gx, gz, scale, z0, w0, u,
     )
     return tuple(o.reshape(right_side.shape) for o in out)
 

time: 75 us -> 67.9 us (0.905)
  local copies, waits for them, and re-layouts: 6.52 us -> 0.01 us
  Pallas kernels: 26.5 us -> 22.7 us
  other arithmetic: 0 us -> 1.95 us
  waiting for transfers between devices: 0.01 us -> 1.34 us
    unnamed x18 -> x6, local copies, waits for them, and re-layouts: 6.52 us -> 0.01 us
    pallas_call x5 -> x6, Pallas kernels: 26.5 us -> 22.7 us  [run(): pl.pallas_call(kernel, out_shape=outs, in_specs=in_specs, out_specs=jax.t...]
    ppermute x2, waiting for transfers between devices: 0.01 us -> 1.34 us  [body(): x_low, x_high = (right(to_high), left(to_low))]
    concatenate x0 -> x1, other arithmetic: none -> 1.09 us  [body(): planes = jnp.concatenate([b, potential, capacity, material.astype(F32)])]
    convert_element_type x0 -> x1, other arithmetic: none -> 0.86 us  [body(): planes = jnp.concatenate([b, potential, capacity, material.astype(F32)])]
  transfers between devices with their start and end apart: 4 -> 4, of which waited for: 0 -> 1; matrix products, arithmetic and copies ran while one was open for 0% -> 0% of each run, Pallas kernels for 0% -> 0%
where the time goes in v3:
time: 67.9 us; the launch traced here: 67.6 us
  blocking collectives  33.5 us (49%)
  Pallas kernels  22.7 us (33%)
  starting transfers between devices  7.41 us (11%)
  other arithmetic  1.95 us (3%)
  waiting for transfers between devices  1.34 us (2%)
  between operations  0.7 us (1%)
    all_to_all x2, blocking collectives, to_all(): got = lax.all_to_all(rows.reshape(TOTAL, -1, COLS), BOTH, 0, 0, tiled=True)  33.5 us
    pallas_call x6, Pallas kernels, run(): pl.pallas_call(kernel, out_shape=outs, in_specs=in_specs, out_specs=jax.t...  22.7 us
    ppermute x2, starting transfers between devices, body(): x_low, x_high = (right(to_high), left(to_low))  3.71 us
    ppermute x2, starting transfers between devices, body(): y_low, y_high = (down(to_high), up(to_low))  3.7 us
  transfers between devices with their start and end apart: 4, of which 1 were waited for; matrix products, arithmetic and copies ran while one was open for 0% of the time, Pallas kernels for 0%

profile of v3, /device:TPU:1, one launch (start us, length us, event | category | flops | bytes accessed | tf_op | source)
XLA Modules:
  0.0 67.6 jit_solution(14357567234253944004)
XLA Ops:
  0.6 0.0 copy-start
  0.6 0.0 copy-start.1
  0.7 0.0 copy-start.2
  0.7 0.9 %convert_element_type.3 = f32[4,32,128]{2,1,0:T(8,128)S(1)} convert(s32[4,32,128]{2,1,0:T(8,128)} %param.11) | non-fusion elementwise | flops 16384 | bytes 131072 | tf_op jit(solution)/shard_map/convert_element_type | solution.py:661
  1.5 1.1 %pad_maximum_fusion.planes = f32[32,32,128]{2,1,0:T(8,128)S(1)} fusion(f32[4,32,128]{2,1,0:T(8,128)S(1)} %convert_element_type.3, f32[4,32,128]{2,1,0:T(8,128)} %param.9, f32[4,32,128]{2,1,0:T(8,128)} %param.8, f32[20,32,128]{2,1,0:T(8,128)} %bitcast.19), kind=kLoop, calls=%fused_computation | loop fusion | flops 393216 | bytes 1048576 | tf_op jit(solution)/shard_map/concatenate | solution.py:661
  2.6 0.3 shard_map.95
  2.9 2.2 %collective-permute-start = (f32[4,32,128]{2,1,0:T(8,128)S(1)}, f32[4,32,128]{2,1,0:T(8,128)S(1)}, u32[]{:S(2)}, u32[]{:S(2)}) collective-permute-start(f32[4,32,128]{2,1,0:T(8,128)S(1)} %get-tuple-element.28), channel_id=1, source_target_pairs={{0,32},{32,64},{64,96},{96,0},{1,33},{33,65},{65,97},{97,1},{2,34}... | collective-permute-start | bytes 196616 | tf_op jit(solution)/shard_map/ppermute | solution.py:664
  5.1 1.5 %collective-permute-start.1 = (f32[4,32,128]{2,1,0:T(8,128)S(1)}, f32[4,32,128]{2,1,0:T(8,128)S(1)}, u32[]{:S(2)}, u32[]{:S(2)}) collective-permute-start(f32[4,32,128]{2,1,0:T(8,128)S(1)} %get-tuple-element.29), channel_id=1, source_target_pairs={{32,0},{64,32},{96,64},{0,96},{33,1},{65,33},{97,65},{1,97},{34,2}... | collective-permute-start | bytes 196616 | tf_op jit(solution)/shard_map/ppermute | solution.py:664
  6.7 0.0 copy-done
  6.7 0.0 copy-done.1
  6.7 0.2 shard_map.94
  6.9 1.3 %collective-permute-done.from_low.x_low = f32[4,32,128]{2,1,0:T(8,128)S(1)} collective-permute-done((f32[4,32,128]{2,1,0:T(8,128)S(1)}, f32[4,32,128]{2,1,0:T(8,128)S(1)}, u32[]{:S(2)}, u32[]{:S(2)}) %collective-permute-start) | collective-permute-done | bytes 65568 | tf_op jit(solution)/shard_map/ppermute | solution.py:664
  8.2 0.0 collective-permute-done.1.from_high.x_high
  8.3 3.7 %collective-permute-start.2 = (f32[40,16,128]{2,1,0:T(8,128)S(1)}, f32[40,16,128]{2,1,0:T(8,128)S(1)}, u32[]{:S(2)}, u32[]{:S(2)}) collective-permute-start(f32[40,16,128]{2,1,0:T(8,128)S(1)} %get-tuple-element.33), channel_id=1, source_target_pairs={{0,1},{1,2},{2,3},{3,4},{4,5},{5,6},{6,7},{7,8},{8,9},{9,10},{10,1... | collective-permute-start | bytes 983048 | tf_op jit(solution)/shard_map/ppermute | solution.py:679
  12.0 0.0 collective-permute-start.3
  12.0 19.1 %all_to_all.10 = f32[128,1,128]{2,1,0:T(1,128)S(1)} all-to-all(f32[128,1,128]{2,1,0:T(1,128)S(1)} %bitcast.15), channel_id=1, replica_groups=mesh['grp'=4,'gy'=32] {'grp','gy'}, dimensions={0} | all-to-all | bytes 131072 | tf_op jit(solution)/shard_map/all_to_all | solution.py:652
  31.1 0.0 collective-permute-done.2.y_low
  31.1 0.0 collective-permute-done.3.y_high
  31.1 0.0 copy-done.2
  31.1 8.4 %shard_map.97 = (f32[4,80,256]{2,1,0:T(8,128)S(1)}, f32[4,80,256]{2,1,0:T(8,128)S(1)}, f32[20,80,256]{2,1,0:T(8,128)S(1)}, f32[20,80,256]{2,1,0:T(8,128)S(1)}, f...) custom-call(f32[4,5]{1,0:T(4,128)S(1)} %bitcast.18, ...), custom_call_target="tpu_custom_call" | custom-call | flops 1073741824 | bytes 1048576 | tf_op jit(solution)/shard_map/pallas_call | solution.py:634
  39.5 6.8 %shard_map.98 = (f32[256,128]{1,0:T(8,128)S(1)}, f32[20,32,128]{2,1,0:T(8,128)S(1)}, f32[20,32,128]{2,1,0:T(8,128)S(1)}, f32[20,80,256]{2,1,0:T(8,128)S(1)}) custom-call(f32[32,32,128]{2,1,0:T(8,128)S(1)} %pad_maximum_fusion.planes, f32[128,128]{1,0:T(8,128)S(1)} %bitcast.12, f32[4,80,256]{2,1,0:T(8,128)S(1)} %get-tuple-element.38.cap_w.cap, ...), custom_call_target="tpu_custom_call" | custom-call | flops 1073741824 | bytes 1048576 | tf_op jit(solution)/shard_map/pallas_call | solution.py:634
  46.3 14.4 %all_to_all.11 = f32[128,2,128]{2,1,0:T(2,128)S(1)} all-to-all(f32[128,2,128]{2,1,0:T(2,128)S(1)} %bitcast.16), channel_id=1, replica_groups=mesh['grp'=4,'gy'=32] {'grp','gy'}, dimensions={0} | all-to-all | bytes 262144 | tf_op jit(solution)/shard_map/all_to_all | solution.py:652
  60.7 6.9 %shard_map.99 = (f32[20,32,128]{2,1,0:T(8,128)}, f32[20,32,128]{2,1,0:T(8,128)}, f32[20,32,128]{2,1,0:T(8,128)}) custom-call(f32[32,32,128]{2,1,0:T(8,128)S(1)} %pad_maximum_fusion.planes, f32[128,128]{1,0:T(8,128)S(1)} %bitcast.13, f32[256,128]{1,0:T(8,128)S(1)} %bitcast.14, f32[4,80,256]{2,1,0:T(8,128)S(1)} %get-tuple-element.38.cap_w.cap, ...), custom_call_target="tpu_custom_call" | custom-call | flops 1073741824 | bytes 1048576 | tf_op jit(solution)/shard_map/pallas_call | solution.py:634
  (1 shorter events, 0.0 us)
Async XLA Ops:
  0.6 6.0 %copy-start = (f32[4,5,5]{2,0,1:T(4,128)S(1)}, f32[4,5,5]{2,0,1:T(4,128)}, u32[]{:S(2)}) copy-start(f32[4,5,5]{2,0,1:T(4,128)} %param.13) | copy-start | bytes 1204
  0.6 6.0 %copy-start.1 = (s32[1,1,4]{2,1,0:T(1,128)S(1)}, s32[1,1,4]{2,1,0:T(1,128)}, u32[]{:S(2)}) copy-start(s32[1,1,4]{2,1,0:T(1,128)} %cmap.1) | copy-start | bytes 52
  0.7 30.5 %copy-start.2 = (f32[5,4]{0,1:T(4,128)S(1)}, f32[5,4]{0,1:T(4,128)}, u32[]{:S(2)}) copy-start(f32[5,4]{0,1:T(4,128)} %param.10) | copy-start | bytes 244
  2.9 5.3 %collective-permute-start = (f32[4,32,128]{2,1,0:T(8,128)S(1)}, f32[4,32,128]{2,1,0:T(8,128)S(1)}, u32[]{:S(2)}, u32[]{:S(2)}) collective-permute-start(f32[4,32,128]{2,1,0:T(8,128)S(1)} %get-tuple-element.28), channel_id=1, source_target_pairs={{0,32},{32,64},{64,96},{96,0},{1,33},{33,65},{65,97},{97,1},{2,34}... | collective-permute-start | bytes 196616 | tf_op jit(solution)/shard_map/ppermute | solution.py:664
  5.1 3.1 %collective-permute-start.1 = (f32[4,32,128]{2,1,0:T(8,128)S(1)}, f32[4,32,128]{2,1,0:T(8,128)S(1)}, u32[]{:S(2)}, u32[]{:S(2)}) collective-permute-start(f32[4,32,128]{2,1,0:T(8,128)S(1)} %get-tuple-element.29), channel_id=1, source_target_pairs={{32,0},{64,32},{96,64},{0,96},{33,1},{65,33},{97,65},{1,97},{34,2}... | collective-permute-start | bytes 196616 | tf_op jit(solution)/shard_map/ppermute | solution.py:664
  8.3 22.8 %collective-permute-start.2 = (f32[40,16,128]{2,1,0:T(8,128)S(1)}, f32[40,16,128]{2,1,0:T(8,128)S(1)}, u32[]{:S(2)}, u32[]{:S(2)}) collective-permute-start(f32[40,16,128]{2,1,0:T(8,128)S(1)} %get-tuple-element.33), channel_id=1, source_target_pairs={{0,1},{1,2},{2,3},{3,4},{4,5},{5,6},{6,7},{7,8},{8,9},{9,10},{10,1... | collective-permute-start | bytes 983048 | tf_op jit(solution)/shard_map/ppermute | solution.py:679
  12.0 19.1 %collective-permute-start.3 = (f32[40,16,128]{2,1,0:T(8,128)S(1)}, f32[40,16,128]{2,1,0:T(8,128)S(1)}, u32[]{:S(2)}, u32[]{:S(2)}) collective-permute-start(f32[40,16,128]{2,1,0:T(8,128)S(1)} %get-tuple-element.34), channel_id=1, source_target_pairs={{1,0},{2,1},{3,2},{4,3},{5,4},{6,5},{7,6},{8,7},{9,8},{10,9},{11,1... | collective-permute-start | bytes 983048 | tf_op jit(solution)/shard_map/ppermute | solution.py:679

commit v4 on v3

v4 whole, which is shorter than its diff:
```python
import functools

import jax
import jax.numpy as jnp
from jax import lax
from jax.experimental import pallas as pl
from jax.experimental.pallas import tpu as pltpu
from jax.sharding import PartitionSpec as P

SPECIES = 5
LAYERS = 4
MATS = 4
FIELDS = SPECIES * LAYERS
PLANES = FIELDS + 3 * LAYERS
POT0, CAP0, MAT0 = FIELDS, FIELDS + LAYERS, FIELDS + 2 * LAYERS
ROWS = 32
COLS = 128
N_GRP = 4
N_GY = 32
TOTAL = N_GRP * N_GY
NC = 512
DAMPING = 2.0 / 3.0
BOTH = ("grp", "gy")

HALO = 12
PER = 10
GROUPS = -(-PLANES // PER)
RHALO = 16
TALL = ROWS + 2 * RHALO
TOP = RHALO
HALF = COLS // 2
LATE = COLS + HALO - HALF
SEAM = 96
F32 = jnp.float32

G_RW, G_RAU, G_S, G_CY, G_CX, G_MOM = 0, 4, 8, 14, 30, 46
ROW_CAP = 250
MAP_LANE = 20
INV_LANE = 24


def lanes(shape):
    return lax.broadcasted_iota(jnp.int32, shape, 1)


def subs(shape):
    return lax.broadcasted_iota(jnp.int32, shape, 0)


def pack_kernel(planes, to_low, to_high):
    lane = lanes((ROWS, COLS))
    for g in range(GROUPS):
        low = jnp.zeros((ROWS, COLS), F32)
        high = jnp.zeros((ROWS, COLS), F32)
        for j in range(min(PER, PLANES - g * PER)):
            v = planes[g * PER + j]
            inside = (lane >= HALO * j) & (lane < HALO * (j + 1))
            low = jnp.where(inside, turn(v, HALO * j), low)
            high = jnp.where(inside, turn(v, HALO * j + HALO), high)
        to_low[g] = low
        to_high[g] = high


def turn(v, shift):
    shift = shift % v.shape[1]
    return v if shift == 0 else pltpu.roll(v, shift, 1)


def place(rows):
    n = rows.shape[0]
    total = jnp.sum(rows, axis=1, keepdims=True)
    spread = jnp.where(lanes((n, COLS)) == subs((n, COLS)), total, 0.0)
    return jnp.sum(spread, axis=0, keepdims=True)


def fold(v):
    return jnp.sum(v, axis=0, keepdims=True)


def harmonic(a, b):
    return 2.0 * a * b / (a + b)


def after(v, nxt, axis):
    first = lax.broadcasted_iota(jnp.int32, v.shape, axis) == 0
    return pltpu.roll(jnp.where(first, nxt, v), v.shape[axis] - 1, axis)


def power(m):
    p = jnp.where(m == 1.0, 2.0, 1.0)
    p = jnp.where(m == 2.0, 4.0, p)
    return jnp.where(m == 3.0, 8.0, p)


def own_kernel(diff, planes, cmap, inverse, out, acc, w, code_y, code_x, code_z, part, ids):
    part[...] = jnp.zeros(part.shape, F32)
    row = jnp.zeros((1, COLS), F32)
    for s in range(SPECIES):
        part[0:4, 0:SPECIES] = inverse[s]
        for k in range(4):
            row = row + turn(part[k : k + 1, :], INV_LANE + (k * SPECIES + s) * SPECIES)
    part[0:4, :] = jnp.zeros((4, COLS), F32)
    ids[...] = jnp.zeros(ids.shape, jnp.int32)
    ids[0:1, 0:MATS] = cmap[0]
    q = ids[0:1, :]
    row = row + turn(((q & 3) * TOTAL + (q >> 2)).astype(F32), MAP_LANE)
    for s in range(SPECIES):
        for m in range(MATS):
            total = jnp.zeros((ROWS, COLS), F32)
            for l in range(LAYERS):
                total = total + jnp.where(planes[MAT0 + l] == m, planes[s * LAYERS + l], 0.0)
            part[m * SPECIES + s : m * SPECIES + s + 1, :] = fold(total)
    out[...] = jnp.broadcast_to(row + place(part[...]), (TOTAL, COLS))

    acc[...] = jnp.zeros(acc.shape, F32)
    lane, sub = lanes((8, COLS)), subs((8, COLS))
    tiles = [8 * t for t in range(ROWS // 8)]
    for r in tiles:
        here = pl.ds(r, 8)
        for l in range(LAYERS):
            m = planes[MAT0 + l, here, :]
            is1, is2, is3 = m == 1.0, m == 2.0, m == 3.0
            down = jnp.exp(-0.5 * planes[POT0 + l, here, :])
            up = jnp.exp(0.5 * planes[POT0 + l, here, :])
            drift = (down, up, down * down, up * up, down)
            for s in range(SPECIES):
                d = jnp.where(is1, diff[1, s], diff[0, s])
                d = jnp.where(is2, diff[2, s], d)
                d = jnp.where(is3, diff[3, s], d)
                w[s * LAYERS + l, here, :] = d * drift[s]
            p = power(m)
            if r == tiles[-1]:
                code = jnp.where(sub == 7, 0.0, p + power(after(m, m, 0)))
            else:
                code = p + power(after(m, planes[MAT0 + l, pl.ds(r + 8, 8), :], 0))
            code_y[l, here, :] = code
            code_x[l, here, :] = jnp.where(lane == COLS - 1, 0.0, p + power(turn(m, -1)))
            if l + 1 < LAYERS:
                code_z[l, here, :] = p + power(planes[MAT0 + l + 1, here, :])

    @pl.loop(0, SPECIES)
    def _(s):
        pairs = [jnp.zeros((8, COLS), F32)] * 6
        codes = (3.0, 5.0, 9.0, 6.0, 10.0, 12.0)
        for r in tiles:
            here = pl.ds(r, 8)
            for l in range(LAYERS):
                k = s * LAYERS + l
                c = w[k, here, :]
                nxt = c if r == tiles[-1] else w[k, pl.ds(r + 8, 8), :]
                kinds = [
                    (code_y[l, here, :], harmonic(c, after(c, nxt, 0))),
                    (code_x[l, here, :], harmonic(c, turn(c, -1))),
                ]
                if l + 1 < LAYERS:
                    kinds.append((code_z[l, here, :], 0.5 * harmonic(c, w[k + 1, here, :])))
                for code, edge in kinds:
                    for i in range(6):
                        pairs[i] = pairs[i] + jnp.where(code == codes[i], edge, 0.0)
        for i in range(6):
            acc[pl.ds((G_S + i) * SPECIES + s, 1), :] = fold(pairs[i])

    for i in range(MATS):
        total = jnp.zeros((ROWS, COLS), F32)
        for l in range(LAYERS):
            total = total + jnp.where(planes[MAT0 + l] == i, planes[CAP0 + l], 0.0)
        acc[ROW_CAP + i : ROW_CAP + i + 1, :] = fold(total)


def rows_kernel(planes, from_low, from_high, to_low, to_high):
    for k in range(PLANES):
        to_low[k] = planes[k, :RHALO]
        to_high[k] = planes[k, ROWS - RHALO :]
    for g in range(GROUPS):
        for i, part in enumerate((from_low, from_high)):
            k = PLANES + i * GROUPS + g
            to_low[k] = part[g, :RHALO]
            to_high[k] = part[g, ROWS - RHALO :]


def at(l, y):
    return pl.ds(pl.multiple_of((y + l * TALL) * 8, 8), 8)


def each_row(first, count, step, carry=()):
    def block(i, carry):
        for r in range(4):
            carry = step(first + 4 * i + r, carry)
        return carry

    return lax.fori_loop(0, count // 4, block, carry)


def stencil(src, ops, wide, emit, carry=()):
    cap, gy, gx, gz = ops[:4]
    first = TOP - wide
    span = range(LAYERS)
    now = [src[at(l, first), :] for l in span]
    flux = [gy[at(l, first - 1), :] * (src[at(l, first - 1), :] - now[l]) for l in span]

    def step(y, carry):
        now, flux, carry = carry
        nxt, out_flux = [], []
        flux_z = None
        for l in span:
            here = at(l, y)
            u = now[l]
            above = src[at(l, y + 1), :]
            flux_x = gx[here, :] * (u - turn(u, -1))
            flux_y = gy[here, :] * (u - above)
            out = cap[here, :] * u + (flux_x - turn(flux_x, 1)) + (flux_y - flux[l])
            if flux_z is not None:
                out = out - flux_z
            if l + 1 < LAYERS:
                flux_z = gz[here, :] * (u - now[l + 1])
                out = out + flux_z
            nxt.append(above)
            out_flux.append(flux_y)
            carry = emit(l, y, u, out, carry)
        return nxt, out_flux, carry

    return each_row(first, ROWS + 2 * wide, step, (now, flux, carry))[2]


def sweep(src, resid, dst, ops, wide):
    scale = ops[4]

    def emit(l, y, u, out, carry):
        here = at(l, y)
        dst[here, :] = u + scale[here, :] * (resid[here, :] - out)
        return carry

    stencil(src, ops, wide, emit)


def image(src, dst, ops, wide):
    def emit(l, y, u, out, carry):
        dst[at(l, y), :] = out
        return carry

    stencil(src, ops, wide, emit)


def start_sweep(resid, dst, scale, wide):
    def step(y, carry):
        for l in range(LAYERS):
            here = at(l, y)
            dst[here, :] = scale[here, :] * resid[here, :]
        return carry

    each_row(TOP - wide, ROWS + 2 * wide, step)


def used(tile):
    lane, sub = lanes(tile.shape), subs(tile.shape)
    early = (sub < SPECIES) & (lane >= HALO) & (lane < HALO + SEAM)
    place_in = lane & (HALF - 1)
    late = (sub >= SPECIES) & (place_in >= SEAM - LATE) & (place_in < COLS - LATE)
    late = late & ((sub < 7) | (lane < HALF))
    return jnp.where(early | late, tile, 0.0)


def by_species(tile):
    lane, sub = lanes(tile.shape), subs(tile.shape)
    left = lane < HALF
    out = tile
    out = out + jnp.where((sub == 0) & left, pltpu.roll(tile, 3, 0), 0.0)
    pick = ((sub == 1) & ~left) | ((sub == 2) & left)
    out = out + jnp.where(pick, pltpu.roll(tile, 4, 0), 0.0)
    pick = ((sub == 3) & ~left) | ((sub == 4) & left)
    out = out + jnp.where(pick, pltpu.roll(tile, 5, 0), 0.0)
    return out[:SPECIES]


def keep(acc, group, tile):
    acc[group * SPECIES : (group + 1) * SPECIES, :] = by_species(tile)


def split3(x):
    hi = x.astype(jnp.bfloat16)
    rest = x - hi.astype(F32)
    mid = rest.astype(jnp.bfloat16)
    lo = (rest - mid.astype(F32)).astype(jnp.bfloat16)
    return jnp.concatenate([hi, mid, lo], axis=0)


def exact_dot(x, onehot):
    n = x.shape[0]
    y = jnp.dot(
        jnp.concatenate([split3(x)], axis=0), onehot, preferred_element_type=F32
    )
    return y[:n] + y[n : 2 * n] + y[2 * n :]


def build_scatter(got, onehot):
    for m in range(MATS):
        col = jnp.broadcast_to(got[:, MAP_LANE + m : MAP_LANE + m + 1], (TOTAL, COLS))
        for k in range(4):
            target = (lanes((TOTAL, COLS)) + k * COLS).astype(F32)
            onehot[m * TOTAL : (m + 1) * TOTAL, k * COLS : (k + 1) * COLS] = jnp.where(
                col == target, 1.0, 0.0
            ).astype(jnp.bfloat16)


def build_gather(turned, onehot):
    for m in range(MATS):
        row = jnp.broadcast_to(turned[MAP_LANE + m : MAP_LANE + m + 1, :], (COLS, TOTAL))
        for k in range(4):
            target = (subs((COLS, TOTAL)) + k * COLS).astype(F32)
            onehot[k * COLS : (k + 1) * COLS, m * TOTAL : (m + 1) * TOTAL] = jnp.where(
                row == target, 1.0, 0.0
            ).astype(jnp.bfloat16)


def build_near(got, onehot):
    gx, gy = lax.axis_index("grp"), lax.axis_index("gy")
    lane = lanes((1, COLS))
    row = jnp.full((1, COLS), -1.0, F32)
    for iy in range(3):
        y = lax.rem(gy + (N_GY - 1 + iy), N_GY)
        for ix in range(3):
            x = jnp.clip(gx + (ix - 1), 0, N_GRP - 1)
            region = iy * 3 + ix
            here = got[pl.ds(x * N_GY + y, 1), :]
            inside = (lane >= region * MATS) & (lane < (region + 1) * MATS)
            row = jnp.where(inside, turn(here, region * MATS - MAP_LANE), row)
    for k in range(4):
        target = (subs((COLS, COLS)) + k * COLS).astype(F32)
        onehot[k * COLS : (k + 1) * COLS, :] = jnp.where(
            jnp.broadcast_to(row, (COLS, COLS)) == target, 1.0, 0.0
        ).astype(jnp.bfloat16)


def coarse_solve(sums, turned, scatter):
    res = exact_dot(sums, scatter[...])
    parts = []
    for k in range(4):
        total = None
        for t in range(SPECIES):
            start = INV_LANE + k * SPECIES * SPECIES + t * SPECIES
            term = turned[start : start + 8, :] * res[t : t + 1, k * COLS : (k + 1) * COLS]
            total = term if total is None else total + term
        parts.append(total)
    sol = jnp.concatenate(parts, axis=1)
    return jnp.where(subs(sol.shape) < SPECIES, sol, 0.0)


def local_sums(turned, group):
    x = jnp.concatenate(
        [turned[(group + m) * SPECIES : (group + m) * SPECIES + 8, :] for m in range(MATS)], axis=1
    )
    return jnp.where(subs(x.shape) < SPECIES, x, 0.0)


def spread_values(near, values):
    lane, sub = lanes((8, COLS)), subs((8, COLS))

    def arrange(a, b, c):
        row = lambda s: jnp.broadcast_to(near[s : s + 1, :], (8, COLS))
        out = jnp.where(sub == 5, row(a), near)
        return jnp.where(sub == 7, row(c), jnp.where(sub == 6, row(b), out))

    left, right = arrange(0, 2, 4), arrange(1, 3, 4)
    early = sub < SPECIES
    for iy in range(3):
        for m in range(MATS):
            column = lambda v, ix: jnp.broadcast_to(
                v[:, (iy * 3 + ix) * MATS + m : (iy * 3 + ix) * MATS + m + 1], (8, COLS)
            )
            first = jnp.where(early & (lane < HALO), column(left, 0), column(left, 1))
            first = jnp.where(~early & (lane >= COLS - LATE), column(left, 2), first)
            second = jnp.where(lane >= HALF + COLS - LATE, column(right, 2), column(right, 1))
            values[(iy * MATS + m) * 8 : (iy * MATS + m + 1) * 8, :] = jnp.where(
                early | (lane < HALF), first, second
            )


def coarse_rows(values, mat, wide, emit):
    for iy, first, count in ((0, TOP - wide, wide), (1, TOP, ROWS), (2, TOP + ROWS, wide)):
        if count == 0:
            continue
        v = [values[(iy * MATS + m) * 8 : (iy * MATS + m + 1) * 8, :] for m in range(MATS)]

        def step(y, carry):
            for l in range(LAYERS):
                emit(l, y, coarse_pick(v, mat[at(l, y), :]))
            return carry

        each_row(first, count, step)


def coarse_pick(v, m):
    out = jnp.where(m == 1.0, v[1], v[0])
    out = jnp.where(m == 2.0, v[2], out)
    return jnp.where(m == 3.0, v[3], out)


def table_kernel(
    diff, planes, x_low, x_high, y_low, y_high, acc_in,
    cap_w, mat_w, gy, gx, gz, scale, y0, acc, b_w,
    w, za,
):
    lane, sub = lanes((8, COLS)), subs((8, COLS))
    left = lane < HALF

    def pick(strip, own, k, t):
        if t < 2:
            return y_low[strip, 8 * t : 8 * t + 8, :]
        if t < 6:
            return own[k, 8 * (t - 2) : 8 * (t - 2) + 8, :]
        return y_high[strip, 8 * (t - 6) : 8 * (t - 6) + 8, :]

    def both(k, t):
        g, j = divmod(k, PER)
        v = pick(k, planes, k, t)
        low = pick(PLANES + g, x_low, g, t)
        high = pick(PLANES + GROUPS + g, x_high, g, t)
        early = jnp.where(lane < HALO, turn(low, -HALO * j), turn(v, HALO))
        late = jnp.where(lane < COLS - LATE, turn(v, -LATE), turn(high, COLS - LATE - HALO * j))
        return early, late

    def put(dst, l, t, s, v):
        dst[pl.ds((l * TALL + 8 * t) * 8 + s, 8, stride=8), :] = v

    pairs = ((0, 1), (2, 3), (4, 4))
    d_late = [
        [jnp.where(left, diff[m, a], diff[m, b]) for m in range(MATS)] for a, b in pairs
    ]

    def choose(v, is1, is2, is3):
        return jnp.where(is3, v[3], jnp.where(is2, v[2], jnp.where(is1, v[1], v[0])))

    for l in range(LAYERS):
        for t in range(TALL // 8):
            late_b = []
            for s in range(SPECIES):
                early, late = both(s * LAYERS + l, t)
                put(b_w, l, t, s, early)
                late_b.append(late)
            for i, (a, b) in enumerate(pairs):
                put(b_w, l, t, SPECIES + i, jnp.where(left, late_b[a], turn(late_b[b], HALF)))
            for dst, base in ((cap_w, CAP0), (mat_w, MAT0)):
                early, late = both(base + l, t)
                late = jnp.where(left, late, turn(late, HALF))
                for s in range(8):
                    put(dst, l, t, s, early if s < SPECIES else late)
            m_early, m_late = early, late
            early, late = both(POT0 + l, t)
            late = jnp.where(left, late, turn(late, HALF))
            is_m = [m_early == float(m) for m in (1, 2, 3)]
            down, up = jnp.exp(-0.5 * early), jnp.exp(0.5 * early)
            drift = (down, up, down * down, up * up, down)
            for s in range(SPECIES):
                put(w, l, t, s, choose([diff[m, s] for m in range(MATS)], *is_m) * drift[s])
            is_m = [m_late == float(m) for m in (1, 2, 3)]
            down, up = jnp.exp(-0.5 * late), jnp.exp(0.5 * late)
            mixed = jnp.where(left, down, up)
            drift = (mixed, mixed * mixed, down)
            for i in range(3):
                put(w, l, t, SPECIES + i, choose(d_late[i], *is_m) * drift[i])

    me_x = lax.axis_index("grp")
    closed = ((sub >= SPECIES) & ((lane & (HALF - 1)) == COLS - 1 - LATE) & (me_x == N_GRP - 1)) | (
        (sub < SPECIES) & (lane == HALO - 1) & (me_x == 0)
    )
    span = range(LAYERS)
    first = TOP - 12

    def edge_step(y, carry):
        now, edge_y = carry
        nxt, out_y = [], []
        ez_below = None
        for l in span:
            here = at(l, y)
            c = now[l]
            above = w[at(l, y + 1), :]
            ey = harmonic(c, above)
            ex = jnp.where(closed, 0.0, harmonic(c, turn(c, -1)))
            gy[here, :] = ey
            gx[here, :] = ex
            d = cap_w[here, :] + ey + edge_y[l] + ex + turn(ex, 1)
            if ez_below is not None:
                d = d + ez_below
            if l + 1 < LAYERS:
                ez_below = 0.5 * harmonic(c, now[l + 1])
                gz[here, :] = ez_below
                d = d + ez_below
            scale[here, :] = DAMPING / d
            nxt.append(above)
            out_y.append(ey)
        return nxt, out_y

    now = [w[at(l, first), :] for l in span]
    edge_y = [harmonic(w[at(l, first - 1), :], now[l]) for l in span]
    each_row(first, ROWS + 24, edge_step, (now, edge_y))

    ops = (cap_w, gy, gx, gz, scale)
    start_sweep(b_w, za, scale, 12)
    sweep(za, b_w, y0, ops, 10)
    sweep(y0, b_w, za, ops, 10)
    sweep(za, b_w, y0, ops, 8)

    acc[...] = acc_in[...]
    zero = jnp.zeros((8, COLS), F32)
    last = TOP + ROWS - 1
    cy = [zero] * 16
    for l in span:
        code = mat_w[at(l, last), :] * 4.0 + mat_w[at(l, last + 1), :]
        edge = gy[at(l, last), :]
        for i in range(16):
            cy[i] = cy[i] + jnp.where(code == float(i), edge, 0.0)
    for i in range(16):
        keep(acc, G_CY + i, used(cy[i]))

    place_in = lane & (HALF - 1)

    def cross_step(y8, cx):
        side, side_code = zero, zero - 1.0
        for r in range(8):
            for l in span:
                here = at(l, TOP + 8 * y8 + r)
                p = r * LAYERS + l
                m = mat_w[here, :]
                code = m * 4.0 + turn(m, -1)
                target = place_in == COLS - 1 - LATE - p
                side = jnp.where(target, turn(gx[here, :], -p), side)
                side_code = jnp.where(target, turn(code, -p), side_code)
        return [cx[i] + jnp.where(side_code == float(i), side, 0.0) for i in range(16)]

    cx = lax.fori_loop(0, ROWS // 8, cross_step, [zero] * 16)
    valid = (sub >= SPECIES) & ((sub < 7) | left)
    for i in range(16):
        keep(acc, G_CX + i, jnp.where(valid, cx[i], 0.0))


def first_kernel(
    planes, got, cap_w, mat_w, gy, gx, gz, scale, y0, acc_in, b_w,
    second, z0, w0, u_out,
    za, zb, scatter, near_hot, turned, values, acc,
):
    ops = (cap_w, gy, gx, gz, scale)

    turned[...] = got[...].T
    build_scatter(got, scatter)
    build_near(got, near_hot)
    sol = coarse_solve(local_sums(turned, 0), turned, scatter)
    spread_values(exact_dot(sol, near_hot[...]), values)

    def add_coarse(l, y, c):
        z0[at(l, y), :] = y0[at(l, y), :] + c

    coarse_rows(values, mat_w, 8, add_coarse)
    image(z0, w0, ops, 8)
    start_sweep(w0, za, scale, 8)
    sweep(za, w0, zb, ops, 6)
    sweep(zb, w0, za, ops, 6)
    sweep(za, w0, u_out, ops, 4)

    acc[...] = acc_in[...]

    def emit(l, y, u, au, carry):
        rw, rau, mom = carry
        here = at(l, y)
        m = mat_w[here, :]
        wv, zv, bv = w0[here, :], z0[here, :], b_w[here, :]
        is_m = [m == float(i) for i in range(MATS)]
        rw = [rw[i] + jnp.where(is_m[i], wv, 0.0) for i in range(MATS)]
        rau = [rau[i] + jnp.where(is_m[i], au, 0.0) for i in range(MATS)]
        mom = [mom[0] + bv * zv, mom[1] + zv * wv, mom[2] + wv * u, mom[3] + u * au]
        return rw, rau, mom

    zero = jnp.zeros((8, COLS), F32)
    sums = stencil(u_out, ops, 0, emit, ([zero] * 4, [zero] * 4, [zero] * 4))
    for group, tiles in zip((G_RW, G_RAU, G_MOM), sums):
        for i, v in enumerate(tiles):
            keep(acc, group + i, used(v))

    even = lax.rem(subs((2 * TOTAL, COLS)), 2) == 0
    second[...] = jnp.where(even, place(acc[0:COLS, :]), place(acc[COLS : 2 * COLS, :]))


def next_y(x):
    y = lax.rem(lanes(x.shape), N_GY)
    return jnp.where(y == N_GY - 1, turn(x, N_GY - 1), turn(x, -1))


def prev_y(x):
    y = lax.rem(lanes(x.shape), N_GY)
    return jnp.where(y == 0, turn(x, -(N_GY - 1)), turn(x, 1))


def total_of(x):
    return jnp.sum(jnp.sum(x, axis=0, keepdims=True), axis=1, keepdims=True)


def second_kernel(
    planes, got, got2, cap, mat, gy, gx, gz, scale, z0, w0, u,
    out_x, out_r, out_z,
    v1, w1, za, zb, px, pr, pz, scatter, gather, near_hot, turned, turned2, values, values2,
):
    turned[...] = got[...].T
    turned2[0:COLS, :] = got2[pl.ds(0, TOTAL, stride=2), :].T
    turned2[COLS : 2 * COLS, :] = got2[pl.ds(1, TOTAL, stride=2), :].T
    build_scatter(got, scatter)
    build_gather(turned, gather)
    build_near(got, near_hot)

    sums_w = local_sums(turned2, G_RW)
    sol = coarse_solve(sums_w, turned, scatter)
    spread_values(exact_dot(sol, near_hot[...]), values)
    c_all = exact_dot(sol, gather[...])
    c = [c_all[:, m * TOTAL : (m + 1) * TOTAL] for m in range(MATS)]

    def rows5(group):
        return turned2[group * SPECIES : group * SPECIES + 8, :]

    live = subs((8, TOTAL)) < SPECIES
    bc = [turned2[ROW_CAP + m : ROW_CAP + m + 1, :] * c[m] for m in range(MATS)]
    n = 0
    for i in range(MATS):
        for j in range(i + 1, MATS):
            f = rows5(G_S + n) * (c[i] - c[j])
            bc[i] = bc[i] + f
            bc[j] = bc[j] - f
            n += 1
    c_y = [next_y(v) for v in c]
    c_x = [turn(v, -N_GY) for v in c]
    back_y = [jnp.zeros((8, TOTAL), F32)] * MATS
    back_x = [jnp.zeros((8, TOTAL), F32)] * MATS
    for i in range(MATS):
        for j in range(MATS):
            f = rows5(G_CY + 4 * i + j) * (c[i] - c_y[j])
            bc[i] = bc[i] + f
            back_y[j] = back_y[j] + f
            f = rows5(G_CX + 4 * i + j) * (c[i] - c_x[j])
            bc[i] = bc[i] + f
            back_x[j] = back_x[j] + f
    for j in range(MATS):
        bc[j] = jnp.where(live, bc[j] - prev_y(back_y[j]) - turn(back_x[j], N_GY), 0.0)
    bc_all = jnp.concatenate(bc, axis=1)
    sums_au = local_sums(turned2, G_RAU)
    sol2 = coarse_solve(sums_au + bc_all, turned, scatter)
    spread_values(exact_dot(sol2, near_hot[...]), values2)

    def moment(i):
        return total_of(jnp.where(live, rows5(G_MOM + i), 0.0))

    m0, m1 = moment(0), moment(1)
    m2 = moment(2) + total_of(sums_w * c_all)
    m3 = moment(3) + total_of((2.0 * sums_au + bc_all) * c_all)
    a0 = m0 / m1
    rz1 = m0 - 2.0 * a0 * m1 + a0 * a0 * m2
    g = 1.0 + rz1 / m0
    a1 = rz1 / (g * g * m1 - 2.0 * a0 * g * m2 + a0 * a0 * m3)
    ca = jnp.broadcast_to(a0 + a1 * g, (8, COLS))
    cb = jnp.broadcast_to(a1 * a0, (8, COLS))

    ops = (cap, gy, gx, gz, scale)

    def add_coarse(l, y, c):
        v1[at(l, y), :] = u[at(l, y), :] + c

    coarse_rows(values, mat, 4, add_coarse)
    image(v1, w1, ops, 4)
    start_sweep(w1, za, scale, 4)
    sweep(za, w1, zb, ops, 2)
    sweep(zb, w1, za, ops, 2)
    own_values = [values2[(MATS + m) * 8 : (MATS + m + 1) * 8, :] for m in range(MATS)]

    def emit(l, y, z, out, carry):
        here = at(l, y)
        w1v, v1v = w1[here, :], v1[here, :]
        z0v, w0v = z0[here, :], w0[here, :]
        v2 = z + scale[here, :] * (w1v - out) + coarse_pick(own_values, mat[here, :])
        px[here, :] = ca * z0v - cb * v1v
        pr[here, :] = ca * w0v - cb * w1v
        pz[here, :] = z0v - ca * v1v + cb * v2
        return carry

    stencil(za, ops, 0, emit)

    lane = lanes((8, COLS))

    def unpacked(src, l, row, s):
        start = (l * TALL + TOP + row) * 8
        early = src[pl.ds(start + s, 8, stride=8), :]
        late = src[pl.ds(start + SPECIES + s // 2, 8, stride=8), :]
        return jnp.where(
            lane < SEAM, turn(early, -HALO), turn(late, LATE - (s % 2) * HALF)
        )

    for s in range(SPECIES):
        for l in range(LAYERS):
            for row in range(0, ROWS, 8):
                k, rows = s * LAYERS + l, slice(row, row + 8)
                out_x[k, rows, :] = unpacked(px, l, row, s)
                out_r[k, rows, :] = planes[k, rows, :] - unpacked(pr, l, row, s)
                out_z[k, rows, :] = unpacked(pz, l, row, s)


def shape(*dims):
    return jax.ShapeDtypeStruct(dims, F32)


VMEM = pl.BlockSpec(memory_space=pltpu.VMEM)
SMEM = pl.BlockSpec(memory_space=pltpu.SMEM)
PARAMS = pltpu.CompilerParams(vmem_limit_bytes=20 * 1024 * 1024)


def run(kernel, outs, scratch, in_specs, cost, *args):
    return pl.pallas_call(
        kernel,
        out_shape=outs,
        in_specs=in_specs,
        out_specs=jax.tree.map(lambda _: VMEM, outs),
        scratch_shapes=scratch,
        compiler_params=PARAMS,
        cost_estimate=pl.CostEstimate(flops=cost, bytes_accessed=1 << 20, transcendentals=0),
    )(*args)


def shifts(axis, count):
    forward = [(i, (i + 1) % count) for i in range(count)]
    backward = [(target, source) for source, target in forward]
    return (functools.partial(lax.ppermute, axis_name=axis, perm=p) for p in (forward, backward))


def to_all(rows):
    got = lax.all_to_all(rows.reshape(TOTAL, -1, COLS), BOTH, 0, 0, tiled=True)
    return got.reshape(rows.shape)


def body(right_side, potential, capacity, diffusivity, material, coarse_map, coarse_inverse):
    b = right_side.reshape(FIELDS, ROWS, COLS)
    right, left = shifts("grp", N_GRP)
    down, up = shifts("gy", N_GY)

    planes = jnp.concatenate([b, potential, capacity, material.astype(F32)])
    packed = shape(GROUPS, ROWS, COLS)
    to_low, to_high = run(pack_kernel, (packed, packed), [], [VMEM], 1 << 20, planes)
    x_low, x_high = right(to_high), left(to_low)
    code = pltpu.VMEM((LAYERS, ROWS, COLS), F32)
    first, acc = run(
        own_kernel,
        (shape(TOTAL, COLS), shape(2 * COLS, COLS)),
        [pltpu.VMEM((FIELDS, ROWS, COLS), F32), code, code, code]
        + [pltpu.VMEM((24, COLS), F32), pltpu.VMEM((8, COLS), jnp.int32)],
        [SMEM] + [VMEM] * 3,
        1 << 20,
        diffusivity.T, planes, coarse_map, jnp.transpose(coarse_inverse, (1, 0, 2)),
    )

    strips = shape(PLANES + 2 * GROUPS, RHALO, COLS)
    to_low, to_high = run(
        rows_kernel, (strips, strips), [], [VMEM] * 3, 1 << 20, planes, x_low, x_high
    )
    first, to_low, to_high = lax.optimization_barrier((first, to_low, to_high))
    y_low, y_high = down(to_high), up(to_low)
    got, y_low, y_high = lax.optimization_barrier((to_all(first), y_low, y_high))

    packed = shape(LAYERS * TALL * 8, COLS)
    field = shape(FIELDS, ROWS, COLS)
    big = pltpu.VMEM(packed.shape, F32)
    hot = pltpu.VMEM((NC, MATS * TOTAL), jnp.bfloat16)
    near = pltpu.VMEM((NC, COLS), jnp.bfloat16)
    square = pltpu.VMEM((COLS, COLS), F32)
    double = pltpu.VMEM((2 * COLS, COLS), F32)
    values = pltpu.VMEM((3 * MATS * 8, COLS), F32)
    cap_w, mat_w, gy, gx, gz, scale, y0, acc, b_w = run(
        table_kernel,
        (packed,) * 7 + (shape(2 * COLS, COLS), packed),
        [big] * 2,
        [SMEM] + [VMEM] * 6,
        1 << 30,
        diffusivity.T, planes, x_low, x_high, y_low, y_high, acc,
    )
    second, z0, w0, u = run(
        first_kernel,
        (shape(2 * TOTAL, COLS), packed, packed, packed),
        [big] * 2 + [hot, near, square, values, double],
        [VMEM] * 11,
        1 << 30,
        planes, got, cap_w, mat_w, gy, gx, gz, scale, y0, acc, b_w,
    )
    got2 = to_all(second)
    out = run(
        second_kernel,
        (field, field, field),
        [big] * 7 + [hot, hot, near, square, double, values, values],
        [VMEM] * 12,
        1 << 30,
        planes, got, got2, cap_w, mat_w, gy, gx, gz, scale, z0, w0, u,
    )
    return tuple(o.reshape(right_side.shape) for o in out)


def solution(mesh):
    placed = (
        P(None, None, "gy", "grp"),
        P(None, "gy", "grp"),
        P(None, "gy", "grp"),
        P(),
        P(None, "gy", "grp"),
        P("gy", "grp", None),
        P(("grp", "gy"), None, None),
    )
    return jax.shard_map(
        body,
        mesh=mesh,
        in_specs=placed,
        out_specs=(P(None, None, "gy", "grp"),) * 3,
        check_vma=False,
    )
```

time: 67.9 us -> 84.8 us (1.25)
  Pallas kernels: 22.7 us -> 41.2 us
  waiting for transfers between devices: 1.34 us -> 0.01 us
  starting transfers between devices: 7.41 us -> 6.48 us
    pallas_call x6, Pallas kernels: 22.7 us -> 41.2 us  [run(): pl.pallas_call(kernel, out_shape=outs, in_specs=in_specs, out_specs=jax.t...]
    ppermute x2, waiting for transfers between devices: 1.34 us -> 0.01 us  [body(): x_low, x_high = (right(to_high), left(to_low))]
    ppermute x2, starting transfers between devices: 3.7 us -> 2.75 us  [body(): y_low, y_high = (down(to_high), up(to_low))]
  transfers between devices with their start and end apart: 4 -> 4, of which waited for: 1 -> 0; matrix products, arithmetic and copies ran while one was open for 0% -> 0% of each run, Pallas kernels for 0% -> 2%
where the time goes in v4:
time: 84.8 us; the launch traced here: 84.5 us
  Pallas kernels  41.2 us (49%)
  blocking collectives  33.5 us (40%)
  starting transfers between devices  6.48 us (8%)
  other arithmetic  1.89 us (2%)
    pallas_call x6, Pallas kernels, run(): pl.pallas_call(kernel, out_shape=outs, in_specs=in_specs, out_specs=jax.t...  41.2 us
    all_to_all x2, blocking collectives, to_all(): got = lax.all_to_all(rows.reshape(TOTAL, -1, COLS), BOTH, 0, 0, tiled=True)  33.5 us
    ppermute x2, starting transfers between devices, body(): x_low, x_high = (right(to_high), left(to_low))  3.72 us
    ppermute x2, starting transfers between devices, body(): y_low, y_high = (down(to_high), up(to_low))  2.75 us
  transfers between devices with their start and end apart: 4, of which 0 were waited for; matrix products, arithmetic and copies ran while one was open for 0% of the time, Pallas kernels for 2%

profile of v4, /device:TPU:1, one launch (start us, length us, event | category | flops | bytes accessed | tf_op | source)
XLA Modules:
  0.0 84.5 jit_solution(17738010847410129292)
XLA Ops:
  0.6 0.0 copy-start.3
  0.6 0.0 copy-start.4
  0.7 0.9 %convert_element_type.3 = f32[4,32,128]{2,1,0:T(8,128)S(1)} convert(s32[4,32,128]{2,1,0:T(8,128)} %param.11) | non-fusion elementwise | flops 16384 | bytes 131072 | tf_op jit(solution)/shard_map/convert_element_type | solution.py:738
  1.5 0.0 copy-done.3
  1.5 0.0 copy-done.4
  1.5 1.0 %pad_maximum_fusion.planes = f32[32,32,128]{2,1,0:T(8,128)S(1)} fusion(f32[4,32,128]{2,1,0:T(8,128)S(1)} %convert_element_type.3, f32[4,32,128]{2,1,0:T(8,128)S(1)} %copy-done.3, f32[4,32,128]{2,1,0:T(8,128)S(1)} %copy-done.4, f32[20,32,128]{2,1,0:T(8,128)} %bitcast.20), kind=kLoop, calls=%fused_computation | loop fusion | flops 393216 | bytes 1048576 | tf_op jit(solution)/shard_map/concatenate | solution.py:738
  2.6 0.0 copy-start
  2.6 0.3 shard_map.95
  2.9 2.2 %collective-permute-start = (f32[4,32,128]{2,1,0:T(8,128)S(1)}, f32[4,32,128]{2,1,0:T(8,128)S(1)}, u32[]{:S(2)}, u32[]{:S(2)}) collective-permute-start(f32[4,32,128]{2,1,0:T(8,128)S(1)} %get-tuple-element.32), channel_id=1, source_target_pairs={{0,32},{32,64},{64,96},{96,0},{1,33},{33,65},{65,97},{97,1},{2,34}... | collective-permute-start | bytes 196616 | tf_op jit(solution)/shard_map/ppermute | solution.py:741
  5.1 0.0 copy-start.1
  5.1 1.5 %collective-permute-start.1 = (f32[4,32,128]{2,1,0:T(8,128)S(1)}, f32[4,32,128]{2,1,0:T(8,128)S(1)}, u32[]{:S(2)}, u32[]{:S(2)}) collective-permute-start(f32[4,32,128]{2,1,0:T(8,128)S(1)} %get-tuple-element.33), channel_id=1, source_target_pairs={{32,0},{64,32},{96,64},{0,96},{33,1},{65,33},{97,65},{1,97},{34,2}... | collective-permute-start | bytes 196616 | tf_op jit(solution)/shard_map/ppermute | solution.py:741
  6.6 0.0 copy-start.2
  6.6 0.0 copy-done
  6.6 0.0 copy-done.1
  6.6 0.6 copy-done.2
  7.3 1.8 %shard_map.94 = (f32[128,128]{1,0:T(8,128)S(1)}, f32[256,128]{1,0:T(8,128)S(1)}) custom-call(f32[4,5]{1,0:T(4,128)S(1)} %bitcast.18, f32[32,32,128]{2,1,0:T(8,128)S(1)} %pad_maximum_fusion.planes, s32[1,1,4]{2,1,0:T(1,128)S(1)} %copy-done.2, f32[5,4,5]{2,1,0:T(4,128)S(1)} %bitcast.17), custom_call_target="tpu_custom_call" | custom-call | flops 1048576 | bytes 1048576 | tf_op jit(solution)/shard_map/pallas_call | solution.py:711
  9.1 0.0 collective-permute-done.from_low.x_low
  9.1 0.0 collective-permute-done.1.from_high.x_high
  9.2 2.7 %collective-permute-start.2 = (f32[40,16,128]{2,1,0:T(8,128)S(1)}, f32[40,16,128]{2,1,0:T(8,128)S(1)}, u32[]{:S(2)}, u32[]{:S(2)}) collective-permute-start(f32[40,16,128]{2,1,0:T(8,128)S(1)} %get-tuple-element.37), channel_id=1, source_target_pairs={{0,1},{1,2},{2,3},{3,4},{4,5},{5,6},{6,7},{7,8},{8,9},{9,10},{10,1... | collective-permute-start | bytes 983048 | tf_op jit(solution)/shard_map/ppermute | solution.py:758
  12.0 0.0 collective-permute-start.3
  12.0 19.1 %all_to_all.10 = f32[128,1,128]{2,1,0:T(1,128)S(1)} all-to-all(f32[128,1,128]{2,1,0:T(1,128)S(1)} %bitcast.16), channel_id=1, replica_groups=mesh['grp'=4,'gy'=32] {'grp','gy'}, dimensions={0} | all-to-all | bytes 131072 | tf_op jit(solution)/shard_map/all_to_all | solution.py:729
  31.1 0.0 collective-permute-done.2.y_low
  31.1 0.0 collective-permute-done.3.y_high
  31.1 19.7 %shard_map.97 = (f32[2048,128]{1,0:T(8,128)S(1)}, f32[2048,128]{1,0:T(8,128)S(1)}, f32[2048,128]{1,0:T(8,128)S(1)}, f32[2048,128]{1,0:T(8,128)S(1)}, f32[2048,12...) custom-call(f32[4,5]{1,0:T(4,128)S(1)} %bitcast.19, ...), custom_call_target="tpu_custom_call" | custom-call | flops 1073741824 | bytes 1048576 | tf_op jit(solution)/shard_map/pallas_call | solution.py:711
  50.7 10.1 %shard_map.98 = (f32[256,128]{1,0:T(8,128)S(1)}, f32[2048,128]{1,0:T(8,128)S(1)}, f32[2048,128]{1,0:T(8,128)S(1)}, f32[2048,128]{1,0:T(8,128)S(1)}) custom-call(f32[32,32,128]{2,1,0:T(8,128)S(1)} %pad_maximum_fusion.planes, f32[128,128]{1,0:T(8,128)S(1)} %bitcast.12, f32[2048,128]{1,0:T(8,128)S(1)} %get-tuple-element.43.cap_w.cap, ...), custom_call_target="tpu_custom_call" | custom-call | flops 1073741824 | bytes 1048576 | tf_op jit(solution)/shard_map/pallas_call | solution.py:711
  60.8 14.4 %all_to_all.11 = f32[128,2,128]{2,1,0:T(2,128)S(1)} all-to-all(f32[128,2,128]{2,1,0:T(2,128)S(1)} %bitcast.15), channel_id=1, replica_groups=mesh['grp'=4,'gy'=32] {'grp','gy'}, dimensions={0} | all-to-all | bytes 262144 | tf_op jit(solution)/shard_map/all_to_all | solution.py:729
  75.2 9.3 %shard_map.99 = (f32[20,32,128]{2,1,0:T(8,128)}, f32[20,32,128]{2,1,0:T(8,128)}, f32[20,32,128]{2,1,0:T(8,128)}) custom-call(f32[32,32,128]{2,1,0:T(8,128)S(1)} %pad_maximum_fusion.planes, f32[128,128]{1,0:T(8,128)S(1)} %bitcast.13, f32[256,128]{1,0:T(8,128)S(1)} %bitcast.14, f32[2048,128]{1,0:T(8,128)S(1)} %get-tuple-element.43.cap_w.cap, ...), custom_call_target="tpu_custom_call" | custom-call | flops 1073741824 | bytes 1048576 | tf_op jit(solution)/shard_map/pallas_call | solution.py:711
  (1 shorter events, 0.0 us)
Async XLA Ops:
  0.6 0.9 %copy-start.3 = (f32[4,32,128]{2,1,0:T(8,128)S(1)}, f32[4,32,128]{2,1,0:T(8,128)}, u32[]{:S(2)}) copy-start(f32[4,32,128]{2,1,0:T(8,128)} %param.9) | copy-start | bytes 196612
  0.6 0.9 %copy-start.4 = (f32[4,32,128]{2,1,0:T(8,128)S(1)}, f32[4,32,128]{2,1,0:T(8,128)}, u32[]{:S(2)}) copy-start(f32[4,32,128]{2,1,0:T(8,128)} %param.8) | copy-start | bytes 196612
  2.6 4.1 %copy-start = (f32[4,5,5]{2,0,1:T(4,128)S(1)}, f32[4,5,5]{2,0,1:T(4,128)}, u32[]{:S(2)}) copy-start(f32[4,5,5]{2,0,1:T(4,128)} %param.13) | copy-start | bytes 1204
  2.9 6.2 %collective-permute-start = (f32[4,32,128]{2,1,0:T(8,128)S(1)}, f32[4,32,128]{2,1,0:T(8,128)S(1)}, u32[]{:S(2)}, u32[]{:S(2)}) collective-permute-start(f32[4,32,128]{2,1,0:T(8,128)S(1)} %get-tuple-element.32), channel_id=1, source_target_pairs={{0,32},{32,64},{64,96},{96,0},{1,33},{33,65},{65,97},{97,1},{2,34}... | collective-permute-start | bytes 196616 | tf_op jit(solution)/shard_map/ppermute | solution.py:741
  5.1 1.5 %copy-start.1 = (f32[5,4]{0,1:T(4,128)S(1)}, f32[5,4]{0,1:T(4,128)}, u32[]{:S(2)}) copy-start(f32[5,4]{0,1:T(4,128)} %param.10) | copy-start | bytes 244
  5.1 4.0 %collective-permute-start.1 = (f32[4,32,128]{2,1,0:T(8,128)S(1)}, f32[4,32,128]{2,1,0:T(8,128)S(1)}, u32[]{:S(2)}, u32[]{:S(2)}) collective-permute-start(f32[4,32,128]{2,1,0:T(8,128)S(1)} %get-tuple-element.33), channel_id=1, source_target_pairs={{32,0},{64,32},{96,64},{0,96},{33,1},{65,33},{97,65},{1,97},{34,2}... | collective-permute-start | bytes 196616 | tf_op jit(solution)/shard_map/ppermute | solution.py:741
  6.6 0.7 copy-start.2
  9.2 21.9 %collective-permute-start.2 = (f32[40,16,128]{2,1,0:T(8,128)S(1)}, f32[40,16,128]{2,1,0:T(8,128)S(1)}, u32[]{:S(2)}, u32[]{:S(2)}) collective-permute-start(f32[40,16,128]{2,1,0:T(8,128)S(1)} %get-tuple-element.37), channel_id=1, source_target_pairs={{0,1},{1,2},{2,3},{3,4},{4,5},{5,6},{6,7},{7,8},{8,9},{9,10},{10,1... | collective-permute-start | bytes 983048 | tf_op jit(solution)/shard_map/ppermute | solution.py:758
  12.0 19.1 %collective-permute-start.3 = (f32[40,16,128]{2,1,0:T(8,128)S(1)}, f32[40,16,128]{2,1,0:T(8,128)S(1)}, u32[]{:S(2)}, u32[]{:S(2)}) collective-permute-start(f32[40,16,128]{2,1,0:T(8,128)S(1)} %get-tuple-element.38), channel_id=1, source_target_pairs={{1,0},{2,1},{3,2},{4,3},{5,4},{6,5},{7,6},{8,7},{9,8},{10,9},{11,1... | collective-permute-start | bytes 983048 | tf_op jit(solution)/shard_map/ppermute | solution.py:758

commit v5 on v4

--- a/solution.py
+++ b/solution.py
@@ -23,8 +23,7 @@
 BOTH = ("grp", "gy")
 
 HALO = 12
-PER = 10
-GROUPS = -(-PLANES // PER)
+GROUPS = LAYERS
 RHALO = 16
 TALL = ROWS + 2 * RHALO
 TOP = RHALO
@@ -52,8 +51,8 @@
     for g in range(GROUPS):
         low = jnp.zeros((ROWS, COLS), F32)
         high = jnp.zeros((ROWS, COLS), F32)
-        for j in range(min(PER, PLANES - g * PER)):
-            v = planes[g * PER + j]
+        for j in range(PLANES // LAYERS):
+            v = planes[j * LAYERS + g]
             inside = (lane >= HALO * j) & (lane < HALO * (j + 1))
             low = jnp.where(inside, turn(v, HALO * j), low)
             high = jnp.where(inside, turn(v, HALO * j + HALO), high)
@@ -179,16 +178,43 @@
 
 
 def at(l, y):
+    if isinstance(y, int):
+        return pl.ds((y + l * TALL) * 8, 8)
     return pl.ds(pl.multiple_of((y + l * TALL) * 8, 8), 8)
 
 
+class Later:
+    def __init__(self):
+        self.held = []
+
+    def put(self, ref, where, value):
+        self.held.append((ref, where, value))
+
+    def flush(self):
+        for ref, where, value in self.held:
+            ref[where, :] = value
+        self.held = []
+
+
+LATER = Later()
+BLOCK = 0
+
+
 def each_row(first, count, step, carry=()):
+    size = BLOCK if BLOCK and count % BLOCK == 0 else 4
+    if BLOCK == 0:
+        for r in range(count):
+            carry = step(first + r, carry)
+            LATER.flush()
+        return carry
+
     def block(i, carry):
-        for r in range(4):
-            carry = step(first + 4 * i + r, carry)
+        for r in range(size):
+            carry = step(first + size * i + r, carry)
+        LATER.flush()
         return carry
 
-    return lax.fori_loop(0, count // 4, block, carry)
+    return lax.fori_loop(0, count // size, block, carry)
 
 
 def stencil(src, ops, wide, emit, carry=()):
@@ -227,7 +253,7 @@
 
     def emit(l, y, u, out, carry):
         here = at(l, y)
-        dst[here, :] = u + scale[here, :] * (resid[here, :] - out)
+        LATER.put(dst, here, u + scale[here, :] * (resid[here, :] - out))
         return carry
 
     stencil(src, ops, wide, emit)
@@ -235,7 +261,7 @@
 
 def image(src, dst, ops, wide):
     def emit(l, y, u, out, carry):
-        dst[at(l, y), :] = out
+        LATER.put(dst, at(l, y), out)
         return carry
 
     stencil(src, ops, wide, emit)
@@ -245,7 +271,7 @@
     def step(y, carry):
         for l in range(LAYERS):
             here = at(l, y)
-            dst[here, :] = scale[here, :] * resid[here, :]
+            LATER.put(dst, here, scale[here, :] * resid[here, :])
         return carry
 
     each_row(TOP - wide, ROWS + 2 * wide, step)
@@ -403,25 +429,6 @@
     lane, sub = lanes((8, COLS)), subs((8, COLS))
     left = lane < HALF
 
-    def pick(strip, own, k, t):
-        if t < 2:
-            return y_low[strip, 8 * t : 8 * t + 8, :]
-        if t < 6:
-            return own[k, 8 * (t - 2) : 8 * (t - 2) + 8, :]
-        return y_high[strip, 8 * (t - 6) : 8 * (t - 6) + 8, :]
-
-    def both(k, t):
-        g, j = divmod(k, PER)
-        v = pick(k, planes, k, t)
-        low = pick(PLANES + g, x_low, g, t)
-        high = pick(PLANES + GROUPS + g, x_high, g, t)
-        early = jnp.where(lane < HALO, turn(low, -HALO * j), turn(v, HALO))
-        late = jnp.where(lane < COLS - LATE, turn(v, -LATE), turn(high, COLS - LATE - HALO * j))
-        return early, late
-
-    def put(dst, l, t, s, v):
-        dst[pl.ds((l * TALL + 8 * t) * 8 + s, 8, stride=8), :] = v
-
     pairs = ((0, 1), (2, 3), (4, 4))
     d_late = [
         [jnp.where(left, diff[m, a], diff[m, b]) for m in range(MATS)] for a, b in pairs
@@ -430,34 +437,62 @@
     def choose(v, is1, is2, is3):
         return jnp.where(is3, v[3], jnp.where(is2, v[2], jnp.where(is1, v[1], v[0])))
 
-    for l in range(LAYERS):
-        for t in range(TALL // 8):
-            late_b = []
-            for s in range(SPECIES):
-                early, late = both(s * LAYERS + l, t)
-                put(b_w, l, t, s, early)
-                late_b.append(late)
-            for i, (a, b) in enumerate(pairs):
-                put(b_w, l, t, SPECIES + i, jnp.where(left, late_b[a], turn(late_b[b], HALF)))
-            for dst, base in ((cap_w, CAP0), (mat_w, MAT0)):
-                early, late = both(base + l, t)
-                late = jnp.where(left, late, turn(late, HALF))
-                for s in range(8):
-                    put(dst, l, t, s, early if s < SPECIES else late)
-            m_early, m_late = early, late
-            early, late = both(POT0 + l, t)
+    def fill(own, low, high, l, row, y):
+        rows = pl.ds(row, 8)
+
+        def both(kind):
+            v = own[kind * LAYERS + l, rows, :]
+            early = jnp.where(lane < HALO, turn(low[l, rows, :], -HALO * kind), turn(v, HALO))
+            beyond = turn(high[l, rows, :], COLS - LATE - HALO * kind)
+            return early, jnp.where(lane < COLS - LATE, turn(v, -LATE), beyond)
+
+        def put(dst, s, v):
+            dst[pl.ds((y + l * TALL) * 8 + s, 8, stride=8), :] = v
+
+        late_b = []
+        for s in range(SPECIES):
+            early, late = both(s)
+            put(b_w, s, early)
+            late_b.append(late)
+        for i, (a, b) in enumerate(pairs):
+            put(b_w, SPECIES + i, jnp.where(left, late_b[a], turn(late_b[b], HALF)))
+        for dst, kind in ((cap_w, SPECIES + 1), (mat_w, SPECIES + 2)):
+            early, late = both(kind)
             late = jnp.where(left, late, turn(late, HALF))
-            is_m = [m_early == float(m) for m in (1, 2, 3)]
-            down, up = jnp.exp(-0.5 * early), jnp.exp(0.5 * early)
-            drift = (down, up, down * down, up * up, down)
-            for s in range(SPECIES):
-                put(w, l, t, s, choose([diff[m, s] for m in range(MATS)], *is_m) * drift[s])
-            is_m = [m_late == float(m) for m in (1, 2, 3)]
-            down, up = jnp.exp(-0.5 * late), jnp.exp(0.5 * late)
-            mixed = jnp.where(left, down, up)
-            drift = (mixed, mixed * mixed, down)
-            for i in range(3):
-                put(w, l, t, SPECIES + i, choose(d_late[i], *is_m) * drift[i])
+            for s in range(8):
+                put(dst, s, early if s < SPECIES else late)
+        m_early, m_late = early, late
+        early, late = both(SPECIES)
+        late = jnp.where(left, late, turn(late, HALF))
+        is_m = [m_early == float(m) for m in (1, 2, 3)]
+        down, up = jnp.exp(-0.5 * early), jnp.exp(0.5 * early)
+        drift = (down, up, down * down, up * up, down)
+        for s in range(SPECIES):
+            put(w, s, choose([diff[m, s] for m in range(MATS)], *is_m) * drift[s])
+        is_m = [m_late == float(m) for m in (1, 2, 3)]
+        down, up = jnp.exp(-0.5 * late), jnp.exp(0.5 * late)
+        mixed = jnp.where(left, down, up)
+        drift = (mixed, mixed * mixed, down)
+        for i in range(3):
+            put(w, SPECIES + i, choose(d_late[i], *is_m) * drift[i])
+
+    edge_low = (y_low.at[PLANES : PLANES + GROUPS], y_low.at[PLANES + GROUPS : PLANES + 2 * GROUPS])
+    edge_high = (y_high.at[PLANES : PLANES + GROUPS], y_high.at[PLANES + GROUPS : PLANES + 2 * GROUPS])
+
+    @pl.loop(0, LAYERS)
+    def _(l):
+        for row in range(0, RHALO, 8):
+            fill(y_low, *edge_low, l, row, row)
+
+    @pl.loop(0, LAYERS)
+    def _(l):
+        for row in range(0, ROWS, 8):
+            fill(planes, x_low, x_high, l, row, TOP + row)
+
+    @pl.loop(0, LAYERS)
+    def _(l):
+        for row in range(0, RHALO, 8):
+            fill(y_high, *edge_high, l, row, TOP + ROWS + row)
 
     me_x = lax.axis_index("grp")
     closed = ((sub >= SPECIES) & ((lane & (HALF - 1)) == COLS - 1 - LATE) & (me_x == N_GRP - 1)) | (
@@ -476,16 +511,16 @@
             above = w[at(l, y + 1), :]
             ey = harmonic(c, above)
             ex = jnp.where(closed, 0.0, harmonic(c, turn(c, -1)))
-            gy[here, :] = ey
-            gx[here, :] = ex
+            LATER.put(gy, here, ey)
+            LATER.put(gx, here, ex)
             d = cap_w[here, :] + ey + edge_y[l] + ex + turn(ex, 1)
             if ez_below is not None:
                 d = d + ez_below
             if l + 1 < LAYERS:
                 ez_below = 0.5 * harmonic(c, now[l + 1])
-                gz[here, :] = ez_below
+                LATER.put(gz, here, ez_below)
                 d = d + ez_below
-            scale[here, :] = DAMPING / d
+            LATER.put(scale, here, DAMPING / d)
             nxt.append(above)
             out_y.append(ey)
         return nxt, out_y
@@ -547,7 +582,7 @@
     spread_values(exact_dot(sol, near_hot[...]), values)
 
     def add_coarse(l, y, c):
-        z0[at(l, y), :] = y0[at(l, y), :] + c
+        LATER.put(z0, at(l, y), y0[at(l, y), :] + c)
 
     coarse_rows(values, mat_w, 8, add_coarse)
     image(z0, w0, ops, 8)
@@ -658,7 +693,7 @@
     ops = (cap, gy, gx, gz, scale)
 
     def add_coarse(l, y, c):
-        v1[at(l, y), :] = u[at(l, y), :] + c
+        LATER.put(v1, at(l, y), u[at(l, y), :] + c)
 
     coarse_rows(values, mat, 4, add_coarse)
     image(v1, w1, ops, 4)
@@ -672,9 +707,9 @@
         w1v, v1v = w1[here, :], v1[here, :]
         z0v, w0v = z0[here, :], w0[here, :]
         v2 = z + scale[here, :] * (w1v - out) + coarse_pick(own_values, mat[here, :])
-        px[here, :] = ca * z0v - cb * v1v
-        pr[here, :] = ca * w0v - cb * w1v
-        pz[here, :] = z0v - ca * v1v + cb * v2
+        LATER.put(px, here, ca * z0v - cb * v1v)
+        LATER.put(pr, here, ca * w0v - cb * w1v)
+        LATER.put(pz, here, z0v - ca * v1v + cb * v2)
         return carry
 
     stencil(za, ops, 0, emit)

time: 84.8 us -> 61.9 us (0.73)
  Pallas kernels: 41.2 us -> 18.3 us
    pallas_call x6, Pallas kernels: 41.2 us -> 18.3 us  [run(): pl.pallas_call(kernel, out_shape=outs, in_specs=in_specs, out_specs=jax.t...]
  transfers between devices with their start and end apart: 4 -> 4, of which waited for: 0 -> 0; matrix products, arithmetic and copies ran while one was open for 0% -> 0% of each run, Pallas kernels for 2% -> 3%
where the time goes in v5:
time: 61.9 us; the launch traced here: 61.6 us
  blocking collectives  33.5 us (54%)
  Pallas kernels  18.3 us (30%)
  starting transfers between devices  6.48 us (10%)
  other arithmetic  1.89 us (3%)
  between operations  0.72 us (1%)
  local copies, waits for them, and re-layouts  0.67 us (1%)
    all_to_all x2, blocking collectives, to_all(): got = lax.all_to_all(rows.reshape(TOTAL, -1, COLS), BOTH, 0, 0, tiled=True)  33.5 us
    pallas_call x6, Pallas kernels, run(): pl.pallas_call(kernel, out_shape=outs, in_specs=in_specs, out_specs=jax.t...  18.3 us
    ppermute x2, starting transfers between devices, body(): x_low, x_high = (right(to_high), left(to_low))  3.72 us
    ppermute x2, starting transfers between devices, body(): y_low, y_high = (down(to_high), up(to_low))  2.75 us
  transfers between devices with their start and end apart: 4, of which 0 were waited for; matrix products, arithmetic and copies ran while one was open for 0% of the time, Pallas kernels for 3%

profile of v5, /device:TPU:1, one launch (start us, length us, event | category | flops | bytes accessed | tf_op | source)
XLA Modules:
  0.0 61.6 jit_solution(18111237865268748887)
XLA Ops:
  0.6 0.0 copy-start.3
  0.6 0.0 copy-start.4
  0.7 0.9 %convert_element_type.3 = f32[4,32,128]{2,1,0:T(8,128)S(1)} convert(s32[4,32,128]{2,1,0:T(8,128)} %param.11) | non-fusion elementwise | flops 16384 | bytes 131072 | tf_op jit(solution)/shard_map/convert_element_type | solution.py:773
  1.5 0.0 copy-done.3
  1.5 0.0 copy-done.4
  1.5 1.0 %pad_maximum_fusion.planes = f32[32,32,128]{2,1,0:T(8,128)S(1)} fusion(f32[4,32,128]{2,1,0:T(8,128)S(1)} %convert_element_type.3, f32[4,32,128]{2,1,0:T(8,128)S(1)} %copy-done.3, f32[4,32,128]{2,1,0:T(8,128)S(1)} %copy-done.4, f32[20,32,128]{2,1,0:T(8,128)} %bitcast.20), kind=kLoop, calls=%fused_computation | loop fusion | flops 393216 | bytes 1048576 | tf_op jit(solution)/shard_map/concatenate | solution.py:773
  2.6 0.0 copy-start
  2.6 0.3 shard_map.95
  2.9 2.2 %collective-permute-start = (f32[4,32,128]{2,1,0:T(8,128)S(1)}, f32[4,32,128]{2,1,0:T(8,128)S(1)}, u32[]{:S(2)}, u32[]{:S(2)}) collective-permute-start(f32[4,32,128]{2,1,0:T(8,128)S(1)} %get-tuple-element.32), channel_id=1, source_target_pairs={{0,32},{32,64},{64,96},{96,0},{1,33},{33,65},{65,97},{97,1},{2,34}... | collective-permute-start | bytes 196616 | tf_op jit(solution)/shard_map/ppermute | solution.py:776
  5.1 0.0 copy-start.1
  5.1 1.5 %collective-permute-start.1 = (f32[4,32,128]{2,1,0:T(8,128)S(1)}, f32[4,32,128]{2,1,0:T(8,128)S(1)}, u32[]{:S(2)}, u32[]{:S(2)}) collective-permute-start(f32[4,32,128]{2,1,0:T(8,128)S(1)} %get-tuple-element.33), channel_id=1, source_target_pairs={{32,0},{64,32},{96,64},{0,96},{33,1},{65,33},{97,65},{1,97},{34,2}... | collective-permute-start | bytes 196616 | tf_op jit(solution)/shard_map/ppermute | solution.py:776
  6.6 0.0 copy-start.2
  6.6 0.0 copy-done
  6.6 0.0 copy-done.1
  6.6 0.6 %copy-done.2 = s32[1,1,4]{2,1,0:T(1,128)S(1)} copy-done((s32[1,1,4]{2,1,0:T(1,128)S(1)}, s32[1,1,4]{2,1,0:T(1,128)}, u32[]{:S(2)}) %copy-start.2) | copy-done | bytes 40
  7.3 1.8 %shard_map.94 = (f32[128,128]{1,0:T(8,128)S(1)}, f32[256,128]{1,0:T(8,128)S(1)}) custom-call(f32[4,5]{1,0:T(4,128)S(1)} %bitcast.18, f32[32,32,128]{2,1,0:T(8,128)S(1)} %pad_maximum_fusion.planes, s32[1,1,4]{2,1,0:T(1,128)S(1)} %copy-done.2, f32[5,4,5]{2,1,0:T(4,128)S(1)} %bitcast.17), custom_call_target="tpu_custom_call" | custom-call | flops 1048576 | bytes 1048576 | tf_op jit(solution)/shard_map/pallas_call | solution.py:746
  9.1 0.0 collective-permute-done.from_low.x_low
  9.1 0.0 collective-permute-done.1.from_high.x_high
  9.2 2.7 %collective-permute-start.2 = (f32[40,16,128]{2,1,0:T(8,128)S(1)}, f32[40,16,128]{2,1,0:T(8,128)S(1)}, u32[]{:S(2)}, u32[]{:S(2)}) collective-permute-start(f32[40,16,128]{2,1,0:T(8,128)S(1)} %get-tuple-element.37), channel_id=1, source_target_pairs={{0,1},{1,2},{2,3},{3,4},{4,5},{5,6},{6,7},{7,8},{8,9},{9,10},{10,1... | collective-permute-start | bytes 983048 | tf_op jit(solution)/shard_map/ppermute | solution.py:793
  12.0 0.0 collective-permute-start.3
  12.0 19.1 %all_to_all.10 = f32[128,1,128]{2,1,0:T(1,128)S(1)} all-to-all(f32[128,1,128]{2,1,0:T(1,128)S(1)} %bitcast.16), channel_id=1, replica_groups=mesh['grp'=4,'gy'=32] {'grp','gy'}, dimensions={0} | all-to-all | bytes 131072 | tf_op jit(solution)/shard_map/all_to_all | solution.py:764
  31.1 0.0 collective-permute-done.2.y_low
  31.1 0.0 collective-permute-done.3.y_high
  31.1 7.1 %shard_map.97 = (f32[2048,128]{1,0:T(8,128)S(1)}, f32[2048,128]{1,0:T(8,128)S(1)}, f32[2048,128]{1,0:T(8,128)S(1)}, f32[2048,128]{1,0:T(8,128)S(1)}, f32[2048,12...) custom-call(f32[4,5]{1,0:T(4,128)S(1)} %bitcast.19, ...), custom_call_target="tpu_custom_call" | custom-call | flops 1073741824 | bytes 1048576 | tf_op jit(solution)/shard_map/pallas_call | solution.py:746
  38.2 4.2 %shard_map.98 = (f32[256,128]{1,0:T(8,128)S(1)}, f32[2048,128]{1,0:T(8,128)S(1)}, f32[2048,128]{1,0:T(8,128)S(1)}, f32[2048,128]{1,0:T(8,128)S(1)}) custom-call(f32[32,32,128]{2,1,0:T(8,128)S(1)} %pad_maximum_fusion.planes, f32[128,128]{1,0:T(8,128)S(1)} %bitcast.12, f32[2048,128]{1,0:T(8,128)S(1)} %get-tuple-element.43.cap_w.cap, ...), custom_call_target="tpu_custom_call" | custom-call | flops 1073741824 | bytes 1048576 | tf_op jit(solution)/shard_map/pallas_call | solution.py:746
  42.4 14.4 %all_to_all.11 = f32[128,2,128]{2,1,0:T(2,128)S(1)} all-to-all(f32[128,2,128]{2,1,0:T(2,128)S(1)} %bitcast.15), channel_id=1, replica_groups=mesh['grp'=4,'gy'=32] {'grp','gy'}, dimensions={0} | all-to-all | bytes 262144 | tf_op jit(solution)/shard_map/all_to_all | solution.py:764
  56.8 4.8 %shard_map.99 = (f32[20,32,128]{2,1,0:T(8,128)}, f32[20,32,128]{2,1,0:T(8,128)}, f32[20,32,128]{2,1,0:T(8,128)}) custom-call(f32[32,32,128]{2,1,0:T(8,128)S(1)} %pad_maximum_fusion.planes, f32[128,128]{1,0:T(8,128)S(1)} %bitcast.13, f32[256,128]{1,0:T(8,128)S(1)} %bitcast.14, f32[2048,128]{1,0:T(8,128)S(1)} %get-tuple-element.43.cap_w.cap, ...), custom_call_target="tpu_custom_call" | custom-call | flops 1073741824 | bytes 1048576 | tf_op jit(solution)/shard_map/pallas_call | solution.py:746
  (1 shorter events, 0.0 us)
Async XLA Ops:
  0.6 0.9 %copy-start.3 = (f32[4,32,128]{2,1,0:T(8,128)S(1)}, f32[4,32,128]{2,1,0:T(8,128)}, u32[]{:S(2)}) copy-start(f32[4,32,128]{2,1,0:T(8,128)} %param.9) | copy-start | bytes 196612
  0.6 0.9 %copy-start.4 = (f32[4,32,128]{2,1,0:T(8,128)S(1)}, f32[4,32,128]{2,1,0:T(8,128)}, u32[]{:S(2)}) copy-start(f32[4,32,128]{2,1,0:T(8,128)} %param.8) | copy-start | bytes 196612
  2.6 4.1 %copy-start = (f32[4,5,5]{2,0,1:T(4,128)S(1)}, f32[4,5,5]{2,0,1:T(4,128)}, u32[]{:S(2)}) copy-start(f32[4,5,5]{2,0,1:T(4,128)} %param.13) | copy-start | bytes 1204
  2.9 6.2 %collective-permute-start = (f32[4,32,128]{2,1,0:T(8,128)S(1)}, f32[4,32,128]{2,1,0:T(8,128)S(1)}, u32[]{:S(2)}, u32[]{:S(2)}) collective-permute-start(f32[4,32,128]{2,1,0:T(8,128)S(1)} %get-tuple-element.32), channel_id=1, source_target_pairs={{0,32},{32,64},{64,96},{96,0},{1,33},{33,65},{65,97},{97,1},{2,34}... | collective-permute-start | bytes 196616 | tf_op jit(solution)/shard_map/ppermute | solution.py:776
  5.1 1.5 %copy-start.1 = (f32[5,4]{0,1:T(4,128)S(1)}, f32[5,4]{0,1:T(4,128)}, u32[]{:S(2)}) copy-start(f32[5,4]{0,1:T(4,128)} %param.10) | copy-start | bytes 244
  5.1 4.0 %collective-permute-start.1 = (f32[4,32,128]{2,1,0:T(8,128)S(1)}, f32[4,32,128]{2,1,0:T(8,128)S(1)}, u32[]{:S(2)}, u32[]{:S(2)}) collective-permute-start(f32[4,32,128]{2,1,0:T(8,128)S(1)} %get-tuple-element.33), channel_id=1, source_target_pairs={{32,0},{64,32},{96,64},{0,96},{33,1},{65,33},{97,65},{1,97},{34,2}... | collective-permute-start | bytes 196616 | tf_op jit(solution)/shard_map/ppermute | solution.py:776
  6.6 0.7 %copy-start.2 = (s32[1,1,4]{2,1,0:T(1,128)S(1)}, s32[1,1,4]{2,1,0:T(1,128)}, u32[]{:S(2)}) copy-start(s32[1,1,4]{2,1,0:T(1,128)} %cmap.1) | copy-start | bytes 52
  9.2 21.9 %collective-permute-start.2 = (f32[40,16,128]{2,1,0:T(8,128)S(1)}, f32[40,16,128]{2,1,0:T(8,128)S(1)}, u32[]{:S(2)}, u32[]{:S(2)}) collective-permute-start(f32[40,16,128]{2,1,0:T(8,128)S(1)} %get-tuple-element.37), channel_id=1, source_target_pairs={{0,1},{1,2},{2,3},{3,4},{4,5},{5,6},{6,7},{7,8},{8,9},{9,10},{10,1... | collective-permute-start | bytes 983048 | tf_op jit(solution)/shard_map/ppermute | solution.py:793
  12.0 19.1 %collective-permute-start.3 = (f32[40,16,128]{2,1,0:T(8,128)S(1)}, f32[40,16,128]{2,1,0:T(8,128)S(1)}, u32[]{:S(2)}, u32[]{:S(2)}) collective-permute-start(f32[40,16,128]{2,1,0:T(8,128)S(1)} %get-tuple-element.38), channel_id=1, source_target_pairs={{1,0},{2,1},{3,2},{4,3},{5,4},{6,5},{7,6},{8,7},{9,8},{10,9},{11,1... | collective-permute-start | bytes 983048 | tf_op jit(solution)/shard_map/ppermute | solution.py:793

commit v6 on v5

--- a/solution.py
+++ b/solution.py
@@ -46,7 +46,9 @@
     return lax.broadcasted_iota(jnp.int32, shape, 0)
 
 
-def pack_kernel(planes, to_low, to_high):
+def pack_kernel(fields, mat, planes, to_low, to_high):
+    planes[0:MAT0] = fields[...]
+    planes[MAT0:PLANES] = mat[...].astype(F32)
     lane = lanes((ROWS, COLS))
     for g in range(GROUPS):
         low = jnp.zeros((ROWS, COLS), F32)
@@ -770,9 +772,15 @@
     right, left = shifts("grp", N_GRP)
     down, up = shifts("gy", N_GY)
 
-    planes = jnp.concatenate([b, potential, capacity, material.astype(F32)])
     packed = shape(GROUPS, ROWS, COLS)
-    to_low, to_high = run(pack_kernel, (packed, packed), [], [VMEM], 1 << 20, planes)
+    planes, to_low, to_high = run(
+        pack_kernel,
+        (shape(PLANES, ROWS, COLS), packed, packed),
+        [],
+        [VMEM] * 2,
+        1 << 20,
+        jnp.concatenate([b, potential, capacity]), material,
+    )
     x_low, x_high = right(to_high), left(to_low)
     code = pltpu.VMEM((LAYERS, ROWS, COLS), F32)
     first, acc = run(

time: 61.9 us -> 61 us (0.985)
  other arithmetic: 1.89 us -> 1.11 us
    convert_element_type x1 -> x0, other arithmetic: 0.88 us -> none  [body(): planes = jnp.concatenate([b, potential, capacity, material.astype(F32)])]
where the time goes in v6:
time: 61 us; the launch traced here: 60.8 us
  blocking collectives  33.5 us (55%)
  Pallas kernels  18.3 us (30%)
  starting transfers between devices  6.45 us (11%)
  other arithmetic  1.11 us (2%)
  between operations  0.71 us (1%)
  local copies, waits for them, and re-layouts  0.69 us (1%)
    all_to_all x2, blocking collectives, to_all(): got = lax.all_to_all(rows.reshape(TOTAL, -1, COLS), BOTH, 0, 0, tiled=True)  33.5 us
    pallas_call x6, Pallas kernels, run(): pl.pallas_call(kernel, out_shape=outs, in_specs=in_specs, out_specs=jax.t...  18.3 us
    ppermute x2, starting transfers between devices, body(): x_low, x_high = (right(to_high), left(to_low))  3.71 us
    ppermute x2, starting transfers between devices, body(): y_low, y_high = (down(to_high), up(to_low))  2.73 us
  transfers between devices with their start and end apart: 4, of which 0 were waited for; matrix products, arithmetic and copies ran while one was open for 0% of the time, Pallas kernels for 3%

profile of v6, /device:TPU:1, one launch (start us, length us, event | category | flops | bytes accessed | tf_op | source)
XLA Modules:
  0.0 60.8 jit_solution(14557955125646153084)
XLA Ops:
  0.6 0.0 copy-start
  0.6 1.1 %pad_maximum_fusion.fields = f32[28,32,128]{2,1,0:T(8,128)S(1)} fusion(f32[4,32,128]{2,1,0:T(8,128)} %param.9, f32[4,32,128]{2,1,0:T(8,128)} %param.8, f32[20,32,128]{2,1,0:T(8,128)} %bitcast.20), kind=kLoop, calls=%fused_computation | loop fusion | flops 229376 | bytes 917504 | tf_op jit(solution)/shard_map/concatenate | solution.py:782
  1.8 0.0 copy-done
  1.8 0.0 copy-start.1
  1.8 0.3 shard_map.94
  2.1 2.2 %collective-permute-start = (f32[4,32,128]{2,1,0:T(8,128)S(1)}, f32[4,32,128]{2,1,0:T(8,128)S(1)}, u32[]{:S(2)}, u32[]{:S(2)}) collective-permute-start(f32[4,32,128]{2,1,0:T(8,128)S(1)} %get-tuple-element.34), channel_id=1, source_target_pairs={{0,32},{32,64},{64,96},{96,0},{1,33},{33,65},{65,97},{97,1},{2,34}... | collective-permute-start | bytes 196616 | tf_op jit(solution)/shard_map/ppermute | solution.py:784
  4.3 1.5 %collective-permute-start.1 = (f32[4,32,128]{2,1,0:T(8,128)S(1)}, f32[4,32,128]{2,1,0:T(8,128)S(1)}, u32[]{:S(2)}, u32[]{:S(2)}) collective-permute-start(f32[4,32,128]{2,1,0:T(8,128)S(1)} %get-tuple-element.35), channel_id=1, source_target_pairs={{32,0},{64,32},{96,64},{0,96},{33,1},{65,33},{97,65},{1,97},{34,2}... | collective-permute-start | bytes 196616 | tf_op jit(solution)/shard_map/ppermute | solution.py:784
  5.8 0.0 copy-start.2
  5.8 0.0 copy-start.3
  5.8 0.0 copy-done.1
  5.8 0.7 %copy-done.2 = f32[5,4]{0,1:T(4,128)S(1)} copy-done((f32[5,4]{0,1:T(4,128)S(1)}, f32[5,4]{0,1:T(4,128)}, u32[]{:S(2)}) %copy-start.2) | copy-done | bytes 104
  6.5 0.0 copy-done.3
  6.5 1.8 %shard_map.95 = (f32[128,128]{1,0:T(8,128)S(1)}, f32[256,128]{1,0:T(8,128)S(1)}) custom-call(f32[4,5]{1,0:T(4,128)S(1)} %bitcast.18, f32[32,32,128]{2,1,0:T(8,128)S(1)} %get-tuple-element.32.planes, s32[1,1,4]{2,1,0:T(1,128)S(1)} %copy-done.3, f32[5,4,5]{2,1,0:T(4,128)S(1)} %bitcast.17), custom_call_target="tpu_custom_call" | custom-call | flops 1048576 | bytes 1048576 | tf_op jit(solution)/shard_map/pallas_call | solution.py:748
  8.4 0.0 collective-permute-done.from_low.x_low
  8.4 0.0 collective-permute-done.1.from_high.x_high
  8.4 2.7 %collective-permute-start.2 = (f32[40,16,128]{2,1,0:T(8,128)S(1)}, f32[40,16,128]{2,1,0:T(8,128)S(1)}, u32[]{:S(2)}, u32[]{:S(2)}) collective-permute-start(f32[40,16,128]{2,1,0:T(8,128)S(1)} %get-tuple-element.39), channel_id=1, source_target_pairs={{0,1},{1,2},{2,3},{3,4},{4,5},{5,6},{6,7},{7,8},{8,9},{9,10},{10,1... | collective-permute-start | bytes 983048 | tf_op jit(solution)/shard_map/ppermute | solution.py:801
  11.2 0.0 collective-permute-start.3
  11.2 19.1 %all_to_all.10 = f32[128,1,128]{2,1,0:T(1,128)S(1)} all-to-all(f32[128,1,128]{2,1,0:T(1,128)S(1)} %bitcast.16), channel_id=1, replica_groups=mesh['grp'=4,'gy'=32] {'grp','gy'}, dimensions={0} | all-to-all | bytes 131072 | tf_op jit(solution)/shard_map/all_to_all | solution.py:766
  30.3 0.0 collective-permute-done.2.y_low
  30.3 0.0 collective-permute-done.3.y_high
  30.3 7.1 %shard_map.97 = (f32[2048,128]{1,0:T(8,128)S(1)}, f32[2048,128]{1,0:T(8,128)S(1)}, f32[2048,128]{1,0:T(8,128)S(1)}, f32[2048,128]{1,0:T(8,128)S(1)}, f32[2048,12...) custom-call(f32[4,5]{1,0:T(4,128)S(1)} %bitcast.19, ...), custom_call_target="tpu_custom_call" | custom-call | flops 1073741824 | bytes 1048576 | tf_op jit(solution)/shard_map/pallas_call | solution.py:748
  37.4 4.2 %shard_map.98 = (f32[256,128]{1,0:T(8,128)S(1)}, f32[2048,128]{1,0:T(8,128)S(1)}, f32[2048,128]{1,0:T(8,128)S(1)}, f32[2048,128]{1,0:T(8,128)S(1)}) custom-call(f32[32,32,128]{2,1,0:T(8,128)S(1)} %get-tuple-element.32.planes, f32[128,128]{1,0:T(8,128)S(1)} %bitcast.12, f32[2048,128]{1,0:T(8,128)S(1)} %get-tuple-element.45.cap_w.cap, ...), custom_call_target="tpu_custom_call" | custom-call | flops 1073741824 | bytes 1048576 | tf_op jit(solution)/shard_map/pallas_call | solution.py:748
  41.6 14.4 %all_to_all.11 = f32[128,2,128]{2,1,0:T(2,128)S(1)} all-to-all(f32[128,2,128]{2,1,0:T(2,128)S(1)} %bitcast.15), channel_id=1, replica_groups=mesh['grp'=4,'gy'=32] {'grp','gy'}, dimensions={0} | all-to-all | bytes 262144 | tf_op jit(solution)/shard_map/all_to_all | solution.py:766
  56.0 4.8 %shard_map.99 = (f32[20,32,128]{2,1,0:T(8,128)}, f32[20,32,128]{2,1,0:T(8,128)}, f32[20,32,128]{2,1,0:T(8,128)}) custom-call(f32[32,32,128]{2,1,0:T(8,128)S(1)} %get-tuple-element.32.planes, f32[128,128]{1,0:T(8,128)S(1)} %bitcast.13, f32[256,128]{1,0:T(8,128)S(1)} %bitcast.14, f32[2048,128]{1,0:T(8,128)S(1)} %get-tuple-element.45.cap_w.cap, ...), custom_call_target="tpu_custom_call" | custom-call | flops 1073741824 | bytes 1048576 | tf_op jit(solution)/shard_map/pallas_call | solution.py:748
  (1 shorter events, 0.0 us)
Async XLA Ops:
  0.6 1.1 %copy-start = (s32[4,32,128]{2,1,0:T(8,128)S(1)}, s32[4,32,128]{2,1,0:T(8,128)}, u32[]{:S(2)}) copy-start(s32[4,32,128]{2,1,0:T(8,128)} %mat.1) | copy-start | bytes 196612
  1.8 4.1 %copy-start.1 = (f32[4,5,5]{2,0,1:T(4,128)S(1)}, f32[4,5,5]{2,0,1:T(4,128)}, u32[]{:S(2)}) copy-start(f32[4,5,5]{2,0,1:T(4,128)} %param.13) | copy-start | bytes 1204
  2.1 6.3 %collective-permute-start = (f32[4,32,128]{2,1,0:T(8,128)S(1)}, f32[4,32,128]{2,1,0:T(8,128)S(1)}, u32[]{:S(2)}, u32[]{:S(2)}) collective-permute-start(f32[4,32,128]{2,1,0:T(8,128)S(1)} %get-tuple-element.34), channel_id=1, source_target_pairs={{0,32},{32,64},{64,96},{96,0},{1,33},{33,65},{65,97},{97,1},{2,34}... | collective-permute-start | bytes 196616 | tf_op jit(solution)/shard_map/ppermute | solution.py:784
  4.3 4.1 %collective-permute-start.1 = (f32[4,32,128]{2,1,0:T(8,128)S(1)}, f32[4,32,128]{2,1,0:T(8,128)S(1)}, u32[]{:S(2)}, u32[]{:S(2)}) collective-permute-start(f32[4,32,128]{2,1,0:T(8,128)S(1)} %get-tuple-element.35), channel_id=1, source_target_pairs={{32,0},{64,32},{96,64},{0,96},{33,1},{65,33},{97,65},{1,97},{34,2}... | collective-permute-start | bytes 196616 | tf_op jit(solution)/shard_map/ppermute | solution.py:784
  5.8 0.7 %copy-start.2 = (f32[5,4]{0,1:T(4,128)S(1)}, f32[5,4]{0,1:T(4,128)}, u32[]{:S(2)}) copy-start(f32[5,4]{0,1:T(4,128)} %param.10) | copy-start | bytes 244
  5.8 0.7 %copy-start.3 = (s32[1,1,4]{2,1,0:T(1,128)S(1)}, s32[1,1,4]{2,1,0:T(1,128)}, u32[]{:S(2)}) copy-start(s32[1,1,4]{2,1,0:T(1,128)} %cmap.1) | copy-start | bytes 52
  8.4 21.9 %collective-permute-start.2 = (f32[40,16,128]{2,1,0:T(8,128)S(1)}, f32[40,16,128]{2,1,0:T(8,128)S(1)}, u32[]{:S(2)}, u32[]{:S(2)}) collective-permute-start(f32[40,16,128]{2,1,0:T(8,128)S(1)} %get-tuple-element.39), channel_id=1, source_target_pairs={{0,1},{1,2},{2,3},{3,4},{4,5},{5,6},{6,7},{7,8},{8,9},{9,10},{10,1... | collective-permute-start | bytes 983048 | tf_op jit(solution)/shard_map/ppermute | solution.py:801
  11.2 19.1 %collective-permute-start.3 = (f32[40,16,128]{2,1,0:T(8,128)S(1)}, f32[40,16,128]{2,1,0:T(8,128)S(1)}, u32[]{:S(2)}, u32[]{:S(2)}) collective-permute-start(f32[40,16,128]{2,1,0:T(8,128)S(1)} %get-tuple-element.40), channel_id=1, source_target_pairs={{1,0},{2,1},{3,2},{4,3},{5,4},{6,5},{7,6},{8,7},{9,8},{10,9},{11,1... | collective-permute-start | bytes 983048 | tf_op jit(solution)/shard_map/ppermute | solution.py:801

commit v7 on v6

--- a/solution.py
+++ b/solution.py
@@ -572,8 +572,8 @@
 
 def first_kernel(
     planes, got, cap_w, mat_w, gy, gx, gz, scale, y0, acc_in, b_w,
-    second, z0, w0, u_out,
-    za, zb, scatter, near_hot, turned, values, acc,
+    second, z0, w0, u_out, scatter, near_hot, turned,
+    za, zb, values, acc,
 ):
     ops = (cap_w, gy, gx, gz, scale)
 
@@ -631,16 +631,13 @@
 
 
 def second_kernel(
-    planes, got, got2, cap, mat, gy, gx, gz, scale, z0, w0, u,
+    planes, scatter, near_hot, turned, got2, cap, mat, gy, gx, gz, scale, z0, w0, u,
     out_x, out_r, out_z,
-    v1, w1, za, zb, px, pr, pz, scatter, gather, near_hot, turned, turned2, values, values2,
+    v1, w1, za, zb, px, pr, pz, gather, turned2, values, values2,
 ):
-    turned[...] = got[...].T
     turned2[0:COLS, :] = got2[pl.ds(0, TOTAL, stride=2), :].T
     turned2[COLS : 2 * COLS, :] = got2[pl.ds(1, TOTAL, stride=2), :].T
-    build_scatter(got, scatter)
     build_gather(turned, gather)
-    build_near(got, near_hot)
 
     sums_w = local_sums(turned2, G_RW)
     sol = coarse_solve(sums_w, turned, scatter)
@@ -805,8 +802,6 @@
     field = shape(FIELDS, ROWS, COLS)
     big = pltpu.VMEM(packed.shape, F32)
     hot = pltpu.VMEM((NC, MATS * TOTAL), jnp.bfloat16)
-    near = pltpu.VMEM((NC, COLS), jnp.bfloat16)
-    square = pltpu.VMEM((COLS, COLS), F32)
     double = pltpu.VMEM((2 * COLS, COLS), F32)
     values = pltpu.VMEM((3 * MATS * 8, COLS), F32)
     cap_w, mat_w, gy, gx, gz, scale, y0, acc, b_w = run(
@@ -817,10 +812,12 @@
         1 << 30,
         diffusivity.T, planes, x_low, x_high, y_low, y_high, acc,
     )
-    second, z0, w0, u = run(
+    hot_shape = jax.ShapeDtypeStruct((NC, MATS * TOTAL), jnp.bfloat16)
+    near_shape = jax.ShapeDtypeStruct((NC, COLS), jnp.bfloat16)
+    second, z0, w0, u, scatter, near_hot, turned = run(
         first_kernel,
-        (shape(2 * TOTAL, COLS), packed, packed, packed),
-        [big] * 2 + [hot, near, square, values, double],
+        (shape(2 * TOTAL, COLS), packed, packed, packed, hot_shape, near_shape, shape(COLS, COLS)),
+        [big] * 2 + [values, double],
         [VMEM] * 11,
         1 << 30,
         planes, got, cap_w, mat_w, gy, gx, gz, scale, y0, acc, b_w,
@@ -829,10 +826,10 @@
     out = run(
         second_kernel,
         (field, field, field),
-        [big] * 7 + [hot, hot, near, square, double, values, values],
-        [VMEM] * 12,
+        [big] * 7 + [hot, double, values, values],
+        [VMEM] * 14,
         1 << 30,
-        planes, got, got2, cap_w, mat_w, gy, gx, gz, scale, z0, w0, u,
+        planes, scatter, near_hot, turned, got2, cap_w, mat_w, gy, gx, gz, scale, z0, w0, u,
     )
     return tuple(o.reshape(right_side.shape) for o in out)
 

time: 61 us -> 61 us (level)
  no operation moved by 1% of the time
where the time goes in v7:
time: 61 us; the launch traced here: 60.8 us
  blocking collectives  33.5 us (55%)
  Pallas kernels  18.4 us (30%)
  starting transfers between devices  6.45 us (11%)
  other arithmetic  1.11 us (2%)
  between operations  0.71 us (1%)
  local copies, waits for them, and re-layouts  0.69 us (1%)
    all_to_all x2, blocking collectives, to_all(): got = lax.all_to_all(rows.reshape(TOTAL, -1, COLS), BOTH, 0, 0, tiled=True)  33.5 us
    pallas_call x6, Pallas kernels, run(): pl.pallas_call(kernel, out_shape=outs, in_specs=in_specs, out_specs=jax.t...  18.4 us
    ppermute x2, starting transfers between devices, body(): x_low, x_high = (right(to_high), left(to_low))  3.71 us
    ppermute x2, starting transfers between devices, body(): y_low, y_high = (down(to_high), up(to_low))  2.73 us
  transfers between devices with their start and end apart: 4, of which 0 were waited for; matrix products, arithmetic and copies ran while one was open for 0% of the time, Pallas kernels for 3%

profile of v7, /device:TPU:1, one launch (start us, length us, event | category | flops | bytes accessed | tf_op | source)
XLA Modules:
  0.0 60.8 jit_solution(3139120807354093519)
XLA Ops:
  0.6 0.0 copy-start
  0.6 1.1 %pad_maximum_fusion.fields = f32[28,32,128]{2,1,0:T(8,128)S(1)} fusion(f32[4,32,128]{2,1,0:T(8,128)} %param.9, f32[4,32,128]{2,1,0:T(8,128)} %param.8, f32[20,32,128]{2,1,0:T(8,128)} %bitcast.19), kind=kLoop, calls=%fused_computation | loop fusion | flops 229376 | bytes 917504 | tf_op jit(solution)/shard_map/concatenate | solution.py:779
  1.8 0.0 copy-done
  1.8 0.0 copy-start.1
  1.8 0.3 shard_map.94
  2.1 2.2 %collective-permute-start = (f32[4,32,128]{2,1,0:T(8,128)S(1)}, f32[4,32,128]{2,1,0:T(8,128)S(1)}, u32[]{:S(2)}, u32[]{:S(2)}) collective-permute-start(f32[4,32,128]{2,1,0:T(8,128)S(1)} %get-tuple-element.37), channel_id=1, source_target_pairs={{0,32},{32,64},{64,96},{96,0},{1,33},{33,65},{65,97},{97,1},{2,34}... | collective-permute-start | bytes 196616 | tf_op jit(solution)/shard_map/ppermute | solution.py:781
  4.3 1.5 %collective-permute-start.1 = (f32[4,32,128]{2,1,0:T(8,128)S(1)}, f32[4,32,128]{2,1,0:T(8,128)S(1)}, u32[]{:S(2)}, u32[]{:S(2)}) collective-permute-start(f32[4,32,128]{2,1,0:T(8,128)S(1)} %get-tuple-element.38), channel_id=1, source_target_pairs={{32,0},{64,32},{96,64},{0,96},{33,1},{65,33},{97,65},{1,97},{34,2}... | collective-permute-start | bytes 196616 | tf_op jit(solution)/shard_map/ppermute | solution.py:781
  5.8 0.0 copy-start.2
  5.8 0.0 copy-start.3
  5.8 0.0 copy-done.1
  5.8 0.7 %copy-done.2 = f32[5,4]{0,1:T(4,128)S(1)} copy-done((f32[5,4]{0,1:T(4,128)S(1)}, f32[5,4]{0,1:T(4,128)}, u32[]{:S(2)}) %copy-start.2) | copy-done | bytes 104
  6.5 0.0 copy-done.3
  6.5 1.8 %shard_map.95 = (f32[128,128]{1,0:T(8,128)S(1)}, f32[256,128]{1,0:T(8,128)S(1)}) custom-call(f32[4,5]{1,0:T(4,128)S(1)} %bitcast.17, f32[32,32,128]{2,1,0:T(8,128)S(1)} %get-tuple-element.35.planes, s32[1,1,4]{2,1,0:T(1,128)S(1)} %copy-done.3, f32[5,4,5]{2,1,0:T(4,128)S(1)} %bitcast.16), custom_call_target="tpu_custom_call" | custom-call | flops 1048576 | bytes 1048576 | tf_op jit(solution)/shard_map/pallas_call | solution.py:745
  8.4 0.0 collective-permute-done.from_low.x_low
  8.4 0.0 collective-permute-done.1.from_high.x_high
  8.4 2.7 %collective-permute-start.2 = (f32[40,16,128]{2,1,0:T(8,128)S(1)}, f32[40,16,128]{2,1,0:T(8,128)S(1)}, u32[]{:S(2)}, u32[]{:S(2)}) collective-permute-start(f32[40,16,128]{2,1,0:T(8,128)S(1)} %get-tuple-element.42), channel_id=1, source_target_pairs={{0,1},{1,2},{2,3},{3,4},{4,5},{5,6},{6,7},{7,8},{8,9},{9,10},{10,1... | collective-permute-start | bytes 983048 | tf_op jit(solution)/shard_map/ppermute | solution.py:798
  11.2 0.0 collective-permute-start.3
  11.2 19.1 %all_to_all.10 = f32[128,1,128]{2,1,0:T(1,128)S(1)} all-to-all(f32[128,1,128]{2,1,0:T(1,128)S(1)} %bitcast.15), channel_id=1, replica_groups=mesh['grp'=4,'gy'=32] {'grp','gy'}, dimensions={0} | all-to-all | bytes 131072 | tf_op jit(solution)/shard_map/all_to_all | solution.py:763
  30.3 0.0 collective-permute-done.2.y_low
  30.3 0.0 collective-permute-done.3.y_high
  30.3 7.2 %shard_map.97 = (f32[2048,128]{1,0:T(8,128)S(1)}, f32[2048,128]{1,0:T(8,128)S(1)}, f32[2048,128]{1,0:T(8,128)S(1)}, f32[2048,128]{1,0:T(8,128)S(1)}, f32[2048,12...) custom-call(f32[4,5]{1,0:T(4,128)S(1)} %bitcast.18, ...), custom_call_target="tpu_custom_call" | custom-call | flops 1073741824 | bytes 1048576 | tf_op jit(solution)/shard_map/pallas_call | solution.py:745
  37.5 4.2 %shard_map.98 = (f32[256,128]{1,0:T(8,128)S(1)}, f32[2048,128]{1,0:T(8,128)S(1)}, f32[2048,128]{1,0:T(8,128)S(1)}, f32[2048,128]{1,0:T(8,128)S(1)}, bf16[512,512...) custom-call(f32[32,32,128]{2,1,0:T(8,128)S(1)} %get-tuple-element.35.planes, ...), custom_call_target="tpu_custom_call" | custom-call | flops 1073741824 | bytes 1048576 | tf_op jit(solution)/shard_map/pallas_call | solution.py:745
  41.7 14.4 %all_to_all.11 = f32[128,2,128]{2,1,0:T(2,128)S(1)} all-to-all(f32[128,2,128]{2,1,0:T(2,128)S(1)} %bitcast.14), channel_id=1, replica_groups=mesh['grp'=4,'gy'=32] {'grp','gy'}, dimensions={0} | all-to-all | bytes 262144 | tf_op jit(solution)/shard_map/all_to_all | solution.py:763
  56.1 4.8 %shard_map.99 = (f32[20,32,128]{2,1,0:T(8,128)}, f32[20,32,128]{2,1,0:T(8,128)}, f32[20,32,128]{2,1,0:T(8,128)}) custom-call(f32[32,32,128]{2,1,0:T(8,128)S(1)} %get-tuple-element.35.planes, bf16[512,512]{1,0:T(8,128)(2,1)S(1)} %get-tuple-element.57.scatter, bf16[512,128]{1,0:T(8,128)(2,1)S(1)} %get-tuple-element.58.near_hot, ...), custom_call_target="tpu_custom_call" | custom-call | flops 1073741824 | bytes 1048576 | tf_op jit(solution)/shard_map/pallas_call | solution.py:745
  (1 shorter events, 0.0 us)
Async XLA Ops:
  0.6 1.1 %copy-start = (s32[4,32,128]{2,1,0:T(8,128)S(1)}, s32[4,32,128]{2,1,0:T(8,128)}, u32[]{:S(2)}) copy-start(s32[4,32,128]{2,1,0:T(8,128)} %mat.1) | copy-start | bytes 196612
  1.8 4.1 %copy-start.1 = (f32[4,5,5]{2,0,1:T(4,128)S(1)}, f32[4,5,5]{2,0,1:T(4,128)}, u32[]{:S(2)}) copy-start(f32[4,5,5]{2,0,1:T(4,128)} %param.13) | copy-start | bytes 1204
  2.1 6.3 %collective-permute-start = (f32[4,32,128]{2,1,0:T(8,128)S(1)}, f32[4,32,128]{2,1,0:T(8,128)S(1)}, u32[]{:S(2)}, u32[]{:S(2)}) collective-permute-start(f32[4,32,128]{2,1,0:T(8,128)S(1)} %get-tuple-element.37), channel_id=1, source_target_pairs={{0,32},{32,64},{64,96},{96,0},{1,33},{33,65},{65,97},{97,1},{2,34}... | collective-permute-start | bytes 196616 | tf_op jit(solution)/shard_map/ppermute | solution.py:781
  4.3 4.1 %collective-permute-start.1 = (f32[4,32,128]{2,1,0:T(8,128)S(1)}, f32[4,32,128]{2,1,0:T(8,128)S(1)}, u32[]{:S(2)}, u32[]{:S(2)}) collective-permute-start(f32[4,32,128]{2,1,0:T(8,128)S(1)} %get-tuple-element.38), channel_id=1, source_target_pairs={{32,0},{64,32},{96,64},{0,96},{33,1},{65,33},{97,65},{1,97},{34,2}... | collective-permute-start | bytes 196616 | tf_op jit(solution)/shard_map/ppermute | solution.py:781
  5.8 0.7 %copy-start.2 = (f32[5,4]{0,1:T(4,128)S(1)}, f32[5,4]{0,1:T(4,128)}, u32[]{:S(2)}) copy-start(f32[5,4]{0,1:T(4,128)} %param.10) | copy-start | bytes 244
  5.8 0.7 %copy-start.3 = (s32[1,1,4]{2,1,0:T(1,128)S(1)}, s32[1,1,4]{2,1,0:T(1,128)}, u32[]{:S(2)}) copy-start(s32[1,1,4]{2,1,0:T(1,128)} %cmap.1) | copy-start | bytes 52
  8.4 21.9 %collective-permute-start.2 = (f32[40,16,128]{2,1,0:T(8,128)S(1)}, f32[40,16,128]{2,1,0:T(8,128)S(1)}, u32[]{:S(2)}, u32[]{:S(2)}) collective-permute-start(f32[40,16,128]{2,1,0:T(8,128)S(1)} %get-tuple-element.42), channel_id=1, source_target_pairs={{0,1},{1,2},{2,3},{3,4},{4,5},{5,6},{6,7},{7,8},{8,9},{9,10},{10,1... | collective-permute-start | bytes 983048 | tf_op jit(solution)/shard_map/ppermute | solution.py:798
  11.2 19.1 %collective-permute-start.3 = (f32[40,16,128]{2,1,0:T(8,128)S(1)}, f32[40,16,128]{2,1,0:T(8,128)S(1)}, u32[]{:S(2)}, u32[]{:S(2)}) collective-permute-start(f32[40,16,128]{2,1,0:T(8,128)S(1)} %get-tuple-element.43), channel_id=1, source_target_pairs={{1,0},{2,1},{3,2},{4,3},{5,4},{6,5},{7,6},{8,7},{9,8},{10,9},{11,1... | collective-permute-start | bytes 983048 | tf_op jit(solution)/shard_map/ppermute | solution.py:798

commit v8 on v7

--- a/solution.py
+++ b/solution.py
@@ -551,23 +551,28 @@
 
     place_in = lane & (HALF - 1)
 
-    def cross_step(y8, cx):
-        side, side_code = zero, zero - 1.0
-        for r in range(8):
+    targets = [place_in == COLS - 1 - LATE - l for l in span]
+    cross = []
+    for row in range(TOP, TOP + ROWS, 8):
+        def strip(ref, s, change):
+            tile = zero - 1.0
             for l in span:
-                here = at(l, TOP + 8 * y8 + r)
-                p = r * LAYERS + l
-                m = mat_w[here, :]
-                code = m * 4.0 + turn(m, -1)
-                target = place_in == COLS - 1 - LATE - p
-                side = jnp.where(target, turn(gx[here, :], -p), side)
-                side_code = jnp.where(target, turn(code, -p), side_code)
-        return [cx[i] + jnp.where(side_code == float(i), side, 0.0) for i in range(16)]
-
-    cx = lax.fori_loop(0, ROWS // 8, cross_step, [zero] * 16)
-    valid = (sub >= SPECIES) & ((sub < 7) | left)
-    for i in range(16):
-        keep(acc, G_CX + i, jnp.where(valid, cx[i], 0.0))
+                v = change(ref[pl.ds((l * TALL + row) * 8 + s, 8, stride=8), :])
+                tile = jnp.where(targets[l], turn(v, -l), tile)
+            return tile
+
+        code = strip(mat_w, SPECIES, lambda m: m * 4.0 + turn(m, -1))
+        cross.append((code, [strip(gx, SPECIES + i, lambda v: v) for i in range(3)]))
+    for k in range(16):
+        for i, (a, b) in enumerate(pairs):
+            total = zero
+            for code, sides in cross:
+                total = total + jnp.where(code == float(k), sides[i], 0.0)
+            total = fold(total)
+            r = (G_CX + k) * SPECIES
+            acc[r + a : r + a + 1, :] = jnp.where(left[0:1], total, 0.0)
+            if b != a:
+                acc[r + b : r + b + 1, :] = jnp.where(left[0:1], 0.0, total)
 
 
 def first_kernel(

time: 61 us -> 60.3 us (0.989)
  Pallas kernels: 18.4 us -> 17.6 us
    pallas_call x6, Pallas kernels: 18.4 us -> 17.6 us  [run(): pl.pallas_call(kernel, out_shape=outs, in_specs=in_specs, out_specs=jax.t...]
where the time goes in v8:
time: 60.3 us; the launch traced here: 60.1 us
  blocking collectives  33.5 us (56%)
  Pallas kernels  17.6 us (29%)
  starting transfers between devices  6.45 us (11%)
  other arithmetic  1.11 us (2%)
  between operations  0.71 us (1%)
  local copies, waits for them, and re-layouts  0.69 us (1%)
    all_to_all x2, blocking collectives, to_all(): got = lax.all_to_all(rows.reshape(TOTAL, -1, COLS), BOTH, 0, 0, tiled=True)  33.5 us
    pallas_call x6, Pallas kernels, run(): pl.pallas_call(kernel, out_shape=outs, in_specs=in_specs, out_specs=jax.t...  17.6 us
    ppermute x2, starting transfers between devices, body(): x_low, x_high = (right(to_high), left(to_low))  3.71 us
    ppermute x2, starting transfers between devices, body(): y_low, y_high = (down(to_high), up(to_low))  2.73 us
  transfers between devices with their start and end apart: 4, of which 0 were waited for; matrix products, arithmetic and copies ran while one was open for 0% of the time, Pallas kernels for 3%

profile of v8, /device:TPU:1, one launch (start us, length us, event | category | flops | bytes accessed | tf_op | source)
XLA Modules:
  0.0 60.1 jit_solution(1807518794279018797)
XLA Ops:
  0.6 0.0 copy-start
  0.6 1.1 %pad_maximum_fusion.fields = f32[28,32,128]{2,1,0:T(8,128)S(1)} fusion(f32[4,32,128]{2,1,0:T(8,128)} %param.9, f32[4,32,128]{2,1,0:T(8,128)} %param.8, f32[20,32,128]{2,1,0:T(8,128)} %bitcast.19), kind=kLoop, calls=%fused_computation | loop fusion | flops 229376 | bytes 917504 | tf_op jit(solution)/shard_map/concatenate | solution.py:784
  1.8 0.0 copy-done
  1.8 0.0 copy-start.1
  1.8 0.3 shard_map.94
  2.1 2.2 %collective-permute-start = (f32[4,32,128]{2,1,0:T(8,128)S(1)}, f32[4,32,128]{2,1,0:T(8,128)S(1)}, u32[]{:S(2)}, u32[]{:S(2)}) collective-permute-start(f32[4,32,128]{2,1,0:T(8,128)S(1)} %get-tuple-element.37), channel_id=1, source_target_pairs={{0,32},{32,64},{64,96},{96,0},{1,33},{33,65},{65,97},{97,1},{2,34}... | collective-permute-start | bytes 196616 | tf_op jit(solution)/shard_map/ppermute | solution.py:786
  4.3 1.5 %collective-permute-start.1 = (f32[4,32,128]{2,1,0:T(8,128)S(1)}, f32[4,32,128]{2,1,0:T(8,128)S(1)}, u32[]{:S(2)}, u32[]{:S(2)}) collective-permute-start(f32[4,32,128]{2,1,0:T(8,128)S(1)} %get-tuple-element.38), channel_id=1, source_target_pairs={{32,0},{64,32},{96,64},{0,96},{33,1},{65,33},{97,65},{1,97},{34,2}... | collective-permute-start | bytes 196616 | tf_op jit(solution)/shard_map/ppermute | solution.py:786
  5.8 0.0 copy-start.2
  5.8 0.0 copy-start.3
  5.8 0.0 copy-done.1
  5.8 0.7 %copy-done.2 = f32[5,4]{0,1:T(4,128)S(1)} copy-done((f32[5,4]{0,1:T(4,128)S(1)}, f32[5,4]{0,1:T(4,128)}, u32[]{:S(2)}) %copy-start.2) | copy-done | bytes 104
  6.5 0.0 copy-done.3
  6.5 1.8 %shard_map.95 = (f32[128,128]{1,0:T(8,128)S(1)}, f32[256,128]{1,0:T(8,128)S(1)}) custom-call(f32[4,5]{1,0:T(4,128)S(1)} %bitcast.17, f32[32,32,128]{2,1,0:T(8,128)S(1)} %get-tuple-element.35.planes, s32[1,1,4]{2,1,0:T(1,128)S(1)} %copy-done.3, f32[5,4,5]{2,1,0:T(4,128)S(1)} %bitcast.16), custom_call_target="tpu_custom_call" | custom-call | flops 1048576 | bytes 1048576 | tf_op jit(solution)/shard_map/pallas_call | solution.py:750
  8.4 0.0 collective-permute-done.from_low.x_low
  8.4 0.0 collective-permute-done.1.from_high.x_high
  8.4 2.7 %collective-permute-start.2 = (f32[40,16,128]{2,1,0:T(8,128)S(1)}, f32[40,16,128]{2,1,0:T(8,128)S(1)}, u32[]{:S(2)}, u32[]{:S(2)}) collective-permute-start(f32[40,16,128]{2,1,0:T(8,128)S(1)} %get-tuple-element.42), channel_id=1, source_target_pairs={{0,1},{1,2},{2,3},{3,4},{4,5},{5,6},{6,7},{7,8},{8,9},{9,10},{10,1... | collective-permute-start | bytes 983048 | tf_op jit(solution)/shard_map/ppermute | solution.py:803
  11.2 0.0 collective-permute-start.3
  11.2 19.1 %all_to_all.10 = f32[128,1,128]{2,1,0:T(1,128)S(1)} all-to-all(f32[128,1,128]{2,1,0:T(1,128)S(1)} %bitcast.15), channel_id=1, replica_groups=mesh['grp'=4,'gy'=32] {'grp','gy'}, dimensions={0} | all-to-all | bytes 131072 | tf_op jit(solution)/shard_map/all_to_all | solution.py:768
  30.3 0.0 collective-permute-done.2.y_low
  30.3 0.0 collective-permute-done.3.y_high
  30.3 6.4 %shard_map.97 = (f32[2048,128]{1,0:T(8,128)S(1)}, f32[2048,128]{1,0:T(8,128)S(1)}, f32[2048,128]{1,0:T(8,128)S(1)}, f32[2048,128]{1,0:T(8,128)S(1)}, f32[2048,12...) custom-call(f32[4,5]{1,0:T(4,128)S(1)} %bitcast.18, ...), custom_call_target="tpu_custom_call" | custom-call | flops 1073741824 | bytes 1048576 | tf_op jit(solution)/shard_map/pallas_call | solution.py:750
  36.7 4.2 %shard_map.98 = (f32[256,128]{1,0:T(8,128)S(1)}, f32[2048,128]{1,0:T(8,128)S(1)}, f32[2048,128]{1,0:T(8,128)S(1)}, f32[2048,128]{1,0:T(8,128)S(1)}, bf16[512,512...) custom-call(f32[32,32,128]{2,1,0:T(8,128)S(1)} %get-tuple-element.35.planes, ...), custom_call_target="tpu_custom_call" | custom-call | flops 1073741824 | bytes 1048576 | tf_op jit(solution)/shard_map/pallas_call | solution.py:750
  40.9 14.4 %all_to_all.11 = f32[128,2,128]{2,1,0:T(2,128)S(1)} all-to-all(f32[128,2,128]{2,1,0:T(2,128)S(1)} %bitcast.14), channel_id=1, replica_groups=mesh['grp'=4,'gy'=32] {'grp','gy'}, dimensions={0} | all-to-all | bytes 262144 | tf_op jit(solution)/shard_map/all_to_all | solution.py:768
  55.3 4.8 %shard_map.99 = (f32[20,32,128]{2,1,0:T(8,128)}, f32[20,32,128]{2,1,0:T(8,128)}, f32[20,32,128]{2,1,0:T(8,128)}) custom-call(f32[32,32,128]{2,1,0:T(8,128)S(1)} %get-tuple-element.35.planes, bf16[512,512]{1,0:T(8,128)(2,1)S(1)} %get-tuple-element.57.scatter, bf16[512,128]{1,0:T(8,128)(2,1)S(1)} %get-tuple-element.58.near_hot, ...), custom_call_target="tpu_custom_call" | custom-call | flops 1073741824 | bytes 1048576 | tf_op jit(solution)/shard_map/pallas_call | solution.py:750
  (1 shorter events, 0.0 us)
Async XLA Ops:
  0.6 1.1 %copy-start = (s32[4,32,128]{2,1,0:T(8,128)S(1)}, s32[4,32,128]{2,1,0:T(8,128)}, u32[]{:S(2)}) copy-start(s32[4,32,128]{2,1,0:T(8,128)} %mat.1) | copy-start | bytes 196612
  1.8 4.1 %copy-start.1 = (f32[4,5,5]{2,0,1:T(4,128)S(1)}, f32[4,5,5]{2,0,1:T(4,128)}, u32[]{:S(2)}) copy-start(f32[4,5,5]{2,0,1:T(4,128)} %param.13) | copy-start | bytes 1204
  2.1 6.3 %collective-permute-start = (f32[4,32,128]{2,1,0:T(8,128)S(1)}, f32[4,32,128]{2,1,0:T(8,128)S(1)}, u32[]{:S(2)}, u32[]{:S(2)}) collective-permute-start(f32[4,32,128]{2,1,0:T(8,128)S(1)} %get-tuple-element.37), channel_id=1, source_target_pairs={{0,32},{32,64},{64,96},{96,0},{1,33},{33,65},{65,97},{97,1},{2,34}... | collective-permute-start | bytes 196616 | tf_op jit(solution)/shard_map/ppermute | solution.py:786
  4.3 4.1 %collective-permute-start.1 = (f32[4,32,128]{2,1,0:T(8,128)S(1)}, f32[4,32,128]{2,1,0:T(8,128)S(1)}, u32[]{:S(2)}, u32[]{:S(2)}) collective-permute-start(f32[4,32,128]{2,1,0:T(8,128)S(1)} %get-tuple-element.38), channel_id=1, source_target_pairs={{32,0},{64,32},{96,64},{0,96},{33,1},{65,33},{97,65},{1,97},{34,2}... | collective-permute-start | bytes 196616 | tf_op jit(solution)/shard_map/ppermute | solution.py:786
  5.8 0.7 %copy-start.2 = (f32[5,4]{0,1:T(4,128)S(1)}, f32[5,4]{0,1:T(4,128)}, u32[]{:S(2)}) copy-start(f32[5,4]{0,1:T(4,128)} %param.10) | copy-start | bytes 244
  5.8 0.7 %copy-start.3 = (s32[1,1,4]{2,1,0:T(1,128)S(1)}, s32[1,1,4]{2,1,0:T(1,128)}, u32[]{:S(2)}) copy-start(s32[1,1,4]{2,1,0:T(1,128)} %cmap.1) | copy-start | bytes 52
  8.4 21.9 %collective-permute-start.2 = (f32[40,16,128]{2,1,0:T(8,128)S(1)}, f32[40,16,128]{2,1,0:T(8,128)S(1)}, u32[]{:S(2)}, u32[]{:S(2)}) collective-permute-start(f32[40,16,128]{2,1,0:T(8,128)S(1)} %get-tuple-element.42), channel_id=1, source_target_pairs={{0,1},{1,2},{2,3},{3,4},{4,5},{5,6},{6,7},{7,8},{8,9},{9,10},{10,1... | collective-permute-start | bytes 983048 | tf_op jit(solution)/shard_map/ppermute | solution.py:803
  11.2 19.1 %collective-permute-start.3 = (f32[40,16,128]{2,1,0:T(8,128)S(1)}, f32[40,16,128]{2,1,0:T(8,128)S(1)}, u32[]{:S(2)}, u32[]{:S(2)}) collective-permute-start(f32[40,16,128]{2,1,0:T(8,128)S(1)} %get-tuple-element.43), channel_id=1, source_target_pairs={{1,0},{2,1},{3,2},{4,3},{5,4},{6,5},{7,6},{8,7},{9,8},{10,9},{11,1... | collective-permute-start | bytes 983048 | tf_op jit(solution)/shard_map/ppermute | solution.py:803
